TPU v7x, 256 devices: a whole 4x4x8 slice. The times are simulated.
256 devices in a mesh: img: 8 (over z_hi, y), mx: 8 (over z_lo, core), my: 4 (over x).
Axes of the slice: x: 4, y: 4, z: 8 (z_hi: 2, z_lo: 4; z = z_hi * 4 + z_lo), core: 2. Of those that a mesh axis runs over, the one named last changes fastest.
Arguments:
- patches: bfloat16 [8192, 6144], P(('img', 'my'), 'mx')
- tile_counts: int32 [16], replicated, may hold values from 1 to 4, as said below
- image_owner: int32 [16], replicated, may hold values from 0 to 7, as said below
- block_target: int32 [8, 8], P('img'), may hold values from 0 to 7, each once within a row
- qkv_weight: bfloat16 [6144, 3, 4096], P('mx', None, 'my')
- out_weight: bfloat16 [4096, 6144], P('my', 'mx'), may hold values from -0.09375 to 0.09375
Outputs:
- routed: bfloat16 [8192, 6144], P(('img', 'my'), 'mx')
Inputs may be any that keep to these rules, and one draw needn't show every extreme that they name: `tile_counts`: each image has 1 to 4 blocks; the two images of an arrival group fit its 8 blocks. `image_owner`: the owner of image k is k // 2 or the group whose index differs from it in the lowest bit; every group owns exactly two images, their blocks sum to at most 8, and in every draw some group owns exactly 8 blocks.
All inputs are finite; a program needn't handle non-finite values.
Results may differ from a plain program's by a relative error of at most 0.015.
Values may be sent and summed in bfloat16 or wider, within the bound.
No kernel may reach another device: no remote copies, remote signals or barrier semaphores. Data moves between devices by JAX's collectives and lax.ppermute only.
A program may use at most 128 MiB of HBM per device.

v0:
```python
import jax
import jax.numpy as jnp
from jax import lax
from jax.experimental import pallas as pl
from jax.experimental.pallas import tpu as pltpu
from jax.sharding import PartitionSpec as P

D = 6144
HD = 128
BLK = 128
GRP = 8
R = 1024
SH = 256
DL = 768
CHIP = 2 * DL
HEAD = 3 * HD
IMG_ROWS = 512
ORDER = (0, 2, 1, 3)
EXTRA = 32
F32 = jnp.float32
BF16 = jnp.bfloat16

VMEM = pl.BlockSpec(memory_space=pltpu.VMEM)
SMEM = pl.BlockSpec(memory_space=pltpu.SMEM)
ANY = pl.BlockSpec(memory_space=pl.ANY)
HBM = pl.BlockSpec(memory_space=pltpu.HBM)


def call(kernel, outs, ins, scratch=(), limit=16, out_specs=None, after=(), aliases=None):
    out_shape = [jax.ShapeDtypeStruct(s, d) for s, d in outs]
    count = len(ins)

    def ordered(*refs):
        kernel(*refs[:count], *refs[count + len(after) :])

    made = pl.pallas_call(
        ordered,
        out_shape=out_shape,
        in_specs=list(ins) + [ANY] * len(after),
        out_specs=out_specs or [VMEM] * len(outs),
        scratch_shapes=list(scratch),
        input_output_aliases=aliases or {},
        compiler_params=pltpu.CompilerParams(vmem_limit_bytes=limit << 20),
        cost_estimate=pl.CostEstimate(flops=0, bytes_accessed=1024, transcendentals=0),
    )
    return lambda *args: made(*args, *after)


def gate(blocks, after):
    def kernel(*refs):
        pass

    outs = [(b.shape, b.dtype) for b in blocks]
    ins = [ANY] * len(blocks)
    same = {i: i for i in range(len(blocks))}
    return call(kernel, outs, ins, limit=4, out_specs=ins, after=after, aliases=same)(*blocks)


def swap(block, axis, bits):
    count = lax.axis_size(axis)
    return lax.ppermute(block, axis, [(i, i ^ bits) for i in range(count)])


def shift(block, axis, step):
    count = lax.axis_size(axis)
    return lax.ppermute(block, axis, [((i + step) % count, i) for i in range(count)])


def weight_heads(w3, sibling):
    def kernel(w_ref, keep_ref, send_ref, sems):
        mx = lax.axis_index("mx")
        z = mx >> 1
        lane = (mx & 1) ^ (1 if sibling else 0)
        copies = []
        for place in (2, 3, 0, 1):
            head = lane * 4 + (z ^ ORDER[place])
            dst = keep_ref if place < 2 else send_ref
            for s in range(3):
                copies.append(
                    pltpu.make_async_copy(
                        w_ref.at[s, :, pl.ds(pl.multiple_of(head * HD, HD), HD)],
                        dst.at[:, pl.ds((place % 2) * HEAD + s * HD, HD)],
                        sems.at[len(copies)],
                    )
                )
        for copy in copies:
            copy.start()
        for copy in copies:
            copy.wait()

    shape = ((DL, 2 * HEAD), BF16)
    return call(kernel, [shape, shape], [HBM], [pltpu.SemaphoreType.DMA((12,))])(w3)


def out_weight_heads(w):
    def kernel(w_ref, out_ref, sems):
        mx = lax.axis_index("mx")
        z = mx >> 1
        copies = []
        for side in range(2):
            lane = (mx & 1) ^ side
            for j in range(4):
                head = lane * 4 + (z ^ j)
                copies.append(
                    pltpu.make_async_copy(
                        w_ref.at[pl.ds(pl.multiple_of(head * HD, HD), HD), :],
                        out_ref.at[pl.ds((side * 4 + j) * HD, HD), :],
                        sems.at[len(copies)],
                    )
                )
        for copy in copies:
            copy.start()
        for copy in copies:
            copy.wait()

    (out,) = call(kernel, [(w.shape, BF16)], [HBM], [pltpu.SemaphoreType.DMA((8,))])(w)
    return out


def table(counts, owner, target):
    def kernel(counts_ref, owner_ref, target_ref, out_ref, source):
        group = lax.axis_index("img")
        my = lax.axis_index("my")
        for t in range(GRP):
            source[t] = -1
        base = (group >> 1) * 4
        offset = jnp.int32(0)
        for i in range(4):
            image = base + i
            count = counts_ref[image]
            owned = owner_ref[image] == group
            side = jnp.where((image >> 1) == group, 0, GRP)
            for b in range(4):

                @pl.when(owned & (b < count))
                def _():
                    place = target_ref[0, jnp.minimum(offset + b, GRP - 1)]
                    source[place] = side + (i & 1) * 4 + b

            offset = offset + jnp.where(owned, count, 0)
        for n, step in enumerate((2, 1, 3, 0)):
            shard = (my + step) & 3
            out_ref[2 * n] = source[2 * shard]
            out_ref[2 * n + 1] = source[2 * shard + 1]
        out_ref[8] = counts_ref[2 * group]
        out_ref[9] = counts_ref[2 * group + 1]

    (out,) = call(
        kernel,
        [((16,), jnp.int32)],
        [SMEM] * 3,
        [pltpu.SMEM((GRP,), jnp.int32)],
        limit=4,
        out_specs=[SMEM],
    )(counts, owner, target)
    return out


def load_rows(rows, xo_ref, xs_ref):
    count = xo_ref.shape[0]
    rows[0:count, 0:DL] = xo_ref[...]
    rows[0:count, DL:CHIP] = xs_ref[...]
    rows[count : count + 16, :] = jnp.ones((16, CHIP), BF16)


def row_stats(xo_ref, xs_ref):
    fo, fs = xo_ref[...].astype(F32), xs_ref[...].astype(F32)
    s1 = jnp.sum(fo, axis=1, keepdims=True) + jnp.sum(fs, axis=1, keepdims=True)
    s2 = jnp.sum(fo * fo, axis=1, keepdims=True) + jnp.sum(fs * fs, axis=1, keepdims=True)
    lane = lax.broadcasted_iota(jnp.int32, (xo_ref.shape[0], HD), 1)
    return jnp.where(lane == 0, s1, jnp.where(lane == 1, s2, F32(0.0)))


def partial_tile(rows, wo_ref, ws_ref, columns, center):
    count = center.shape[0]
    acc = jnp.dot(rows[:, 0:DL], wo_ref[:, columns], preferred_element_type=F32)
    acc = acc + jnp.dot(rows[:, DL:CHIP], ws_ref[:, columns], preferred_element_type=F32)
    sums = acc[count : count + 8, :]
    return acc[0:count, :] - center * sums[0:1, :], sums


def rows_scratch(count):
    return pltpu.VMEM((count + 16, CHIP), BF16)


def send_part(xo, xs, wo, ws, after=()):
    count = xo.shape[0]

    def kernel(xo_ref, xs_ref, wo_ref, ws_ref, out_ref, stat_ref, copy_ref, rows):
        load_rows(rows, xo_ref, xs_ref)
        copy_ref[...] = xo_ref[...]
        stat = row_stats(xo_ref, xs_ref)
        stat_ref[...] = stat
        center = stat[:, 0:1] / CHIP
        for n in range(3):
            columns = slice(n * 256, (n + 1) * 256)
            tile, _ = partial_tile(rows, wo_ref, ws_ref, columns, center)
            out_ref[:, columns] = tile.astype(BF16)

    outs = [((count, 2 * HEAD), BF16), ((count, HD), F32), ((count, DL), BF16)]
    return call(kernel, outs, [VMEM] * 4, [rows_scratch(count)], after=after)(xo, xs, wo, ws)


def keep_part(xo, xs, wo, ws, stat, got, more=None, pieces=1, after=()):
    count = xo.shape[0]
    size = count // pieces
    extra = list(more or ())

    def kernel(xo_ref, xs_ref, wo_ref, ws_ref, stat_ref, got_ref, *refs):
        refs, rows = refs[:-1], refs[-1]
        own_ref, sends = refs[len(extra)], refs[len(extra) + 1 : len(extra) + 1 + pieces]
        load_rows(rows, xo_ref, xs_ref)
        center = stat_ref[:, 0:1] / CHIP
        for n in reversed(range(6)):
            columns = slice(n * HD, (n + 1) * HD)
            if n % 2 == 1:
                pair, _ = partial_tile(rows, wo_ref, ws_ref, slice((n - 1) * HD, (n + 1) * HD), center)
            tile = pair[:, (n % 2) * HD : (n % 2 + 1) * HD] + got_ref[:, columns].astype(F32)
            if n < 3:
                own_ref[:, columns] = tile
            else:
                for i, send_ref in enumerate(sends):
                    send_ref[:, (n - 3) * HD : (n - 2) * HD] = tile[i * size : (i + 1) * size, :].astype(BF16)
        if extra:
            refs[-1][...] = refs[0][...] + refs[1][...].astype(F32)

    outs = [((count, HEAD), F32)] + [((size, HEAD), BF16)] * pieces
    outs += [((SH, HEAD), F32)] if extra else []
    ins = [VMEM] * (6 + len(extra))
    return call(kernel, outs, ins, [rows_scratch(count)], after=after)(xo, xs, wo, ws, stat, got, *extra)


def whole_tiles(refs, sends, own_ref, rows, center, done):
    ko_ref, ks_ref, so_ref, ss_ref = refs
    p1_ref, p2_ref, p3_ref = sends
    count = center.shape[0]
    for wo_ref, ws_ref, outs, js in ((so_ref, ss_ref, (p1_ref, p3_ref), (1, 3)), (ko_ref, ks_ref, (own_ref, p2_ref), (0, 2))):
        for n in range(0, 6, 2):
            pair, sums = partial_tile(rows, wo_ref, ws_ref, slice(n * HD, (n + 2) * HD), center)
            for h in range(2):
                half = slice(h * HD, (h + 1) * HD)
                side, place = divmod(n + h, 3)
                out_ref = outs[side]
                out_ref[0:count, place * HD : (place + 1) * HD] = pair[:, half].astype(out_ref.dtype)
                done(js[side], place, sums[:, half])


def last_part(xo, xs, weights, stats, after):
    def kernel(xo_ref, xs_ref, *refs):
        ws, (t0_ref, t12_ref) = refs[0:4], refs[4:6]
        own_ref, p1_ref, p2_ref, p3_ref, note_ref, rows = refs[6:]
        load_rows(rows, xo_ref, xs_ref)
        stat = row_stats(xo_ref, xs_ref)
        turned = [one[k * SH : (k + 1) * SH, :].T for one, k in ((t0_ref, 0), (t12_ref, 0), (t12_ref, 1), (stat, 0))]
        sums = jnp.concatenate([t[0:1, :] for t in turned] + [t[1:2, :] for t in turned], axis=0)
        column_sums = {}

        def done(j, place, tile_sums):
            column_sums[j, place] = tile_sums[0:1, :]

        whole_tiles(ws, (p1_ref, p2_ref, p3_ref), own_ref, rows, stat[:, 0:1] / CHIP, done)
        for j, ref in enumerate((note_ref, p1_ref, p2_ref, p3_ref)):
            heads = [column_sums[j, place] for place in range(3)] + [jnp.zeros((5, HD), F32)]
            note = jnp.concatenate([sums, jnp.concatenate(heads, axis=0)], axis=1)
            if j == 0:
                ref[...] = note
                continue
            terms = []
            for _ in range(3):
                terms.append(note.astype(BF16).astype(F32))
                note = note - terms[-1]
            terms.append(jnp.zeros((8, HEAD), F32))
            ref[SH : SH + EXTRA, :] = jnp.concatenate(terms, axis=0).astype(BF16)

    part = ((SH + EXTRA, HEAD), BF16)
    outs = [((SH, HEAD), F32), part, part, part, ((8, HEAD), F32)]
    return call(kernel, outs, [VMEM] * 8, [rows_scratch(SH)], after=after)(xo, xs, *weights, *stats)


def last_sum(own, got, note):
    def kernel(own_ref, g1_ref, g2_ref, g3_ref, note_ref, out_ref, coef_ref, cs_ref):
        total = own_ref[...]
        notes = [note_ref[...]]
        for ref in (g1_ref, g2_ref, g3_ref):
            total = total + ref[0:SH, :].astype(F32)
            terms = ref[SH : SH + EXTRA, :].astype(F32)
            notes.append(terms[0:8, :] + terms[8:16, :] + terms[16:24, :])
        out_ref[...] = total
        for k in range(4):
            sums = [n[k : k + 1, 0:SH] for n in notes]
            squares = [n[4 + k : 5 + k, 0:SH] for n in notes]
            mean = (sums[0] + sums[1] + sums[2] + sums[3]) / D
            var = (squares[0] + squares[1] + squares[2] + squares[3]) / D - mean * mean
            lines = [lax.rsqrt(var + 1e-06)] + [s / CHIP - mean for s in sums] + [jnp.zeros((HD - 5, SH), F32)]
            coef_ref[k * SH : (k + 1) * SH, :] = jnp.concatenate(lines, axis=0).T
        for c, n in enumerate(notes):
            for place in range(3):
                cs_ref[c : c + 1, place * HD : (place + 1) * HD] = n[place : place + 1, SH:HEAD]
        cs_ref[4:8, :] = jnp.zeros((4, HEAD), F32)

    outs = [((SH, HEAD), F32), ((R, HD), F32), ((8, HEAD), F32)]
    return call(kernel, outs, [VMEM] * 5)(own, *got, note)


def join(blocks, axis, after=()):
    size = blocks[0].shape[axis]

    def kernel(*refs):
        for i, ref in enumerate(refs[:-1]):
            at = slice(i * size, (i + 1) * size)
            if axis == 0:
                refs[-1][at, :] = ref[...]
            else:
                refs[-1][:, at] = ref[...]

    shape = list(blocks[0].shape)
    shape[axis] *= len(blocks)
    (out,) = call(kernel, [(tuple(shape), BF16)], [VMEM] * len(blocks), after=after)(*blocks)
    return out


def attention(places, coef, cs, tot0, own12, ends, tot3):
    def kernel(places_ref, coef_ref, cs_ref, tot0_ref, own12_ref, end1_ref, end2_ref, tot3_ref, out_ref, qkv):
        my = lax.axis_index("my")
        for k, offset in enumerate((0, 1, 3, 2)):
            if k in (1, 2):
                end_ref = end1_ref if k == 1 else end2_ref
                total = own12_ref[(k - 1) * SH : k * SH, :] + end_ref[...].astype(F32)
            else:
                total = (tot3_ref if k else tot0_ref)[...]
            coef = coef_ref[k * SH : (k + 1) * SH, :]
            for c in range(4):
                total = total + coef[:, c + 1 : c + 2] * cs_ref[c : c + 1, :]
            total = total * coef[:, 0:1]
            shard = (my + offset) & 3
            qkv[pl.ds(pl.multiple_of(shard * SH, SH), SH), :] = total.astype(BF16)
        first, second = places_ref[8], places_ref[9]
        for image in range(2):
            start = pl.multiple_of(first * BLK, BLK) if image else 0
            live = (second if image else first) * BLK
            q = qkv[pl.ds(start, IMG_ROWS), 0:HD]
            key = qkv[pl.ds(start, IMG_ROWS), HD : 2 * HD]
            value = qkv[pl.ds(start, IMG_ROWS), 2 * HD : 3 * HD]
            rows = lax.broadcasted_iota(jnp.int32, (IMG_ROWS, HD), 0)
            value = jnp.where(rows < live, value, jnp.zeros_like(value))
            scores = lax.dot_general(q, key, (((1,), (1,)), ((), ())), preferred_element_type=F32)
            columns = lax.broadcasted_iota(jnp.int32, (IMG_ROWS, IMG_ROWS), 1)
            scores = jnp.where(columns < live, scores * HD ** (-0.5), F32(-1e30))
            top = jnp.max(scores, axis=1, keepdims=True)
            powers = jnp.exp(scores - top)
            weights = (powers / jnp.sum(powers, axis=1, keepdims=True)).astype(BF16)
            mixture = jnp.dot(weights, value, preferred_element_type=F32)
            out_ref[image * IMG_ROWS : (image + 1) * IMG_ROWS, :] = mixture.astype(BF16)

    (out,) = call(
        kernel, [((R, HD), BF16)], [SMEM] + [VMEM] * 7, [pltpu.VMEM((R, HEAD), BF16)], limit=24
    )(places, coef, cs, tot0, own12, *ends, tot3)
    return out


def route(places, mine, other):
    def kernel(places_ref, mine_ref, other_ref, *outs):
        for n in range(GRP):
            out_ref, at = (outs[0], n) if n < 6 else (outs[1], n - 6)
            place = slice(at * BLK, (at + 1) * BLK)
            src = places_ref[n]
            row = pl.multiple_of((src & 7) * BLK, BLK)

            @pl.when(src < 0)
            def _():
                out_ref[place, :] = jnp.zeros((BLK, HD), BF16)

            @pl.when((src >= 0) & (src < GRP))
            def _():
                out_ref[place, :] = mine_ref[pl.ds(row, BLK), :]

            @pl.when(src >= GRP)
            def _():
                out_ref[place, :] = other_ref[pl.ds(row, BLK), :]

    outs = [((3 * SH, HD), BF16), ((SH, HD), BF16)]
    return call(kernel, outs, [SMEM, VMEM, VMEM])(places, mine, other)


def project(block, wo, dtype, after=()):
    lane = join([block] + [swap(block, "mx", 2 * j) for j in (1, 2, 3)], 1, after)
    sib = swap(lane, "mx", 1)
    count = block.shape[0] // SH

    def kernel(lane_ref, sib_ref, w_ref, *outs):
        for i, out_ref in enumerate(outs):
            at = slice(i * SH, (i + 1) * SH)
            for n in range(3):
                columns = slice(n * 256, (n + 1) * 256)
                tile = jnp.dot(lane_ref[at, :], w_ref[0 : 4 * HD, columns], preferred_element_type=F32)
                tile = tile + jnp.dot(sib_ref[at, :], w_ref[4 * HD :, columns], preferred_element_type=F32)
                out_ref[:, columns] = tile.astype(dtype)

    return call(kernel, [((SH, DL), dtype)] * count, [VMEM] * 3)(lane, sib, wo)


def shards(patches, tile_counts, image_owner, block_target, qkv_weight, out_weight):
    scope = jax.named_scope
    with scope("rows_near"):
        next_rows, last_rows = shift(patches, "my", 1), shift(patches, "my", -1)
    w3 = jnp.transpose(qkv_weight, (1, 0, 2))
    with scope("weights"):
        theirs_keep, theirs_send = weight_heads(w3, True)
        sib_send = swap(theirs_send, "mx", 1)
        sib_keep = swap(theirs_keep, "mx", 1)
        own_keep, own_send = weight_heads(w3, False)
        wo = out_weight_heads(out_weight)
        places = table(tile_counts, image_owner, block_target)
    weights = (own_keep, sib_keep, own_send, sib_send)

    with scope("chunk0"):
        s0 = swap(patches, "mx", 1)
        part0, stat0, again = send_part(patches, s0, own_send, sib_send)
        got0 = swap(part0, "mx", 2)
    with scope("rows_far"):
        x3 = shift(again, "my", 2)
    with scope("chunk12"):
        x12 = join([next_rows, last_rows], 0, (got0,))
        s12 = swap(x12, "mx", 1)
    with scope("sum0"):
        own0, next0 = keep_part(patches, s0, own_keep, sib_keep, stat0, got0)
        end0 = swap(next0, "mx", 4)
    with scope("chunk12"):
        part12, stat12, _ = send_part(x12, s12, own_send, sib_send, (next0,))
        got12 = swap(part12, "mx", 2)
    with scope("chunk3"):
        (x3,) = gate([x3], (part12,))
        s3 = swap(x3, "mx", 1)
        own3, p1, p2, p3, note = last_part(x3, s3, weights, (stat0, stat12), (part12, wo, places))
        got3 = [swap(p1, "mx", 2), swap(p2, "mx", 4), swap(p3, "mx", 6)]
    with scope("sum12"):
        own12, next1, next2, tot0 = keep_part(x12, s12, own_keep, sib_keep, stat12, got12, (own0, end0), 2, (own3,))
        ends = [swap(next1, "mx", 4), swap(next2, "mx", 4)]
    with scope("sum3"):
        tot3, coef, cs = last_sum(own3, got3, note)

    with scope("attention"):
        attended = attention(places, coef, cs, tot0, own12, ends, tot3)
        other = swap(attended, "img", 1)
        across, here = route(places, attended, other)

    with scope("out"):
        far, up, down = project(across, wo, BF16)
        arrived = [shift(far, "my", 2), shift(up, "my", -1), shift(down, "my", 1)]
    with scope("own_out"):
        (mine,) = project(here, wo, F32)
    for one in arrived:
        mine = mine + one.astype(F32)
    return mine.astype(BF16)


def solution(mesh):
    in_specs = (
        P(("img", "my"), "mx"),
        P(),
        P(),
        P("img", None),
        P("mx", None, "my"),
        P("my", "mx"),
    )
    out_specs = P(("img", "my"), "mx")
    return jax.shard_map(shards, mesh=mesh, in_specs=in_specs, out_specs=out_specs, check_vma=False)
```

profile of v0, /device:TPU:1, one launch (start us, length us, event | category | flops | bytes accessed | tf_op | source)
XLA Modules:
  0.0 141.1 jit_solution(11186885096108637885)
XLA Ops:
  0.0 2.3 %copy-done = bf16[768,3,1024]{2,0,1:T(8,128)(2,1)S(1)} copy-done((bf16[768,3,1024]{2,0,1:T(8,128)(2,1)S(1)}, bf16[768,3,1024]{2,0,1:T(8,128)(2,1)}, u32[]{:S(2)}) %copy-start) | copy-done | bytes 4718616
  3.1 3.3 %collective-permute-start.1 = (bf16[768,768]{1,0:T(8,128)(2,1)S(1)}, bf16[768,768]{1,0:T(8,128)(2,1)S(1)}, u32[]{:S(2)}, u32[]{:S(2)}) collective-permute-start(bf16[768,768]{1,0:T(8,128)(2,1)S(1)} %get-tuple-element.34), channel_id=1, source_target_pairs={{0,4},{4,0},{8,12},{12,8},{16,20},{20,16},{24,28},{28,24},{1,5},{5... | collective-permute-start | bytes 3538952 | tf_op jit(solution)/shard_map/weights/ppermute | solution.py:61
  11.5 5.5 %collective-permute-done.3.refs_0_ = bf16[256,768]{1,0:T(8,128)(2,1)S(1)} collective-permute-done((bf16[256,768]{1,0:T(8,128)(2,1)S(1)}, bf16[256,768]{1,0:T(8,128)(2,1)S(1)}, u32[]{:S(2)}, u32[]{:S(2)}) %collective-permute-start.3) | collective-permute-done | bytes 393248 | tf_op jit(solution)/shard_map/rows_near/ppermute | solution.py:66
  18.6 3.0 %collective-permute-done.5.refs_2_.refs_5_ = bf16[256,768]{1,0:T(8,128)(2,1)S(1)} collective-permute-done((bf16[256,768]{1,0:T(8,128)(2,1)S(1)}, bf16[256,768]{1,0:T(8,128)(2,1)S(1)}, u32[]{:S(2)}, u32[]{:S(2)}) %collective-permute-start.5) | collective-permute-done | bytes 393248 | tf_op jit(solution)/shard_map/chunk0/ppermute | solution.py:61
  24.7 2.7 %chunk12.3 = (bf16[512,768]{1,0:T(8,128)(2,1)S(1)}, f32[512,128]{1,0:T(8,128)S(1)}, bf16[512,768]{1,0:T(8,128)(2,1)}) custom-call(bf16[512,768]{1,0:T(8,128)(2,1)S(1)} %chunk12.2.refs_0_, bf16[512,768]{1,0:T(8,128)(2,1)S(1)} %collective-permute-done.6.refs_1_, bf16[768,768]{1,0:T(8,128)(2,1)S(1)} %get-tuple-element.33.refs_2_.refs_4_, ...), custom_call_target="tpu_custom_call" | custom-call | bytes 1024 | tf_op jit(solution)/shard_map/chunk12/pallas_call | solution.py:46
  28.9 5.8 %collective-permute-done.2.refs_0_ = bf16[256,768]{1,0:T(8,128)(2,1)S(1)} collective-permute-done((bf16[256,768]{1,0:T(8,128)(2,1)S(1)}, bf16[256,768]{1,0:T(8,128)(2,1)S(1)}, u32[]{:S(2)}, u32[]{:S(2)}) %collective-permute-start.2) | collective-permute-done | bytes 393248 | tf_op jit(solution)/shard_map/rows_far/ppermute | solution.py:66
  35.7 2.2 %collective-permute-start.13 = (bf16[256,384]{1,0:T(8,128)(2,1)S(1)}, bf16[256,384]{1,0:T(8,128)(2,1)S(1)}, u32[]{:S(2)}, u32[]{:S(2)}) collective-permute-start(bf16[256,384]{1,0:T(8,128)(2,1)S(1)} %get-tuple-element.40.refs_4_), channel_id=1, source_target_pairs={{0,16},{4,20},{8,24},{12,28},{16,0},{20,4},{24,8},{28,12},{1,17},{... | collective-permute-start | bytes 589832 | tf_op jit(solution)/shard_map/sum0/ppermute | solution.py:61
  44.4 2.2 %collective-permute-start.11 = (bf16[288,384]{1,0:T(8,128)(2,1)S(1)}, bf16[288,384]{1,0:T(8,128)(2,1)S(1)}, u32[]{:S(2)}, u32[]{:S(2)}) collective-permute-start(bf16[288,384]{1,0:T(8,128)(2,1)S(1)} %get-tuple-element.46), channel_id=1, source_target_pairs={{0,24},{4,28},{8,16},{12,20},{16,8},{20,12},{24,0},{28,4},{1,25},{... | collective-permute-start | bytes 663560 | tf_op jit(solution)/shard_map/chunk3/ppermute | solution.py:61
  46.6 3.1 %collective-permute-done.13.refs_7_ = bf16[256,384]{1,0:T(8,128)(2,1)S(1)} collective-permute-done((bf16[256,384]{1,0:T(8,128)(2,1)S(1)}, bf16[256,384]{1,0:T(8,128)(2,1)S(1)}, u32[]{:S(2)}, u32[]{:S(2)}) %collective-permute-start.13) | collective-permute-done | bytes 196640 | tf_op jit(solution)/shard_map/sum0/ppermute | solution.py:61
  49.7 2.5 %collective-permute-done.12.refs_5_ = bf16[512,768]{1,0:T(8,128)(2,1)S(1)} collective-permute-done((bf16[512,768]{1,0:T(8,128)(2,1)S(1)}, bf16[512,768]{1,0:T(8,128)(2,1)S(1)}, u32[]{:S(2)}, u32[]{:S(2)}) %collective-permute-start.12) | collective-permute-done | bytes 786464 | tf_op jit(solution)/shard_map/chunk12/ppermute | solution.py:61
  54.0 5.3 %collective-permute-start.14 = (bf16[256,384]{1,0:T(8,128)(2,1)S(1)}, bf16[256,384]{1,0:T(8,128)(2,1)S(1)}, u32[]{:S(2)}, u32[]{:S(2)}) collective-permute-start(bf16[256,384]{1,0:T(8,128)(2,1)S(1)} %get-tuple-element.53), channel_id=1, source_target_pairs={{0,16},{4,20},{8,24},{12,28},{16,0},{20,4},{24,8},{28,12},{1,17},{... | collective-permute-start | bytes 589832 | tf_op jit(solution)/shard_map/sum12/ppermute | solution.py:61
  59.9 7.5 %collective-permute-done.11.refs_3_ = bf16[288,384]{1,0:T(8,128)(2,1)S(1)} collective-permute-done((bf16[288,384]{1,0:T(8,128)(2,1)S(1)}, bf16[288,384]{1,0:T(8,128)(2,1)S(1)}, u32[]{:S(2)}, u32[]{:S(2)}) %collective-permute-start.11) | collective-permute-done | bytes 221216 | tf_op jit(solution)/shard_map/chunk3/ppermute | solution.py:61
  67.8 15.0 %collective-permute-done.14.refs_5_ = bf16[256,384]{1,0:T(8,128)(2,1)S(1)} collective-permute-done((bf16[256,384]{1,0:T(8,128)(2,1)S(1)}, bf16[256,384]{1,0:T(8,128)(2,1)S(1)}, u32[]{:S(2)}, u32[]{:S(2)}) %collective-permute-start.14) | collective-permute-done | bytes 196640 | tf_op jit(solution)/shard_map/sum12/ppermute | solution.py:61
  82.8 4.2 %collective-permute-done.15.refs_6_ = bf16[256,384]{1,0:T(8,128)(2,1)S(1)} collective-permute-done((bf16[256,384]{1,0:T(8,128)(2,1)S(1)}, bf16[256,384]{1,0:T(8,128)(2,1)S(1)}, u32[]{:S(2)}, u32[]{:S(2)}) %collective-permute-start.15) | collective-permute-done | bytes 196640 | tf_op jit(solution)/shard_map/sum12/ppermute | solution.py:61
  87.0 2.9 %attention.2.refs_1_ = bf16[1024,128]{1,0:T(8,128)(2,1)S(1)} custom-call(s32[16]{0:T(128)S(1)} %weights.4.refs_10_.refs_0_, f32[1024,128]{1,0:T(8,128)S(1)} %get-tuple-element.48.refs_1_, f32[8,384]{1,0:T(8,128)S(1)} %get-tuple-element.49.refs_2_, f32[256,384]{1,0:T(8,128)S(1)} %get-tuple-element.51.refs_3_, f32[512,384]{1,0:T(8,128)S(1)} %get-tuple-element.52.refs_4_, ...), custom_call_target="tpu_custom_call" | custom-call | bytes 1024 | tf_op jit(solution)/shard_map/attention/pallas_call | solution.py:46
  91.3 5.0 %collective-permute-done.16.refs_2_ = bf16[1024,128]{1,0:T(8,128)(2,1)S(1)} collective-permute-done((bf16[1024,128]{1,0:T(8,128)(2,1)S(1)}, bf16[1024,128]{1,0:T(8,128)(2,1)S(1)}, u32[]{:S(2)}, u32[]{:S(2)}) %collective-permute-start.16) | collective-permute-done | bytes 262176 | tf_op jit(solution)/shard_map/attention/ppermute | solution.py:61
  97.1 3.4 %collective-permute-start.21 = (bf16[768,128]{1,0:T(8,128)(2,1)S(1)}, bf16[768,128]{1,0:T(8,128)(2,1)S(1)}, u32[]{:S(2)}, u32[]{:S(2)}) collective-permute-start(bf16[768,128]{1,0:T(8,128)(2,1)S(1)} %get-tuple-element.57.refs_0_), channel_id=1, source_target_pairs={{0,8},{4,12},{8,0},{12,4},{16,24},{20,28},{24,16},{28,20},{1,9},{5... | collective-permute-start | bytes 589832 | tf_op jit(solution)/shard_map/out/ppermute | solution.py:61
  100.6 3.0 %collective-permute-done.23.refs_3_ = bf16[768,128]{1,0:T(8,128)(2,1)S(1)} collective-permute-done((bf16[768,128]{1,0:T(8,128)(2,1)S(1)}, bf16[768,128]{1,0:T(8,128)(2,1)S(1)}, u32[]{:S(2)}, u32[]{:S(2)}) %collective-permute-start.23) | collective-permute-done | bytes 196640 | tf_op jit(solution)/shard_map/out/ppermute | solution.py:61
  103.6 9.8 %collective-permute-done.22.refs_2_ = bf16[768,128]{1,0:T(8,128)(2,1)S(1)} collective-permute-done((bf16[768,128]{1,0:T(8,128)(2,1)S(1)}, bf16[768,128]{1,0:T(8,128)(2,1)S(1)}, u32[]{:S(2)}, u32[]{:S(2)}) %collective-permute-start.22) | collective-permute-done | bytes 196640 | tf_op jit(solution)/shard_map/out/ppermute | solution.py:61
  118.9 2.8 %collective-permute-start.25 = (bf16[256,768]{1,0:T(8,128)(2,1)S(1)}, bf16[256,768]{1,0:T(8,128)(2,1)S(1)}, u32[]{:S(2)}, u32[]{:S(2)}) collective-permute-start(bf16[256,768]{1,0:T(8,128)(2,1)S(1)} %get-tuple-element.58), channel_id=1, source_target_pairs={{2,0},{3,1},{0,2},{1,3},{6,4},{7,5},{4,6},{5,7},{10,8},{11,9},{8,1... | collective-permute-start | bytes 1179656 | tf_op jit(solution)/shard_map/out/ppermute | solution.py:66
  124.4 2.2 %collective-permute-start.17 = (bf16[256,128]{1,0:T(8,128)(2,1)S(1)}, bf16[256,128]{1,0:T(8,128)(2,1)S(1)}, u32[]{:S(2)}, u32[]{:S(2)}) collective-permute-start(bf16[256,128]{1,0:T(8,128)(2,1)S(1)} %get-tuple-element.56.refs_0_), channel_id=1, source_target_pairs={{0,8},{4,12},{8,0},{12,4},{16,24},{20,28},{24,16},{28,20},{1,9},{5... | collective-permute-start | bytes 196616 | tf_op jit(solution)/shard_map/own_out/ppermute | solution.py:61
  126.6 2.4 %collective-permute-done.18.refs_2_ = bf16[256,128]{1,0:T(8,128)(2,1)S(1)} collective-permute-done((bf16[256,128]{1,0:T(8,128)(2,1)S(1)}, bf16[256,128]{1,0:T(8,128)(2,1)S(1)}, u32[]{:S(2)}, u32[]{:S(2)}) %collective-permute-start.18) | collective-permute-done | bytes 65568 | tf_op jit(solution)/shard_map/own_out/ppermute | solution.py:61
  129.3 2.2 %collective-permute-start.20 = (bf16[256,512]{1,0:T(8,128)(2,1)S(1)}, bf16[256,512]{1,0:T(8,128)(2,1)S(1)}, u32[]{:S(2)}, u32[]{:S(2)}) collective-permute-start(bf16[256,512]{1,0:T(8,128)(2,1)S(1)} %own_out.2.refs_0_), channel_id=1, source_target_pairs={{0,4},{4,0},{8,12},{12,8},{16,20},{20,16},{24,28},{28,24},{1,5},{5... | collective-permute-start | bytes 786440 | tf_op jit(solution)/shard_map/own_out/ppermute | solution.py:61
  133.2 6.8 %collective-permute-done.26 = bf16[256,768]{1,0:T(8,128)(2,1)S(1)} collective-permute-done((bf16[256,768]{1,0:T(8,128)(2,1)S(1)}, bf16[256,768]{1,0:T(8,128)(2,1)S(1)}, u32[]{:S(2)}, u32[]{:S(2)}) %collective-permute-start.26) | collective-permute-done | bytes 393248 | tf_op jit(solution)/shard_map/out/ppermute | solution.py:66
  (63 shorter events, 36.0 us)
Async XLA Ops:
  3.1 6.6 %collective-permute-start.1 = (bf16[768,768]{1,0:T(8,128)(2,1)S(1)}, bf16[768,768]{1,0:T(8,128)(2,1)S(1)}, u32[]{:S(2)}, u32[]{:S(2)}) collective-permute-start(bf16[768,768]{1,0:T(8,128)(2,1)S(1)} %get-tuple-element.34), channel_id=1, source_target_pairs={{0,4},{4,0},{8,12},{12,8},{16,20},{20,16},{24,28},{28,24},{1,5},{5... | collective-permute-start | bytes 3538952 | tf_op jit(solution)/shard_map/weights/ppermute | solution.py:61
  6.6 10.3 %collective-permute-start.3 = (bf16[256,768]{1,0:T(8,128)(2,1)S(1)}, bf16[256,768]{1,0:T(8,128)(2,1)S(1)}, u32[]{:S(2)}, u32[]{:S(2)}) collective-permute-start(bf16[256,768]{1,0:T(8,128)(2,1)S(1)} %copy-done.1), channel_id=1, source_target_pairs={{1,0},{2,1},{3,2},{0,3},{5,4},{6,5},{7,6},{4,7},{9,8},{10,9},{11,1... | collective-permute-start | bytes 1179656 | tf_op jit(solution)/shard_map/rows_near/ppermute | solution.py:66
  7.3 11.2 %collective-permute-start.4 = (bf16[256,768]{1,0:T(8,128)(2,1)S(1)}, bf16[256,768]{1,0:T(8,128)(2,1)S(1)}, u32[]{:S(2)}, u32[]{:S(2)}) collective-permute-start(bf16[256,768]{1,0:T(8,128)(2,1)S(1)} %copy-done.1), channel_id=1, source_target_pairs={{3,0},{0,1},{1,2},{2,3},{7,4},{4,5},{5,6},{6,7},{11,8},{8,9},{9,10... | collective-permute-start | bytes 1179656 | tf_op jit(solution)/shard_map/rows_near/ppermute | solution.py:66
  8.0 15.7 %collective-permute-start.7 = (bf16[768,768]{1,0:T(8,128)(2,1)S(1)}, bf16[768,768]{1,0:T(8,128)(2,1)S(1)}, u32[]{:S(2)}, u32[]{:S(2)}) collective-permute-start(bf16[768,768]{1,0:T(8,128)(2,1)S(1)} %get-tuple-element.38), channel_id=1, source_target_pairs={{0,4},{4,0},{8,12},{12,8},{16,20},{20,16},{24,28},{28,24},{1,5},{5... | collective-permute-start | bytes 3538952 | tf_op jit(solution)/shard_map/weights/ppermute | solution.py:61
  10.8 10.8 %collective-permute-start.5 = (bf16[256,768]{1,0:T(8,128)(2,1)S(1)}, bf16[256,768]{1,0:T(8,128)(2,1)S(1)}, u32[]{:S(2)}, u32[]{:S(2)}) collective-permute-start(bf16[256,768]{1,0:T(8,128)(2,1)S(1)} %get-tuple-element.36), channel_id=1, source_target_pairs={{0,8},{4,12},{8,0},{12,4},{16,24},{20,28},{24,16},{28,20},{1,9},{5... | collective-permute-start | bytes 1179656 | tf_op jit(solution)/shard_map/chunk0/ppermute | solution.py:61
  22.5 12.2 %collective-permute-start.2 = (bf16[256,768]{1,0:T(8,128)(2,1)S(1)}, bf16[256,768]{1,0:T(8,128)(2,1)S(1)}, u32[]{:S(2)}, u32[]{:S(2)}) collective-permute-start(bf16[256,768]{1,0:T(8,128)(2,1)S(1)} %get-tuple-element.35), channel_id=1, source_target_pairs={{2,0},{3,1},{0,2},{1,3},{6,4},{7,5},{4,6},{5,7},{10,8},{11,9},{8,1... | collective-permute-start | bytes 1179656 | tf_op jit(solution)/shard_map/rows_far/ppermute | solution.py:66
  27.4 24.8 %collective-permute-start.12 = (bf16[512,768]{1,0:T(8,128)(2,1)S(1)}, bf16[512,768]{1,0:T(8,128)(2,1)S(1)}, u32[]{:S(2)}, u32[]{:S(2)}) collective-permute-start(bf16[512,768]{1,0:T(8,128)(2,1)S(1)} %get-tuple-element.41.refs_1_.refs_8_), channel_id=1, source_target_pairs={{0,8},{4,12},{8,0},{12,4},{16,24},{20,28},{24,16},{28,20},{1,9},{5... | collective-permute-start | bytes 2359304 | tf_op jit(solution)/shard_map/chunk12/ppermute | solution.py:61
  34.7 6.5 %collective-permute-start.8 = (bf16[256,768]{1,0:T(8,128)(2,1)S(1)}, bf16[256,768]{1,0:T(8,128)(2,1)S(1)}, u32[]{:S(2)}, u32[]{:S(2)}) collective-permute-start(bf16[256,768]{1,0:T(8,128)(2,1)S(1)} %chunk3.2.refs_0_), channel_id=1, source_target_pairs={{0,4},{4,0},{8,12},{12,8},{16,20},{20,16},{24,28},{28,24},{1,5},{5... | collective-permute-start | bytes 1179656 | tf_op jit(solution)/shard_map/chunk3/ppermute | solution.py:61
  35.7 14.0 %collective-permute-start.13 = (bf16[256,384]{1,0:T(8,128)(2,1)S(1)}, bf16[256,384]{1,0:T(8,128)(2,1)S(1)}, u32[]{:S(2)}, u32[]{:S(2)}) collective-permute-start(bf16[256,384]{1,0:T(8,128)(2,1)S(1)} %get-tuple-element.40.refs_4_), channel_id=1, source_target_pairs={{0,16},{4,20},{8,24},{12,28},{16,0},{20,4},{24,8},{28,12},{1,17},{... | collective-permute-start | bytes 589832 | tf_op jit(solution)/shard_map/sum0/ppermute | solution.py:61
  42.9 17.0 %collective-permute-start.9 = (bf16[288,384]{1,0:T(8,128)(2,1)S(1)}, bf16[288,384]{1,0:T(8,128)(2,1)S(1)}, u32[]{:S(2)}, u32[]{:S(2)}) collective-permute-start(bf16[288,384]{1,0:T(8,128)(2,1)S(1)} %get-tuple-element.44), channel_id=1, source_target_pairs={{0,8},{4,12},{8,0},{12,4},{16,24},{20,28},{24,16},{28,20},{1,9},{5... | collective-permute-start | bytes 663560 | tf_op jit(solution)/shard_map/chunk3/ppermute | solution.py:61
  44.4 15.5 %collective-permute-start.10 = (bf16[288,384]{1,0:T(8,128)(2,1)S(1)}, bf16[288,384]{1,0:T(8,128)(2,1)S(1)}, u32[]{:S(2)}, u32[]{:S(2)}) collective-permute-start(bf16[288,384]{1,0:T(8,128)(2,1)S(1)} %get-tuple-element.45), channel_id=1, source_target_pairs={{0,16},{4,20},{8,24},{12,28},{16,0},{20,4},{24,8},{28,12},{1,17},{... | collective-permute-start | bytes 663560 | tf_op jit(solution)/shard_map/chunk3/ppermute | solution.py:61
  44.4 23.0 %collective-permute-start.11 = (bf16[288,384]{1,0:T(8,128)(2,1)S(1)}, bf16[288,384]{1,0:T(8,128)(2,1)S(1)}, u32[]{:S(2)}, u32[]{:S(2)}) collective-permute-start(bf16[288,384]{1,0:T(8,128)(2,1)S(1)} %get-tuple-element.46), channel_id=1, source_target_pairs={{0,24},{4,28},{8,16},{12,20},{16,8},{20,12},{24,0},{28,4},{1,25},{... | collective-permute-start | bytes 663560 | tf_op jit(solution)/shard_map/chunk3/ppermute | solution.py:61
  54.0 28.8 %collective-permute-start.14 = (bf16[256,384]{1,0:T(8,128)(2,1)S(1)}, bf16[256,384]{1,0:T(8,128)(2,1)S(1)}, u32[]{:S(2)}, u32[]{:S(2)}) collective-permute-start(bf16[256,384]{1,0:T(8,128)(2,1)S(1)} %get-tuple-element.53), channel_id=1, source_target_pairs={{0,16},{4,20},{8,24},{12,28},{16,0},{20,4},{24,8},{28,12},{1,17},{... | collective-permute-start | bytes 589832 | tf_op jit(solution)/shard_map/sum12/ppermute | solution.py:61
  59.3 27.7 %collective-permute-start.15 = (bf16[256,384]{1,0:T(8,128)(2,1)S(1)}, bf16[256,384]{1,0:T(8,128)(2,1)S(1)}, u32[]{:S(2)}, u32[]{:S(2)}) collective-permute-start(bf16[256,384]{1,0:T(8,128)(2,1)S(1)} %get-tuple-element.54), channel_id=1, source_target_pairs={{0,16},{4,20},{8,24},{12,28},{16,0},{20,4},{24,8},{28,12},{1,17},{... | collective-permute-start | bytes 589832 | tf_op jit(solution)/shard_map/sum12/ppermute | solution.py:61
  89.9 6.4 %collective-permute-start.16 = (bf16[1024,128]{1,0:T(8,128)(2,1)S(1)}, bf16[1024,128]{1,0:T(8,128)(2,1)S(1)}, u32[]{:S(2)}, u32[]{:S(2)}) collective-permute-start(bf16[1024,128]{1,0:T(8,128)(2,1)S(1)} %attention.2.refs_1_), channel_id=1, source_target_pairs={{0,32},{32,0},{64,96},{96,64},{128,160},{160,128},{192,224},{224,1... | collective-permute-start | bytes 786440 | tf_op jit(solution)/shard_map/attention/ppermute | solution.py:61
  96.9 6.6 %collective-permute-start.23 = (bf16[768,128]{1,0:T(8,128)(2,1)S(1)}, bf16[768,128]{1,0:T(8,128)(2,1)S(1)}, u32[]{:S(2)}, u32[]{:S(2)}) collective-permute-start(bf16[768,128]{1,0:T(8,128)(2,1)S(1)} %get-tuple-element.57.refs_0_), channel_id=1, source_target_pairs={{0,24},{4,28},{8,16},{12,20},{16,8},{20,12},{24,0},{28,4},{1,25},{... | collective-permute-start | bytes 589832 | tf_op jit(solution)/shard_map/out/ppermute | solution.py:61
  97.0 16.3 %collective-permute-start.22 = (bf16[768,128]{1,0:T(8,128)(2,1)S(1)}, bf16[768,128]{1,0:T(8,128)(2,1)S(1)}, u32[]{:S(2)}, u32[]{:S(2)}) collective-permute-start(bf16[768,128]{1,0:T(8,128)(2,1)S(1)} %get-tuple-element.57.refs_0_), channel_id=1, source_target_pairs={{0,16},{4,20},{8,24},{12,28},{16,0},{20,4},{24,8},{28,12},{1,17},{... | collective-permute-start | bytes 589832 | tf_op jit(solution)/shard_map/out/ppermute | solution.py:61
  97.1 16.2 %collective-permute-start.21 = (bf16[768,128]{1,0:T(8,128)(2,1)S(1)}, bf16[768,128]{1,0:T(8,128)(2,1)S(1)}, u32[]{:S(2)}, u32[]{:S(2)}) collective-permute-start(bf16[768,128]{1,0:T(8,128)(2,1)S(1)} %get-tuple-element.57.refs_0_), channel_id=1, source_target_pairs={{0,8},{4,12},{8,0},{12,4},{16,24},{20,28},{24,16},{28,20},{1,9},{5... | collective-permute-start | bytes 589832 | tf_op jit(solution)/shard_map/out/ppermute | solution.py:61
  115.6 8.8 %collective-permute-start.19 = (bf16[256,128]{1,0:T(8,128)(2,1)S(1)}, bf16[256,128]{1,0:T(8,128)(2,1)S(1)}, u32[]{:S(2)}, u32[]{:S(2)}) collective-permute-start(bf16[256,128]{1,0:T(8,128)(2,1)S(1)} %get-tuple-element.56.refs_0_), channel_id=1, source_target_pairs={{0,24},{4,28},{8,16},{12,20},{16,8},{20,12},{24,0},{28,4},{1,25},{... | collective-permute-start | bytes 196616 | tf_op jit(solution)/shard_map/own_out/ppermute | solution.py:61
  118.9 14.3 %collective-permute-start.25 = (bf16[256,768]{1,0:T(8,128)(2,1)S(1)}, bf16[256,768]{1,0:T(8,128)(2,1)S(1)}, u32[]{:S(2)}, u32[]{:S(2)}) collective-permute-start(bf16[256,768]{1,0:T(8,128)(2,1)S(1)} %get-tuple-element.58), channel_id=1, source_target_pairs={{2,0},{3,1},{0,2},{1,3},{6,4},{7,5},{4,6},{5,7},{10,8},{11,9},{8,1... | collective-permute-start | bytes 1179656 | tf_op jit(solution)/shard_map/out/ppermute | solution.py:66
  121.7 18.2 %collective-permute-start.26 = (bf16[256,768]{1,0:T(8,128)(2,1)S(1)}, bf16[256,768]{1,0:T(8,128)(2,1)S(1)}, u32[]{:S(2)}, u32[]{:S(2)}) collective-permute-start(bf16[256,768]{1,0:T(8,128)(2,1)S(1)} %get-tuple-element.59), channel_id=1, source_target_pairs={{3,0},{0,1},{1,2},{2,3},{7,4},{4,5},{5,6},{6,7},{11,8},{8,9},{9,10... | collective-permute-start | bytes 1179656 | tf_op jit(solution)/shard_map/out/ppermute | solution.py:66
  123.2 17.1 %collective-permute-start.27 = (bf16[256,768]{1,0:T(8,128)(2,1)S(1)}, bf16[256,768]{1,0:T(8,128)(2,1)S(1)}, u32[]{:S(2)}, u32[]{:S(2)}) collective-permute-start(bf16[256,768]{1,0:T(8,128)(2,1)S(1)} %get-tuple-element.60), channel_id=1, source_target_pairs={{1,0},{2,1},{3,2},{0,3},{5,4},{6,5},{7,6},{4,7},{9,8},{10,9},{11,1... | collective-permute-start | bytes 1179656 | tf_op jit(solution)/shard_map/out/ppermute | solution.py:66
  124.4 4.6 %collective-permute-start.18 = (bf16[256,128]{1,0:T(8,128)(2,1)S(1)}, bf16[256,128]{1,0:T(8,128)(2,1)S(1)}, u32[]{:S(2)}, u32[]{:S(2)}) collective-permute-start(bf16[256,128]{1,0:T(8,128)(2,1)S(1)} %get-tuple-element.56.refs_0_), channel_id=1, source_target_pairs={{0,16},{4,20},{8,24},{12,28},{16,0},{20,4},{24,8},{28,12},{1,17},{... | collective-permute-start | bytes 196616 | tf_op jit(solution)/shard_map/own_out/ppermute | solution.py:61
  124.4 4.8 %collective-permute-start.17 = (bf16[256,128]{1,0:T(8,128)(2,1)S(1)}, bf16[256,128]{1,0:T(8,128)(2,1)S(1)}, u32[]{:S(2)}, u32[]{:S(2)}) collective-permute-start(bf16[256,128]{1,0:T(8,128)(2,1)S(1)} %get-tuple-element.56.refs_0_), channel_id=1, source_target_pairs={{0,8},{4,12},{8,0},{12,4},{16,24},{20,28},{24,16},{28,20},{1,9},{5... | collective-permute-start | bytes 196616 | tf_op jit(solution)/shard_map/own_out/ppermute | solution.py:61
  (10 other events, 46.2 us)
where the time goes:
time: 141 us
  waiting for transfers between devices  77.4 us (55%)
  starting transfers between devices  41.1 us (29%)
  Pallas kernels  19.1 us (14%)
  local copies, waits for them, and re-layouts  2.35 us (2%)
    ppermute x22, waiting for transfers between devices, swap(): return lax.ppermute(block, axis, [(i, i ^ bits) for i in range(count)])  57.5 us
    ppermute x22, starting transfers between devices, swap(): return lax.ppermute(block, axis, [(i, i ^ bits) for i in range(count)])  33 us
    ppermute x6, waiting for transfers between devices, shift(): lax.ppermute(block, axis, [((i + step) % count, i) for i in range(count)])  20 us
    pallas_call x18, Pallas kernels, call(): return lambda *args: made(*args, *after)  19.1 us
    ppermute x6, starting transfers between devices, shift(): lax.ppermute(block, axis, [((i + step) % count, i) for i in range(count)])  8.13 us
  transfers between devices with their start and end apart: 28, of which 19 were waited for; matrix products, arithmetic and copies ran while one was open for 0% of the time, Pallas kernels for 10%

commit v1 on v0

--- a/solution.py
+++ b/solution.py
@@ -90,31 +90,6 @@
 
     shape = ((DL, 2 * HEAD), BF16)
     return call(kernel, [shape, shape], [HBM], [pltpu.SemaphoreType.DMA((12,))])(w3)
-
-
-def out_weight_heads(w):
-    def kernel(w_ref, out_ref, sems):
-        mx = lax.axis_index("mx")
-        z = mx >> 1
-        copies = []
-        for side in range(2):
-            lane = (mx & 1) ^ side
-            for j in range(4):
-                head = lane * 4 + (z ^ j)
-                copies.append(
-                    pltpu.make_async_copy(
-                        w_ref.at[pl.ds(pl.multiple_of(head * HD, HD), HD), :],
-                        out_ref.at[pl.ds((side * 4 + j) * HD, HD), :],
-                        sems.at[len(copies)],
-                    )
-                )
-        for copy in copies:
-            copy.start()
-        for copy in copies:
-            copy.wait()
-
-    (out,) = call(kernel, [(w.shape, BF16)], [HBM], [pltpu.SemaphoreType.DMA((8,))])(w)
-    return out
 
 
 def table(counts, owner, target):
@@ -361,8 +336,8 @@
 def route(places, mine, other):
     def kernel(places_ref, mine_ref, other_ref, *outs):
         for n in range(GRP):
-            out_ref, at = (outs[0], n) if n < 6 else (outs[1], n - 6)
-            place = slice(at * BLK, (at + 1) * BLK)
+            out_ref = outs[n // 2]
+            place = slice((n % 2) * BLK, (n % 2 + 1) * BLK)
             src = places_ref[n]
             row = pl.multiple_of((src & 7) * BLK, BLK)
 
@@ -378,25 +353,38 @@
             def _():
                 out_ref[place, :] = other_ref[pl.ds(row, BLK), :]
 
-    outs = [((3 * SH, HD), BF16), ((SH, HD), BF16)]
-    return call(kernel, outs, [SMEM, VMEM, VMEM])(places, mine, other)
-
-
-def project(block, wo, dtype, after=()):
-    lane = join([block] + [swap(block, "mx", 2 * j) for j in (1, 2, 3)], 1, after)
-    sib = swap(lane, "mx", 1)
-    count = block.shape[0] // SH
-
-    def kernel(lane_ref, sib_ref, w_ref, *outs):
-        for i, out_ref in enumerate(outs):
-            at = slice(i * SH, (i + 1) * SH)
-            for n in range(3):
-                columns = slice(n * 256, (n + 1) * 256)
-                tile = jnp.dot(lane_ref[at, :], w_ref[0 : 4 * HD, columns], preferred_element_type=F32)
-                tile = tile + jnp.dot(sib_ref[at, :], w_ref[4 * HD :, columns], preferred_element_type=F32)
-                out_ref[:, columns] = tile.astype(dtype)
-
-    return call(kernel, [((SH, DL), dtype)] * count, [VMEM] * 3)(lane, sib, wo)
+    return call(kernel, [((SH, HD), BF16)] * 4, [SMEM, VMEM, VMEM])(places, mine, other)
+
+
+def lane_rows(blocks):
+    def kernel(*refs):
+        z = lax.axis_index("mx") >> 1
+        for j, ref in enumerate(refs[:-1]):
+            for d in range(4):
+                at = pl.multiple_of((d * 4 + (z ^ j)) * HD, HD)
+                refs[-1][:, pl.ds(at, HD)] = ref[:, d * HD : (d + 1) * HD]
+
+    (out,) = call(kernel, [((SH, 16 * HD), BF16)], [VMEM] * 4)(*blocks)
+    return out
+
+
+def project(lane, sib, weight):
+    def kernel(lane_ref, sib_ref, w_ref, out_ref):
+        my = lax.axis_index("my")
+        side = lax.axis_index("mx") & 1
+        for n in range(3):
+            columns = slice(n * 256, (n + 1) * 256)
+            total = jnp.zeros((SH, 256), F32)
+            for d, offset in enumerate((0, 1, 3, 2)):
+                base = ((my + offset) & 3) * R
+                for ref, lane_side in ((lane_ref, side), (sib_ref, 1 - side)):
+                    row = pl.multiple_of(base + lane_side * 4 * HD, 4 * HD)
+                    part = ref[:, d * 4 * HD : (d + 1) * 4 * HD]
+                    total = total + jnp.dot(part, w_ref[pl.ds(row, 4 * HD), columns], preferred_element_type=F32)
+            out_ref[:, columns] = total.astype(BF16)
+
+    (out,) = call(kernel, [((SH, DL), BF16)], [VMEM] * 3, limit=24)(lane, sib, weight)
+    return out
 
 
 def shards(patches, tile_counts, image_owner, block_target, qkv_weight, out_weight):
@@ -409,7 +397,6 @@
         sib_send = swap(theirs_send, "mx", 1)
         sib_keep = swap(theirs_keep, "mx", 1)
         own_keep, own_send = weight_heads(w3, False)
-        wo = out_weight_heads(out_weight)
         places = table(tile_counts, image_owner, block_target)
     weights = (own_keep, sib_keep, own_send, sib_send)
 
@@ -422,6 +409,9 @@
     with scope("chunk12"):
         x12 = join([next_rows, last_rows], 0, (got0,))
         s12 = swap(x12, "mx", 1)
+    with scope("out_weight"):
+        (held,) = gate([out_weight], (x12,))
+        whole_weight = lax.all_gather(held, "my", axis=0, tiled=True)
     with scope("sum0"):
         own0, next0 = keep_part(patches, s0, own_keep, sib_keep, stat0, got0)
         end0 = swap(next0, "mx", 4)
@@ -429,9 +419,9 @@
         part12, stat12, _ = send_part(x12, s12, own_send, sib_send, (next0,))
         got12 = swap(part12, "mx", 2)
     with scope("chunk3"):
-        (x3,) = gate([x3], (part12,))
+        (x3,) = gate([x3], (part12, end0))
         s3 = swap(x3, "mx", 1)
-        own3, p1, p2, p3, note = last_part(x3, s3, weights, (stat0, stat12), (part12, wo, places))
+        own3, p1, p2, p3, note = last_part(x3, s3, weights, (stat0, stat12), (part12, places))
         got3 = [swap(p1, "mx", 2), swap(p2, "mx", 4), swap(p3, "mx", 6)]
     with scope("sum12"):
         own12, next1, next2, tot0 = keep_part(x12, s12, own_keep, sib_keep, stat12, got12, (own0, end0), 2, (own3,))
@@ -442,16 +432,13 @@
     with scope("attention"):
         attended = attention(places, coef, cs, tot0, own12, ends, tot3)
         other = swap(attended, "img", 1)
-        across, here = route(places, attended, other)
+        far, up, down, own = route(places, attended, other)
+        near = [own, shift(down, "my", 1), shift(up, "my", -1), shift(far, "my", 2)]
 
     with scope("out"):
-        far, up, down = project(across, wo, BF16)
-        arrived = [shift(far, "my", 2), shift(up, "my", -1), shift(down, "my", 1)]
-    with scope("own_out"):
-        (mine,) = project(here, wo, F32)
-    for one in arrived:
-        mine = mine + one.astype(F32)
-    return mine.astype(BF16)
+        block = join(near, 1)
+        lane = lane_rows([block] + [swap(block, "mx", 2 * j) for j in (1, 2, 3)])
+        return project(lane, swap(lane, "mx", 1), whole_weight)
 
 
 def solution(mesh):

time: 141 us -> 169 us (1.20); the launches traced: 141 us -> 167 us
  between operations: 0.22 us -> 13.6 us
  local copies, waits for them, and re-layouts: 2.35 us -> 12.6 us
  waiting for transfers between devices: 77.4 us -> 84 us
  starting transfers between devices: 41.1 us -> 39.2 us
    ppermute x22 -> x18, waiting for transfers between devices: 57.5 us -> 73.4 us  [swap(): return lax.ppermute(block, axis, [(i, i ^ bits) for i in range(count)])]
    unnamed x12 -> x35, local copies, waits for them, and re-layouts: 2.35 us -> 12.6 us
    ppermute x6, waiting for transfers between devices: 20 us -> 10.6 us  [shift(): lax.ppermute(block, axis, [((i + step) % count, i) for i in range(count)])]
    pallas_call x18 -> x17, Pallas kernels: 19.1 us -> 17.7 us  [call(): return lambda *args: made(*args, *after)]
    ppermute x22 -> x18, starting transfers between devices: 33 us -> 32.5 us  [swap(): return lax.ppermute(block, axis, [(i, i ^ bits) for i in range(count)])]
  transfers between devices with their start and end apart: 28 -> 25, of which waited for: 19 -> 18; matrix products, arithmetic and copies ran while one was open for 0% -> 0% of each run, Pallas kernels for 10% -> 9%
where the time goes in v1:
time: 169 us; the launch traced here: 167 us
  waiting for transfers between devices  84 us (50%)
  starting transfers between devices  39.2 us (23%)
  Pallas kernels  17.7 us (10%)
  between operations  13.6 us (8%)
  local copies, waits for them, and re-layouts  12.6 us (7%)
    ppermute x18, waiting for transfers between devices, swap(): return lax.ppermute(block, axis, [(i, i ^ bits) for i in range(count)])  73.4 us
    ppermute x18, starting transfers between devices, swap(): return lax.ppermute(block, axis, [(i, i ^ bits) for i in range(count)])  32.5 us
    pallas_call x17, Pallas kernels, call(): return lambda *args: made(*args, *after)  17.7 us
    unnamed x35, local copies, waits for them, and re-layouts  12.6 us
    ppermute x6, waiting for transfers between devices, shift(): lax.ppermute(block, axis, [((i + step) % count, i) for i in range(count)])  10.6 us
    ppermute x6, starting transfers between devices, shift(): lax.ppermute(block, axis, [((i + step) % count, i) for i in range(count)])  6.69 us
  transfers between devices with their start and end apart: 25, of which 18 were waited for; matrix products, arithmetic and copies ran while one was open for 0% of the time, Pallas kernels for 9%

profile of v1, /device:TPU:1, one launch (start us, length us, event | category | flops | bytes accessed | tf_op | source)
XLA Modules:
  0.0 167.1 jit_solution(1167542096220655578)
XLA Ops:
  6.5 2.7 %copy.12.refs_0_ = bf16[1024,768]{1,0:T(8,128)(2,1)} copy(bf16[1024,768]{1,0:T(8,128)(2,1)} %param.11) | data formatting | bytes 3145728
  9.2 2.3 %copy-done = bf16[768,3,1024]{2,0,1:T(8,128)(2,1)S(1)} copy-done((bf16[768,3,1024]{2,0,1:T(8,128)(2,1)S(1)}, bf16[768,3,1024]{2,0,1:T(8,128)(2,1)}, u32[]{:S(2)}) %copy-start) | copy-done | bytes 4718616
  12.3 3.3 %collective-permute-start.1 = (bf16[768,768]{1,0:T(8,128)(2,1)S(1)}, bf16[768,768]{1,0:T(8,128)(2,1)S(1)}, u32[]{:S(2)}, u32[]{:S(2)}) collective-permute-start(bf16[768,768]{1,0:T(8,128)(2,1)S(1)} %get-tuple-element.33), channel_id=1, source_target_pairs={{0,4},{4,0},{8,12},{12,8},{16,20},{20,16},{24,28},{28,24},{1,5},{5... | collective-permute-start | bytes 3538952 | tf_op jit(solution)/shard_map/weights/ppermute | solution.py:61
  21.0 5.2 %collective-permute-done.3.refs_0_ = bf16[256,768]{1,0:T(8,128)(2,1)S(1)} collective-permute-done((bf16[256,768]{1,0:T(8,128)(2,1)S(1)}, bf16[256,768]{1,0:T(8,128)(2,1)S(1)}, u32[]{:S(2)}, u32[]{:S(2)}) %collective-permute-start.3) | collective-permute-done | bytes 393248 | tf_op jit(solution)/shard_map/rows_near/ppermute | solution.py:66
  27.8 2.8 %collective-permute-done.5.refs_2_.refs_5_ = bf16[256,768]{1,0:T(8,128)(2,1)S(1)} collective-permute-done((bf16[256,768]{1,0:T(8,128)(2,1)S(1)}, bf16[256,768]{1,0:T(8,128)(2,1)S(1)}, u32[]{:S(2)}, u32[]{:S(2)}) %collective-permute-start.5) | collective-permute-done | bytes 393248 | tf_op jit(solution)/shard_map/chunk0/ppermute | solution.py:61
  40.5 2.8 %chunk12.3 = (bf16[512,768]{1,0:T(8,128)(2,1)S(1)}, f32[512,128]{1,0:T(8,128)S(1)}, bf16[512,768]{1,0:T(8,128)(2,1)}) custom-call(bf16[512,768]{1,0:T(8,128)(2,1)S(1)} %chunk12.2.refs_0_.refs_1_, bf16[512,768]{1,0:T(8,128)(2,1)S(1)} %collective-permute-done.6.refs_1_, bf16[768,768]{1,0:T(8,128)(2,1)S(1)} %copy-done.2, ...), custom_call_target="tpu_custom_call" | custom-call | bytes 1024 | tf_op jit(solution)/shard_map/chunk12/pallas_call | solution.py:46
  43.9 3.0 %collective-permute-start.8 = (bf16[256,384]{1,0:T(8,128)(2,1)S(1)}, bf16[256,384]{1,0:T(8,128)(2,1)S(1)}, u32[]{:S(2)}, u32[]{:S(2)}) collective-permute-start(bf16[256,384]{1,0:T(8,128)(2,1)S(1)} %get-tuple-element.39.refs_4_), channel_id=1, source_target_pairs={{0,16},{4,20},{8,24},{12,28},{16,0},{20,4},{24,8},{28,12},{1,17},{... | collective-permute-start | bytes 589832 | tf_op jit(solution)/shard_map/sum0/ppermute | solution.py:61
  46.9 17.8 %collective-permute-done.8.refs_2_.refs_7_ = bf16[256,384]{1,0:T(8,128)(2,1)S(1)} collective-permute-done((bf16[256,384]{1,0:T(8,128)(2,1)S(1)}, bf16[256,384]{1,0:T(8,128)(2,1)S(1)}, u32[]{:S(2)}, u32[]{:S(2)}) %collective-permute-start.8) | collective-permute-done | bytes 196640 | tf_op jit(solution)/shard_map/sum0/ppermute | solution.py:61
  68.8 3.8 %collective-permute-start.10 = (bf16[288,384]{1,0:T(8,128)(2,1)S(1)}, bf16[288,384]{1,0:T(8,128)(2,1)S(1)}, u32[]{:S(2)}, u32[]{:S(2)}) collective-permute-start(bf16[288,384]{1,0:T(8,128)(2,1)S(1)} %get-tuple-element.43), channel_id=1, source_target_pairs={{0,8},{4,12},{8,0},{12,4},{16,24},{20,28},{24,16},{28,20},{1,9},{5... | collective-permute-start | bytes 663560 | tf_op jit(solution)/shard_map/chunk3/ppermute | solution.py:61
  81.2 16.8 %collective-permute-done.11.refs_2_ = bf16[288,384]{1,0:T(8,128)(2,1)S(1)} collective-permute-done((bf16[288,384]{1,0:T(8,128)(2,1)S(1)}, bf16[288,384]{1,0:T(8,128)(2,1)S(1)}, u32[]{:S(2)}, u32[]{:S(2)}) %collective-permute-start.11) | collective-permute-done | bytes 221216 | tf_op jit(solution)/shard_map/chunk3/ppermute | solution.py:61
  98.3 8.5 %collective-permute-done.14.refs_5_ = bf16[256,384]{1,0:T(8,128)(2,1)S(1)} collective-permute-done((bf16[256,384]{1,0:T(8,128)(2,1)S(1)}, bf16[256,384]{1,0:T(8,128)(2,1)S(1)}, u32[]{:S(2)}, u32[]{:S(2)}) %collective-permute-start.14) | collective-permute-done | bytes 196640 | tf_op jit(solution)/shard_map/sum12/ppermute | solution.py:61
  106.8 4.2 %collective-permute-done.15.refs_6_ = bf16[256,384]{1,0:T(8,128)(2,1)S(1)} collective-permute-done((bf16[256,384]{1,0:T(8,128)(2,1)S(1)}, bf16[256,384]{1,0:T(8,128)(2,1)S(1)}, u32[]{:S(2)}, u32[]{:S(2)}) %collective-permute-start.15) | collective-permute-done | bytes 196640 | tf_op jit(solution)/shard_map/sum12/ppermute | solution.py:61
  111.1 2.9 %attention.2.refs_1_ = bf16[1024,128]{1,0:T(8,128)(2,1)S(1)} custom-call(s32[16]{0:T(128)S(1)} %weights.3.refs_9_.refs_0_, f32[1024,128]{1,0:T(8,128)S(1)} %get-tuple-element.47.refs_1_, f32[8,384]{1,0:T(8,128)S(1)} %get-tuple-element.48.refs_2_, f32[256,384]{1,0:T(8,128)S(1)} %get-tuple-element.50.refs_3_, f32[512,384]{1,0:T(8,128)S(1)} %get-tuple-element.51.refs_4_, ...), custom_call_target="tpu_custom_call" | custom-call | bytes 1024 | tf_op jit(solution)/shard_map/attention/pallas_call | solution.py:46
  115.4 5.0 %collective-permute-done.16.refs_2_ = bf16[1024,128]{1,0:T(8,128)(2,1)S(1)} collective-permute-done((bf16[1024,128]{1,0:T(8,128)(2,1)S(1)}, bf16[1024,128]{1,0:T(8,128)(2,1)S(1)}, u32[]{:S(2)}, u32[]{:S(2)}) %collective-permute-start.16) | collective-permute-done | bytes 262176 | tf_op jit(solution)/shard_map/attention/ppermute | solution.py:61
  121.1 2.8 %collective-permute-start.17 = (bf16[256,128]{1,0:T(8,128)(2,1)S(1)}, bf16[256,128]{1,0:T(8,128)(2,1)S(1)}, u32[]{:S(2)}, u32[]{:S(2)}) collective-permute-start(bf16[256,128]{1,0:T(8,128)(2,1)S(1)} %get-tuple-element.56), channel_id=1, source_target_pairs={{1,0},{2,1},{3,2},{0,3},{5,4},{6,5},{7,6},{4,7},{9,8},{10,9},{11,1... | collective-permute-start | bytes 196616 | tf_op jit(solution)/shard_map/attention/ppermute | solution.py:66
  125.2 3.7 %collective-permute-done.18.refs_2_ = bf16[256,128]{1,0:T(8,128)(2,1)S(1)} collective-permute-done((bf16[256,128]{1,0:T(8,128)(2,1)S(1)}, bf16[256,128]{1,0:T(8,128)(2,1)S(1)}, u32[]{:S(2)}, u32[]{:S(2)}) %collective-permute-start.18) | collective-permute-done | bytes 65568 | tf_op jit(solution)/shard_map/attention/ppermute | solution.py:66
  129.9 2.7 %collective-permute-start.22 = (bf16[256,512]{1,0:T(8,128)(2,1)S(1)}, bf16[256,512]{1,0:T(8,128)(2,1)S(1)}, u32[]{:S(2)}, u32[]{:S(2)}) collective-permute-start(bf16[256,512]{1,0:T(8,128)(2,1)S(1)} %out.3.refs_0_), channel_id=1, source_target_pairs={{0,24},{4,28},{8,16},{12,20},{16,8},{20,12},{24,0},{28,4},{1,25},{... | collective-permute-start | bytes 786440 | tf_op jit(solution)/shard_map/out/ppermute | solution.py:61
  132.6 3.7 %collective-permute-done.20.refs_1_ = bf16[256,512]{1,0:T(8,128)(2,1)S(1)} collective-permute-done((bf16[256,512]{1,0:T(8,128)(2,1)S(1)}, bf16[256,512]{1,0:T(8,128)(2,1)S(1)}, u32[]{:S(2)}, u32[]{:S(2)}) %collective-permute-start.20) | collective-permute-done | bytes 262176 | tf_op jit(solution)/shard_map/out/ppermute | solution.py:61
  136.3 3.6 %collective-permute-done.21.refs_2_ = bf16[256,512]{1,0:T(8,128)(2,1)S(1)} collective-permute-done((bf16[256,512]{1,0:T(8,128)(2,1)S(1)}, bf16[256,512]{1,0:T(8,128)(2,1)S(1)}, u32[]{:S(2)}, u32[]{:S(2)}) %collective-permute-start.21) | collective-permute-done | bytes 262176 | tf_op jit(solution)/shard_map/out/ppermute | solution.py:61
  139.9 3.8 %collective-permute-done.22.refs_3_ = bf16[256,512]{1,0:T(8,128)(2,1)S(1)} collective-permute-done((bf16[256,512]{1,0:T(8,128)(2,1)S(1)}, bf16[256,512]{1,0:T(8,128)(2,1)S(1)}, u32[]{:S(2)}, u32[]{:S(2)}) %collective-permute-start.22) | collective-permute-done | bytes 262176 | tf_op jit(solution)/shard_map/out/ppermute | solution.py:61
  144.0 8.7 %collective-permute-start.23 = (bf16[256,2048]{1,0:T(8,128)(2,1)S(1)}, bf16[256,2048]{1,0:T(8,128)(2,1)S(1)}, u32[]{:S(2)}, u32[]{:S(2)}) collective-permute-start(bf16[256,2048]{1,0:T(8,128)(2,1)S(1)} %out.4.refs_0_), channel_id=1, source_target_pairs={{0,4},{4,0},{8,12},{12,8},{16,20},{20,16},{24,28},{28,24},{1,5},{5... | collective-permute-start | bytes 3145736 | tf_op jit(solution)/shard_map/out/ppermute | solution.py:61
  152.6 2.3 %collective-permute-done.23.refs_1_ = bf16[256,2048]{1,0:T(8,128)(2,1)S(1)} collective-permute-done((bf16[256,2048]{1,0:T(8,128)(2,1)S(1)}, bf16[256,2048]{1,0:T(8,128)(2,1)S(1)}, u32[]{:S(2)}, u32[]{:S(2)}) %collective-permute-start.23) | collective-permute-done | bytes 1048608 | tf_op jit(solution)/shard_map/out/ppermute | solution.py:61
  154.9 2.8 %copy-done.3 = bf16[4096,768]{1,0:T(8,128)(2,1)S(1)} copy-done((bf16[4096,768]{1,0:T(8,128)(2,1)S(1)}, bf16[4096,768]{1,0:T(8,128)(2,1)}, u32[]{:S(2)}) %copy-start.3) | copy-done | bytes 6291480
  157.7 2.5 %out.5 = bf16[256,768]{1,0:T(8,128)(2,1)} custom-call(bf16[256,2048]{1,0:T(8,128)(2,1)S(1)} %out.4.refs_0_, bf16[256,2048]{1,0:T(8,128)(2,1)S(1)} %collective-permute-done.23.refs_1_, bf16[4096,768]{1,0:T(8,128)(2,1)S(1)} %copy-done.3), custom_call_target="tpu_custom_call" | custom-call | bytes 1024 | tf_op jit(solution)/shard_map/out/pallas_call | solution.py:46
  (79 shorter events, 35.8 us)
Async XLA Ops:
  6.5 148.4 %all-gather.2.cloned.1.call-start = ((), (), s32[]{:S(2)}) async-start(), calls=%async_computation | async-start | bytes 7864320 | tf_op jit(solution)/shard_map/out_weight/all_gather | solution.py:414
  12.3 6.4 %collective-permute-start.1 = (bf16[768,768]{1,0:T(8,128)(2,1)S(1)}, bf16[768,768]{1,0:T(8,128)(2,1)S(1)}, u32[]{:S(2)}, u32[]{:S(2)}) collective-permute-start(bf16[768,768]{1,0:T(8,128)(2,1)S(1)} %get-tuple-element.33), channel_id=1, source_target_pairs={{0,4},{4,0},{8,12},{12,8},{16,20},{20,16},{24,28},{28,24},{1,5},{5... | collective-permute-start | bytes 3538952 | tf_op jit(solution)/shard_map/weights/ppermute | solution.py:61
  15.7 3.0 %collective-permute-start = (bf16[256,768]{1,0:T(8,128)(2,1)S(1)}, bf16[256,768]{1,0:T(8,128)(2,1)S(1)}, u32[]{:S(2)}, u32[]{:S(2)}) collective-permute-start(bf16[256,768]{1,0:T(8,128)(2,1)S(1)} %copy-done.4), channel_id=1, source_target_pairs={{0,4},{4,0},{8,12},{12,8},{16,20},{20,16},{24,28},{28,24},{1,5},{5... | collective-permute-start | bytes 1179656 | tf_op jit(solution)/shard_map/chunk0/ppermute | solution.py:61
  15.8 10.3 %collective-permute-start.3 = (bf16[256,768]{1,0:T(8,128)(2,1)S(1)}, bf16[256,768]{1,0:T(8,128)(2,1)S(1)}, u32[]{:S(2)}, u32[]{:S(2)}) collective-permute-start(bf16[256,768]{1,0:T(8,128)(2,1)S(1)} %copy-done.4), channel_id=1, source_target_pairs={{1,0},{2,1},{3,2},{0,3},{5,4},{6,5},{7,6},{4,7},{9,8},{10,9},{11,1... | collective-permute-start | bytes 1179656 | tf_op jit(solution)/shard_map/rows_near/ppermute | solution.py:66
  16.6 11.2 %collective-permute-start.4 = (bf16[256,768]{1,0:T(8,128)(2,1)S(1)}, bf16[256,768]{1,0:T(8,128)(2,1)S(1)}, u32[]{:S(2)}, u32[]{:S(2)}) collective-permute-start(bf16[256,768]{1,0:T(8,128)(2,1)S(1)} %copy-done.4), channel_id=1, source_target_pairs={{3,0},{0,1},{1,2},{2,3},{7,4},{4,5},{5,6},{6,7},{11,8},{8,9},{9,10... | collective-permute-start | bytes 1179656 | tf_op jit(solution)/shard_map/rows_near/ppermute | solution.py:66
  20.4 10.1 %collective-permute-start.5 = (bf16[256,768]{1,0:T(8,128)(2,1)S(1)}, bf16[256,768]{1,0:T(8,128)(2,1)S(1)}, u32[]{:S(2)}, u32[]{:S(2)}) collective-permute-start(bf16[256,768]{1,0:T(8,128)(2,1)S(1)} %get-tuple-element.35), channel_id=1, source_target_pairs={{0,8},{4,12},{8,0},{12,4},{16,24},{20,28},{24,16},{28,20},{1,9},{5... | collective-permute-start | bytes 1179656 | tf_op jit(solution)/shard_map/chunk0/ppermute | solution.py:61
  31.4 4.9 %collective-permute-start.7 = (bf16[768,768]{1,0:T(8,128)(2,1)}, bf16[768,768]{1,0:T(8,128)(2,1)S(1)}, u32[]{:S(2)}, u32[]{:S(2)}) collective-permute-start(bf16[768,768]{1,0:T(8,128)(2,1)} %copy-done.15), channel_id=1, source_target_pairs={{0,4},{4,0},{8,12},{12,8},{16,20},{20,16},{24,28},{28,24},{1,5},{5... | collective-permute-start | bytes 3538952 | tf_op jit(solution)/shard_map/weights/ppermute | solution.py:61
  32.9 7.2 %collective-permute-start.6 = (bf16[512,768]{1,0:T(8,128)(2,1)S(1)}, bf16[512,768]{1,0:T(8,128)(2,1)S(1)}, u32[]{:S(2)}, u32[]{:S(2)}) collective-permute-start(bf16[512,768]{1,0:T(8,128)(2,1)S(1)} %chunk12.2.refs_0_.refs_1_), channel_id=1, source_target_pairs={{0,4},{4,0},{8,12},{12,8},{16,20},{20,16},{24,28},{28,24},{1,5},{5... | collective-permute-start | bytes 2359304 | tf_op jit(solution)/shard_map/chunk12/ppermute | solution.py:61
  33.0 13.8 %collective-permute-start.2 = (bf16[256,768]{1,0:T(8,128)(2,1)}, bf16[256,768]{1,0:T(8,128)(2,1)S(1)}, u32[]{:S(2)}, u32[]{:S(2)}) collective-permute-start(bf16[256,768]{1,0:T(8,128)(2,1)} %copy-done.16), channel_id=1, source_target_pairs={{2,0},{3,1},{0,2},{1,3},{6,4},{7,5},{4,6},{5,7},{10,8},{11,9},{8,1... | collective-permute-start | bytes 1179656 | tf_op jit(solution)/shard_map/rows_far/ppermute | solution.py:66
  43.3 31.6 %collective-permute-start.13 = (bf16[512,768]{1,0:T(8,128)(2,1)S(1)}, bf16[512,768]{1,0:T(8,128)(2,1)S(1)}, u32[]{:S(2)}, u32[]{:S(2)}) collective-permute-start(bf16[512,768]{1,0:T(8,128)(2,1)S(1)} %get-tuple-element.40.refs_1_.refs_8_), channel_id=1, source_target_pairs={{0,8},{4,12},{8,0},{12,4},{16,24},{20,28},{24,16},{28,20},{1,9},{5... | collective-permute-start | bytes 2359304 | tf_op jit(solution)/shard_map/chunk12/ppermute | solution.py:61
  43.9 20.8 %collective-permute-start.8 = (bf16[256,384]{1,0:T(8,128)(2,1)S(1)}, bf16[256,384]{1,0:T(8,128)(2,1)S(1)}, u32[]{:S(2)}, u32[]{:S(2)}) collective-permute-start(bf16[256,384]{1,0:T(8,128)(2,1)S(1)} %get-tuple-element.39.refs_4_), channel_id=1, source_target_pairs={{0,16},{4,20},{8,24},{12,28},{16,0},{20,4},{24,8},{28,12},{1,17},{... | collective-permute-start | bytes 589832 | tf_op jit(solution)/shard_map/sum0/ppermute | solution.py:61
  68.8 12.4 %collective-permute-start.10 = (bf16[288,384]{1,0:T(8,128)(2,1)S(1)}, bf16[288,384]{1,0:T(8,128)(2,1)S(1)}, u32[]{:S(2)}, u32[]{:S(2)}) collective-permute-start(bf16[288,384]{1,0:T(8,128)(2,1)S(1)} %get-tuple-element.43), channel_id=1, source_target_pairs={{0,8},{4,12},{8,0},{12,4},{16,24},{20,28},{24,16},{28,20},{1,9},{5... | collective-permute-start | bytes 663560 | tf_op jit(solution)/shard_map/chunk3/ppermute | solution.py:61
  72.7 25.3 %collective-permute-start.11 = (bf16[288,384]{1,0:T(8,128)(2,1)S(1)}, bf16[288,384]{1,0:T(8,128)(2,1)S(1)}, u32[]{:S(2)}, u32[]{:S(2)}) collective-permute-start(bf16[288,384]{1,0:T(8,128)(2,1)S(1)} %get-tuple-element.44), channel_id=1, source_target_pairs={{0,16},{4,20},{8,24},{12,28},{16,0},{20,4},{24,8},{28,12},{1,17},{... | collective-permute-start | bytes 663560 | tf_op jit(solution)/shard_map/chunk3/ppermute | solution.py:61
  72.7 25.3 %collective-permute-start.12 = (bf16[288,384]{1,0:T(8,128)(2,1)S(1)}, bf16[288,384]{1,0:T(8,128)(2,1)S(1)}, u32[]{:S(2)}, u32[]{:S(2)}) collective-permute-start(bf16[288,384]{1,0:T(8,128)(2,1)S(1)} %get-tuple-element.45), channel_id=1, source_target_pairs={{0,24},{4,28},{8,16},{12,20},{16,8},{20,12},{24,0},{28,4},{1,25},{... | collective-permute-start | bytes 663560 | tf_op jit(solution)/shard_map/chunk3/ppermute | solution.py:61
  76.6 30.2 %collective-permute-start.14 = (bf16[256,384]{1,0:T(8,128)(2,1)S(1)}, bf16[256,384]{1,0:T(8,128)(2,1)S(1)}, u32[]{:S(2)}, u32[]{:S(2)}) collective-permute-start(bf16[256,384]{1,0:T(8,128)(2,1)S(1)} %get-tuple-element.52), channel_id=1, source_target_pairs={{0,16},{4,20},{8,24},{12,28},{16,0},{20,4},{24,8},{28,12},{1,17},{... | collective-permute-start | bytes 589832 | tf_op jit(solution)/shard_map/sum12/ppermute | solution.py:61
  76.9 34.1 %collective-permute-start.15 = (bf16[256,384]{1,0:T(8,128)(2,1)S(1)}, bf16[256,384]{1,0:T(8,128)(2,1)S(1)}, u32[]{:S(2)}, u32[]{:S(2)}) collective-permute-start(bf16[256,384]{1,0:T(8,128)(2,1)S(1)} %get-tuple-element.53), channel_id=1, source_target_pairs={{0,16},{4,20},{8,24},{12,28},{16,0},{20,4},{24,8},{28,12},{1,17},{... | collective-permute-start | bytes 589832 | tf_op jit(solution)/shard_map/sum12/ppermute | solution.py:61
  114.0 6.4 %collective-permute-start.16 = (bf16[1024,128]{1,0:T(8,128)(2,1)S(1)}, bf16[1024,128]{1,0:T(8,128)(2,1)S(1)}, u32[]{:S(2)}, u32[]{:S(2)}) collective-permute-start(bf16[1024,128]{1,0:T(8,128)(2,1)S(1)} %attention.2.refs_1_), channel_id=1, source_target_pairs={{0,32},{32,0},{64,96},{96,64},{128,160},{160,128},{192,224},{224,1... | collective-permute-start | bytes 786440 | tf_op jit(solution)/shard_map/attention/ppermute | solution.py:61
  121.1 4.1 %collective-permute-start.17 = (bf16[256,128]{1,0:T(8,128)(2,1)S(1)}, bf16[256,128]{1,0:T(8,128)(2,1)S(1)}, u32[]{:S(2)}, u32[]{:S(2)}) collective-permute-start(bf16[256,128]{1,0:T(8,128)(2,1)S(1)} %get-tuple-element.56), channel_id=1, source_target_pairs={{1,0},{2,1},{3,2},{0,3},{5,4},{6,5},{7,6},{4,7},{9,8},{10,9},{11,1... | collective-permute-start | bytes 196616 | tf_op jit(solution)/shard_map/attention/ppermute | solution.py:66
  123.9 5.0 %collective-permute-start.18 = (bf16[256,128]{1,0:T(8,128)(2,1)S(1)}, bf16[256,128]{1,0:T(8,128)(2,1)S(1)}, u32[]{:S(2)}, u32[]{:S(2)}) collective-permute-start(bf16[256,128]{1,0:T(8,128)(2,1)S(1)} %get-tuple-element.57), channel_id=1, source_target_pairs={{3,0},{0,1},{1,2},{2,3},{7,4},{4,5},{5,6},{6,7},{11,8},{8,9},{9,10... | collective-permute-start | bytes 196616 | tf_op jit(solution)/shard_map/attention/ppermute | solution.py:66
  123.9 5.0 %collective-permute-start.19 = (bf16[256,128]{1,0:T(8,128)(2,1)S(1)}, bf16[256,128]{1,0:T(8,128)(2,1)S(1)}, u32[]{:S(2)}, u32[]{:S(2)}) collective-permute-start(bf16[256,128]{1,0:T(8,128)(2,1)S(1)} %get-tuple-element.58), channel_id=1, source_target_pairs={{2,0},{3,1},{0,2},{1,3},{6,4},{7,5},{4,6},{5,7},{10,8},{11,9},{8,1... | collective-permute-start | bytes 196616 | tf_op jit(solution)/shard_map/attention/ppermute | solution.py:66
  129.0 7.4 %collective-permute-start.20 = (bf16[256,512]{1,0:T(8,128)(2,1)S(1)}, bf16[256,512]{1,0:T(8,128)(2,1)S(1)}, u32[]{:S(2)}, u32[]{:S(2)}) collective-permute-start(bf16[256,512]{1,0:T(8,128)(2,1)S(1)} %out.3.refs_0_), channel_id=1, source_target_pairs={{0,8},{4,12},{8,0},{12,4},{16,24},{20,28},{24,16},{28,20},{1,9},{5... | collective-permute-start | bytes 786440 | tf_op jit(solution)/shard_map/out/ppermute | solution.py:61
  129.1 10.8 %collective-permute-start.21 = (bf16[256,512]{1,0:T(8,128)(2,1)S(1)}, bf16[256,512]{1,0:T(8,128)(2,1)S(1)}, u32[]{:S(2)}, u32[]{:S(2)}) collective-permute-start(bf16[256,512]{1,0:T(8,128)(2,1)S(1)} %out.3.refs_0_), channel_id=1, source_target_pairs={{0,16},{4,20},{8,24},{12,28},{16,0},{20,4},{24,8},{28,12},{1,17},{... | collective-permute-start | bytes 786440 | tf_op jit(solution)/shard_map/out/ppermute | solution.py:61
  129.9 13.8 %collective-permute-start.22 = (bf16[256,512]{1,0:T(8,128)(2,1)S(1)}, bf16[256,512]{1,0:T(8,128)(2,1)S(1)}, u32[]{:S(2)}, u32[]{:S(2)}) collective-permute-start(bf16[256,512]{1,0:T(8,128)(2,1)S(1)} %out.3.refs_0_), channel_id=1, source_target_pairs={{0,24},{4,28},{8,16},{12,20},{16,8},{20,12},{24,0},{28,4},{1,25},{... | collective-permute-start | bytes 786440 | tf_op jit(solution)/shard_map/out/ppermute | solution.py:61
  144.0 10.9 %collective-permute-start.23 = (bf16[256,2048]{1,0:T(8,128)(2,1)S(1)}, bf16[256,2048]{1,0:T(8,128)(2,1)S(1)}, u32[]{:S(2)}, u32[]{:S(2)}) collective-permute-start(bf16[256,2048]{1,0:T(8,128)(2,1)S(1)} %out.4.refs_0_), channel_id=1, source_target_pairs={{0,4},{4,0},{8,12},{12,8},{16,20},{20,16},{24,28},{28,24},{1,5},{5... | collective-permute-start | bytes 3145736 | tf_op jit(solution)/shard_map/out/ppermute | solution.py:61
  (18 other events, 127.6 us)
Sparse Core Ops, SparseCore 0:
  31.5 70.6 all-gather.1

commit v2 on v1

--- a/solution.py
+++ b/solution.py
@@ -16,6 +16,7 @@
 HEAD = 3 * HD
 IMG_ROWS = 512
 ORDER = (0, 2, 1, 3)
+FIRST = 160
 EXTRA = 32
 F32 = jnp.float32
 BF16 = jnp.bfloat16
@@ -92,6 +93,21 @@
     return call(kernel, [shape, shape], [HBM], [pltpu.SemaphoreType.DMA((12,))])(w3)
 
 
+def fetch(block, after):
+    rows = block.shape[0] // 4
+
+    def kernel(block_ref, out_ref, sems):
+        parts = [pl.ds(i * rows, rows) for i in range(4)]
+        copies = [pltpu.make_async_copy(block_ref.at[p, :], out_ref.at[p, :], sems.at[i]) for i, p in enumerate(parts)]
+        for copy in copies:
+            copy.start()
+        for copy in copies:
+            copy.wait()
+
+    (out,) = call(kernel, [(block.shape, BF16)], [HBM], [pltpu.SemaphoreType.DMA((4,))], after=after)(block)
+    return out
+
+
 def table(counts, owner, target):
     def kernel(counts_ref, owner_ref, target_ref, out_ref, source):
         group = lax.axis_index("img")
@@ -158,109 +174,98 @@
     return pltpu.VMEM((count + 16, CHIP), BF16)
 
 
-def send_part(xo, xs, wo, ws, after=()):
+def note_terms(note):
+    terms = []
+    for _ in range(3):
+        terms.append(note.astype(BF16).astype(F32))
+        note = note - terms[-1]
+    return jnp.concatenate(terms + [jnp.zeros_like(note)], axis=0).astype(BF16)
+
+
+def read_note(rows):
+    terms = rows.astype(F32)
+    return terms[0:8, :] + terms[8:16, :] + terms[16:24, :]
+
+
+def head_note(sums, columns):
+    return jnp.concatenate([sums, jnp.concatenate(columns + [jnp.zeros((5, HD), F32)], axis=0)], axis=1)
+
+
+def send_part(xo, xs, wo, ws, earlier=(), after=()):
     count = xo.shape[0]
-
-    def kernel(xo_ref, xs_ref, wo_ref, ws_ref, out_ref, stat_ref, copy_ref, rows):
+    last = len(earlier) > 0
+
+    def kernel(xo_ref, xs_ref, wo_ref, ws_ref, *refs):
+        others, (out_ref, stat_ref, copy_ref, rows) = refs[: len(earlier)], refs[len(earlier) :]
         load_rows(rows, xo_ref, xs_ref)
         copy_ref[...] = xo_ref[...]
         stat = row_stats(xo_ref, xs_ref)
-        stat_ref[...] = stat
         center = stat[:, 0:1] / CHIP
+        column_sums = []
         for n in range(3):
             columns = slice(n * 256, (n + 1) * 256)
-            tile, _ = partial_tile(rows, wo_ref, ws_ref, columns, center)
-            out_ref[:, columns] = tile.astype(BF16)
-
-    outs = [((count, 2 * HEAD), BF16), ((count, HD), F32), ((count, DL), BF16)]
-    return call(kernel, outs, [VMEM] * 4, [rows_scratch(count)], after=after)(xo, xs, wo, ws)
-
-
-def keep_part(xo, xs, wo, ws, stat, got, more=None, pieces=1, after=()):
+            tile, sums = partial_tile(rows, wo_ref, ws_ref, columns, center)
+            out_ref[0:count, columns] = tile.astype(BF16)
+            column_sums += [sums[0:1, 0:HD], sums[0:1, HD:256]]
+        if not last:
+            stat_ref[...] = stat
+            return
+        turned = [ref[k * SH : (k + 1) * SH, :].T for ref in others for k in range(ref.shape[0] // SH)] + [stat.T]
+        lines = jnp.concatenate([t[0:1, :] for t in turned] + [t[1:2, :] for t in turned], axis=0)
+        stat_ref[...] = lines
+        for half in range(2):
+            note = head_note(lines, column_sums[3 * half : 3 * half + 3])
+            out_ref[count : count + EXTRA, half * HEAD : (half + 1) * HEAD] = note_terms(note)
+
+    outs = [((count + EXTRA if last else count, 2 * HEAD), BF16), ((8, SH) if last else (count, HD), F32), ((count, DL), BF16)]
+    ins = [VMEM] * (4 + len(earlier))
+    return call(kernel, outs, ins, [rows_scratch(count)], after=after)(xo, xs, wo, ws, *earlier)
+
+
+def keep_part(xo, xs, wo, ws, stat, got, more=None, last=False, after=()):
     count = xo.shape[0]
-    size = count // pieces
     extra = list(more or ())
 
     def kernel(xo_ref, xs_ref, wo_ref, ws_ref, stat_ref, got_ref, *refs):
         refs, rows = refs[:-1], refs[-1]
-        own_ref, sends = refs[len(extra)], refs[len(extra) + 1 : len(extra) + 1 + pieces]
+        own_ref, send_ref = refs[len(extra)], refs[len(extra) + 1]
         load_rows(rows, xo_ref, xs_ref)
-        center = stat_ref[:, 0:1] / CHIP
+        stat = row_stats(xo_ref, xs_ref) if last else stat_ref[...]
+        center = stat[:, 0:1] / CHIP
+        column_sums = {}
         for n in reversed(range(6)):
             columns = slice(n * HD, (n + 1) * HD)
             if n % 2 == 1:
-                pair, _ = partial_tile(rows, wo_ref, ws_ref, slice((n - 1) * HD, (n + 1) * HD), center)
-            tile = pair[:, (n % 2) * HD : (n % 2 + 1) * HD] + got_ref[:, columns].astype(F32)
+                pair, sums = partial_tile(rows, wo_ref, ws_ref, slice((n - 1) * HD, (n + 1) * HD), center)
+            half = slice((n % 2) * HD, (n % 2 + 1) * HD)
+            tile = pair[:, half] + got_ref[0:count, columns].astype(F32)
+            column_sums[n] = sums[0:1, half]
             if n < 3:
                 own_ref[:, columns] = tile
             else:
-                for i, send_ref in enumerate(sends):
-                    send_ref[:, (n - 3) * HD : (n - 2) * HD] = tile[i * size : (i + 1) * size, :].astype(BF16)
+                send_ref[0:count, (n - 3) * HD : (n - 2) * HD] = tile.astype(BF16)
         if extra:
             refs[-1][...] = refs[0][...] + refs[1][...].astype(F32)
-
-    outs = [((count, HEAD), F32)] + [((size, HEAD), BF16)] * pieces
+        if last:
+            under = slice(count, count + EXTRA)
+            send_ref[under, :] = note_terms(head_note(stat_ref[...], [column_sums[n] for n in (3, 4, 5)]))
+            send_ref[count + EXTRA : count + 2 * EXTRA, :] = got_ref[under, HEAD : 2 * HEAD]
+            refs[-2][...] = head_note(stat_ref[...], [column_sums[n] for n in (0, 1, 2)])
+            refs[-1][...] = read_note(got_ref[under, 0:HEAD])
+
+    outs = [((count, HEAD), F32), ((count + 2 * EXTRA if last else count, HEAD), BF16)]
     outs += [((SH, HEAD), F32)] if extra else []
+    outs += [((8, HEAD), F32)] * 2 if last else []
     ins = [VMEM] * (6 + len(extra))
     return call(kernel, outs, ins, [rows_scratch(count)], after=after)(xo, xs, wo, ws, stat, got, *extra)
 
 
-def whole_tiles(refs, sends, own_ref, rows, center, done):
-    ko_ref, ks_ref, so_ref, ss_ref = refs
-    p1_ref, p2_ref, p3_ref = sends
-    count = center.shape[0]
-    for wo_ref, ws_ref, outs, js in ((so_ref, ss_ref, (p1_ref, p3_ref), (1, 3)), (ko_ref, ks_ref, (own_ref, p2_ref), (0, 2))):
-        for n in range(0, 6, 2):
-            pair, sums = partial_tile(rows, wo_ref, ws_ref, slice(n * HD, (n + 2) * HD), center)
-            for h in range(2):
-                half = slice(h * HD, (h + 1) * HD)
-                side, place = divmod(n + h, 3)
-                out_ref = outs[side]
-                out_ref[0:count, place * HD : (place + 1) * HD] = pair[:, half].astype(out_ref.dtype)
-                done(js[side], place, sums[:, half])
-
-
-def last_part(xo, xs, weights, stats, after):
-    def kernel(xo_ref, xs_ref, *refs):
-        ws, (t0_ref, t12_ref) = refs[0:4], refs[4:6]
-        own_ref, p1_ref, p2_ref, p3_ref, note_ref, rows = refs[6:]
-        load_rows(rows, xo_ref, xs_ref)
-        stat = row_stats(xo_ref, xs_ref)
-        turned = [one[k * SH : (k + 1) * SH, :].T for one, k in ((t0_ref, 0), (t12_ref, 0), (t12_ref, 1), (stat, 0))]
-        sums = jnp.concatenate([t[0:1, :] for t in turned] + [t[1:2, :] for t in turned], axis=0)
-        column_sums = {}
-
-        def done(j, place, tile_sums):
-            column_sums[j, place] = tile_sums[0:1, :]
-
-        whole_tiles(ws, (p1_ref, p2_ref, p3_ref), own_ref, rows, stat[:, 0:1] / CHIP, done)
-        for j, ref in enumerate((note_ref, p1_ref, p2_ref, p3_ref)):
-            heads = [column_sums[j, place] for place in range(3)] + [jnp.zeros((5, HD), F32)]
-            note = jnp.concatenate([sums, jnp.concatenate(heads, axis=0)], axis=1)
-            if j == 0:
-                ref[...] = note
-                continue
-            terms = []
-            for _ in range(3):
-                terms.append(note.astype(BF16).astype(F32))
-                note = note - terms[-1]
-            terms.append(jnp.zeros((8, HEAD), F32))
-            ref[SH : SH + EXTRA, :] = jnp.concatenate(terms, axis=0).astype(BF16)
-
-    part = ((SH + EXTRA, HEAD), BF16)
-    outs = [((SH, HEAD), F32), part, part, part, ((8, HEAD), F32)]
-    return call(kernel, outs, [VMEM] * 8, [rows_scratch(SH)], after=after)(xo, xs, *weights, *stats)
-
-
-def last_sum(own, got, note):
-    def kernel(own_ref, g1_ref, g2_ref, g3_ref, note_ref, out_ref, coef_ref, cs_ref):
-        total = own_ref[...]
-        notes = [note_ref[...]]
-        for ref in (g1_ref, g2_ref, g3_ref):
-            total = total + ref[0:SH, :].astype(F32)
-            terms = ref[SH : SH + EXTRA, :].astype(F32)
-            notes.append(terms[0:8, :] + terms[8:16, :] + terms[16:24, :])
-        out_ref[...] = total
+def last_sum(own, got, mine, near):
+    def kernel(own_ref, got_ref, mine_ref, near_ref, out_ref, coef_ref, cs_ref):
+        out_ref[...] = own_ref[...] + got_ref[0:SH, :].astype(F32)
+        notes = [mine_ref[...], near_ref[...]]
+        for at in (SH, SH + EXTRA):
+            notes.append(read_note(got_ref[at : at + EXTRA, :]))
         for k in range(4):
             sums = [n[k : k + 1, 0:SH] for n in notes]
             squares = [n[4 + k : 5 + k, 0:SH] for n in notes]
@@ -274,7 +279,7 @@
         cs_ref[4:8, :] = jnp.zeros((4, HEAD), F32)
 
     outs = [((SH, HEAD), F32), ((R, HD), F32), ((8, HEAD), F32)]
-    return call(kernel, outs, [VMEM] * 5)(own, *got, note)
+    return call(kernel, outs, [VMEM] * 4)(own, got, mine, near)
 
 
 def join(blocks, axis, after=()):
@@ -294,13 +299,13 @@
     return out
 
 
-def attention(places, coef, cs, tot0, own12, ends, tot3):
-    def kernel(places_ref, coef_ref, cs_ref, tot0_ref, own12_ref, end1_ref, end2_ref, tot3_ref, out_ref, qkv):
+def attention(places, coef, cs, tot0, own12, end12, tot3):
+    def kernel(places_ref, coef_ref, cs_ref, tot0_ref, own12_ref, end12_ref, tot3_ref, out_ref, qkv):
         my = lax.axis_index("my")
         for k, offset in enumerate((0, 1, 3, 2)):
             if k in (1, 2):
-                end_ref = end1_ref if k == 1 else end2_ref
-                total = own12_ref[(k - 1) * SH : k * SH, :] + end_ref[...].astype(F32)
+                at = slice((k - 1) * SH, k * SH)
+                total = own12_ref[at, :] + end12_ref[at, :].astype(F32)
             else:
                 total = (tot3_ref if k else tot0_ref)[...]
             coef = coef_ref[k * SH : (k + 1) * SH, :]
@@ -328,8 +333,8 @@
             out_ref[image * IMG_ROWS : (image + 1) * IMG_ROWS, :] = mixture.astype(BF16)
 
     (out,) = call(
-        kernel, [((R, HD), BF16)], [SMEM] + [VMEM] * 7, [pltpu.VMEM((R, HEAD), BF16)], limit=24
-    )(places, coef, cs, tot0, own12, *ends, tot3)
+        kernel, [((R, HD), BF16)], [SMEM] + [VMEM] * 6, [pltpu.VMEM((R, HEAD), BF16)], limit=24
+    )(places, coef, cs, tot0, own12, end12, tot3)
     return out
 
 
@@ -359,31 +364,35 @@
 def lane_rows(blocks):
     def kernel(*refs):
         z = lax.axis_index("mx") >> 1
-        for j, ref in enumerate(refs[:-1]):
+        for j, ref in enumerate(refs[:4]):
             for d in range(4):
                 at = pl.multiple_of((d * 4 + (z ^ j)) * HD, HD)
-                refs[-1][:, pl.ds(at, HD)] = ref[:, d * HD : (d + 1) * HD]
-
-    (out,) = call(kernel, [((SH, 16 * HD), BF16)], [VMEM] * 4)(*blocks)
-    return out
-
-
-def project(lane, sib, weight):
-    def kernel(lane_ref, sib_ref, w_ref, out_ref):
-        my = lax.axis_index("my")
+                refs[4][:, pl.ds(at, HD)] = ref[0:FIRST, d * HD : (d + 1) * HD]
+                refs[5][:, pl.ds(at, HD)] = ref[FIRST:SH, d * HD : (d + 1) * HD]
+
+    return call(kernel, [((FIRST, 16 * HD), BF16), ((SH - FIRST, 16 * HD), BF16)], [VMEM] * 4)(*blocks)
+
+
+def project(lanes, sibs, weights):
+    def kernel(lane0_ref, lane1_ref, sib0_ref, sib1_ref, w0_ref, w1_ref, w2_ref, top_ref, bottom_ref, out_ref, low, high):
         side = lax.axis_index("mx") & 1
+        for at, lane_ref, sib_ref in ((slice(0, FIRST), lane0_ref, sib0_ref), (slice(FIRST, SH), lane1_ref, sib1_ref)):
+            one, two = lane_ref[...], sib_ref[...]
+            low[at, :] = jnp.where(side == 0, one, two)
+            high[at, :] = jnp.where(side == 0, two, one)
         for n in range(3):
             columns = slice(n * 256, (n + 1) * 256)
             total = jnp.zeros((SH, 256), F32)
-            for d, offset in enumerate((0, 1, 3, 2)):
-                base = ((my + offset) & 3) * R
-                for ref, lane_side in ((lane_ref, side), (sib_ref, 1 - side)):
-                    row = pl.multiple_of(base + lane_side * 4 * HD, 4 * HD)
-                    part = ref[:, d * 4 * HD : (d + 1) * 4 * HD]
-                    total = total + jnp.dot(part, w_ref[pl.ds(row, 4 * HD), columns], preferred_element_type=F32)
+            for d, ref in enumerate((w0_ref, w1_ref, w2_ref, None)):
+                heads = slice(d * 4 * HD, (d + 1) * 4 * HD)
+                upper = top_ref[:, columns] if ref is None else ref[0 : 4 * HD, columns]
+                lower = bottom_ref[:, columns] if ref is None else ref[4 * HD : R, columns]
+                total = total + jnp.dot(low[:, heads], upper, preferred_element_type=F32)
+                total = total + jnp.dot(high[:, heads], lower, preferred_element_type=F32)
             out_ref[:, columns] = total.astype(BF16)
 
-    (out,) = call(kernel, [((SH, DL), BF16)], [VMEM] * 3, limit=24)(lane, sib, weight)
+    scratch = [pltpu.VMEM((SH, 16 * HD), BF16)] * 2
+    (out,) = call(kernel, [((SH, DL), BF16)], [VMEM] * 9, scratch, limit=24)(*lanes, *sibs, *weights)
     return out
 
 
@@ -409,36 +418,38 @@
     with scope("chunk12"):
         x12 = join([next_rows, last_rows], 0, (got0,))
         s12 = swap(x12, "mx", 1)
-    with scope("out_weight"):
-        (held,) = gate([out_weight], (x12,))
-        whole_weight = lax.all_gather(held, "my", axis=0, tiled=True)
     with scope("sum0"):
         own0, next0 = keep_part(patches, s0, own_keep, sib_keep, stat0, got0)
         end0 = swap(next0, "mx", 4)
     with scope("chunk12"):
-        part12, stat12, _ = send_part(x12, s12, own_send, sib_send, (next0,))
+        part12, stat12, _ = send_part(x12, s12, own_send, sib_send, after=(next0,))
         got12 = swap(part12, "mx", 2)
     with scope("chunk3"):
         (x3,) = gate([x3], (part12, end0))
         s3 = swap(x3, "mx", 1)
-        own3, p1, p2, p3, note = last_part(x3, s3, weights, (stat0, stat12), (part12, places))
-        got3 = [swap(p1, "mx", 2), swap(p2, "mx", 4), swap(p3, "mx", 6)]
+        part3, stat3, _ = send_part(x3, s3, own_send, sib_send, (stat0, stat12), (part12, places))
+        got3 = swap(part3, "mx", 2)
     with scope("sum12"):
-        own12, next1, next2, tot0 = keep_part(x12, s12, own_keep, sib_keep, stat12, got12, (own0, end0), 2, (own3,))
-        ends = [swap(next1, "mx", 4), swap(next2, "mx", 4)]
+        own12, next12, tot0 = keep_part(x12, s12, own_keep, sib_keep, stat12, got12, (own0, end0), after=(part3,))
+        end12 = swap(next12, "mx", 4)
     with scope("sum3"):
-        tot3, coef, cs = last_sum(own3, got3, note)
+        own3, next3, mine, near = keep_part(x3, s3, own_keep, sib_keep, stat3, got3, last=True, after=(next12,))
+        tot3, coef, cs = last_sum(own3, swap(next3, "mx", 4), mine, near)
+    with scope("out_weight"):
+        held = fetch(out_weight, (x3,))
+        w_next, w_last = shift(held, "my", 1), shift(held, "my", -1)
+        w_far = [shift(w_next[: 4 * HD], "my", 1), shift(w_last[4 * HD :], "my", -1)]
 
     with scope("attention"):
-        attended = attention(places, coef, cs, tot0, own12, ends, tot3)
+        attended = attention(places, coef, cs, tot0, own12, end12, tot3)
         other = swap(attended, "img", 1)
         far, up, down, own = route(places, attended, other)
         near = [own, shift(down, "my", 1), shift(up, "my", -1), shift(far, "my", 2)]
 
     with scope("out"):
         block = join(near, 1)
-        lane = lane_rows([block] + [swap(block, "mx", 2 * j) for j in (1, 2, 3)])
-        return project(lane, swap(lane, "mx", 1), whole_weight)
+        lanes = lane_rows([block] + [swap(block, "mx", 2 * j) for j in (1, 2, 3)])
+        return project(lanes, [swap(lane, "mx", 1) for lane in lanes], [held, w_next, w_last] + w_far)
 
 
 def solution(mesh):

time: 169 us -> 129 us (0.76); the launches traced: 167 us -> 129 us
  between operations: 13.6 us -> 0.16 us
  waiting for transfers between devices: 84 us -> 73.6 us
  local copies, waits for them, and re-layouts: 12.6 us -> 2.46 us
  starting transfers between devices: 39.2 us -> 33.7 us
  Pallas kernels: 17.7 us -> 19.4 us
    ppermute x18 -> x17, waiting for transfers between devices: 73.4 us -> 59.7 us  [swap(): return lax.ppermute(block, axis, [(i, i ^ bits) for i in range(count)])]
    ppermute x18 -> x17, starting transfers between devices: 32.5 us -> 22 us  [swap(): return lax.ppermute(block, axis, [(i, i ^ bits) for i in range(count)])]
    unnamed x35 -> x12, local copies, waits for them, and re-layouts: 12.6 us -> 2.36 us
    ppermute x6 -> x10, starting transfers between devices: 6.69 us -> 11.7 us  [shift(): lax.ppermute(block, axis, [((i + step) % count, i) for i in range(count)])]
    ppermute x6 -> x10, waiting for transfers between devices: 10.6 us -> 13.9 us  [shift(): lax.ppermute(block, axis, [((i + step) % count, i) for i in range(count)])]
    pallas_call x17 -> x18, Pallas kernels: 17.7 us -> 19.4 us  [call(): return lambda *args: made(*args, *after)]
  transfers between devices with their start and end apart: 25 -> 27, of which waited for: 18 -> 17; matrix products, arithmetic and copies ran while one was open for 0% -> 0% of each run, Pallas kernels for 9% -> 12%
where the time goes in v2:
time: 129 us
  waiting for transfers between devices  73.6 us (57%)
  starting transfers between devices  33.7 us (26%)
  Pallas kernels  19.4 us (15%)
  local copies, waits for them, and re-layouts  2.46 us (2%)
    ppermute x17, waiting for transfers between devices, swap(): return lax.ppermute(block, axis, [(i, i ^ bits) for i in range(count)])  59.7 us
    ppermute x17, starting transfers between devices, swap(): return lax.ppermute(block, axis, [(i, i ^ bits) for i in range(count)])  22 us
    pallas_call x18, Pallas kernels, call(): return lambda *args: made(*args, *after)  19.4 us
    ppermute x10, waiting for transfers between devices, shift(): lax.ppermute(block, axis, [((i + step) % count, i) for i in range(count)])  13.9 us
    ppermute x10, starting transfers between devices, shift(): lax.ppermute(block, axis, [((i + step) % count, i) for i in range(count)])  11.7 us
  transfers between devices with their start and end apart: 27, of which 17 were waited for; matrix products, arithmetic and copies ran while one was open for 0% of the time, Pallas kernels for 12%

profile of v2, /device:TPU:1, one launch (start us, length us, event | category | flops | bytes accessed | tf_op | source)
XLA Modules:
  0.0 129.3 jit_solution(16208738536022315302)
XLA Ops:
  0.0 2.3 %copy-done = bf16[768,3,1024]{2,0,1:T(8,128)(2,1)S(1)} copy-done((bf16[768,3,1024]{2,0,1:T(8,128)(2,1)S(1)}, bf16[768,3,1024]{2,0,1:T(8,128)(2,1)}, u32[]{:S(2)}) %copy-start) | copy-done | bytes 4718616
  3.1 3.3 %collective-permute-start.1 = (bf16[768,768]{1,0:T(8,128)(2,1)S(1)}, bf16[768,768]{1,0:T(8,128)(2,1)S(1)}, u32[]{:S(2)}, u32[]{:S(2)}) collective-permute-start(bf16[768,768]{1,0:T(8,128)(2,1)S(1)} %get-tuple-element.35), channel_id=1, source_target_pairs={{0,4},{4,0},{8,12},{12,8},{16,20},{20,16},{24,28},{28,24},{1,5},{5... | collective-permute-start | bytes 3538952 | tf_op jit(solution)/shard_map/weights/ppermute | solution.py:62
  11.1 6.4 %collective-permute-done.3.refs_0_ = bf16[256,768]{1,0:T(8,128)(2,1)S(1)} collective-permute-done((bf16[256,768]{1,0:T(8,128)(2,1)S(1)}, bf16[256,768]{1,0:T(8,128)(2,1)S(1)}, u32[]{:S(2)}, u32[]{:S(2)}) %collective-permute-start.3) | collective-permute-done | bytes 393248 | tf_op jit(solution)/shard_map/rows_near/ppermute | solution.py:67
  17.5 1.6 %collective-permute-done.4.refs_1_ = bf16[256,768]{1,0:T(8,128)(2,1)S(1)} collective-permute-done((bf16[256,768]{1,0:T(8,128)(2,1)S(1)}, bf16[256,768]{1,0:T(8,128)(2,1)S(1)}, u32[]{:S(2)}, u32[]{:S(2)}) %collective-permute-start.4) | collective-permute-done | bytes 393248 | tf_op jit(solution)/shard_map/rows_near/ppermute | solution.py:67
  19.1 1.6 %collective-permute-done.5.refs_2_.refs_5_ = bf16[256,768]{1,0:T(8,128)(2,1)S(1)} collective-permute-done((bf16[256,768]{1,0:T(8,128)(2,1)S(1)}, bf16[256,768]{1,0:T(8,128)(2,1)S(1)}, u32[]{:S(2)}, u32[]{:S(2)}) %collective-permute-start.5) | collective-permute-done | bytes 393248 | tf_op jit(solution)/shard_map/chunk0/ppermute | solution.py:62
  24.3 3.1 %collective-permute-start.8 = (bf16[256,384]{1,0:T(8,128)(2,1)S(1)}, bf16[256,384]{1,0:T(8,128)(2,1)S(1)}, u32[]{:S(2)}, u32[]{:S(2)}) collective-permute-start(bf16[256,384]{1,0:T(8,128)(2,1)S(1)} %get-tuple-element.41.refs_4_), channel_id=1, source_target_pairs={{0,16},{4,20},{8,24},{12,28},{16,0},{20,4},{24,8},{28,12},{1,17},{... | collective-permute-start | bytes 589832 | tf_op jit(solution)/shard_map/sum0/ppermute | solution.py:62
  27.4 2.7 %chunk12.3 = (bf16[512,768]{1,0:T(8,128)(2,1)S(1)}, f32[512,128]{1,0:T(8,128)S(1)}, bf16[512,768]{1,0:T(8,128)(2,1)}) custom-call(bf16[512,768]{1,0:T(8,128)(2,1)S(1)} %chunk12.2.refs_0_, bf16[512,768]{1,0:T(8,128)(2,1)S(1)} %collective-permute-done.6.refs_1_, bf16[768,768]{1,0:T(8,128)(2,1)S(1)} %get-tuple-element.34.refs_2_, ...), custom_call_target="tpu_custom_call" | custom-call | bytes 1024 | tf_op jit(solution)/shard_map/chunk12/pallas_call | solution.py:47
  31.6 2.8 %collective-permute-done.2.refs_0_ = bf16[256,768]{1,0:T(8,128)(2,1)S(1)} collective-permute-done((bf16[256,768]{1,0:T(8,128)(2,1)S(1)}, bf16[256,768]{1,0:T(8,128)(2,1)S(1)}, u32[]{:S(2)}, u32[]{:S(2)}) %collective-permute-start.2) | collective-permute-done | bytes 393248 | tf_op jit(solution)/shard_map/rows_far/ppermute | solution.py:67
  34.4 2.3 %collective-permute-done.8.refs_2_.refs_7_ = bf16[256,384]{1,0:T(8,128)(2,1)S(1)} collective-permute-done((bf16[256,384]{1,0:T(8,128)(2,1)S(1)}, bf16[256,384]{1,0:T(8,128)(2,1)S(1)}, u32[]{:S(2)}, u32[]{:S(2)}) %collective-permute-start.8) | collective-permute-done | bytes 196640 | tf_op jit(solution)/shard_map/sum0/ppermute | solution.py:62
  43.1 1.7 %chunk3.3 = (bf16[288,768]{1,0:T(8,128)(2,1)S(1)}, f32[8,256]{1,0:T(8,128)S(1)}, bf16[256,768]{1,0:T(8,128)(2,1)}) custom-call(bf16[256,768]{1,0:T(8,128)(2,1)S(1)} %chunk3.2.refs_0_.refs_1_, bf16[256,768]{1,0:T(8,128)(2,1)S(1)} %collective-permute-done.9.refs_1_, bf16[768,768]{1,0:T(8,128)(2,1)S(1)} %get-tuple-element.34.refs_2_, ...), custom_call_target="tpu_custom_call" | custom-call | bytes 1024 | tf_op jit(solution)/shard_map/chunk3/pallas_call | solution.py:47
  45.1 6.4 %collective-permute-done.11.refs_5_ = bf16[512,768]{1,0:T(8,128)(2,1)S(1)} collective-permute-done((bf16[512,768]{1,0:T(8,128)(2,1)S(1)}, bf16[512,768]{1,0:T(8,128)(2,1)S(1)}, u32[]{:S(2)}, u32[]{:S(2)}) %collective-permute-start.11) | collective-permute-done | bytes 786464 | tf_op jit(solution)/shard_map/chunk12/ppermute | solution.py:62
  51.6 1.8 %sum12.1 = (f32[512,384]{1,0:T(8,128)S(1)}, bf16[512,384]{1,0:T(8,128)(2,1)S(1)}, f32[256,384]{1,0:T(8,128)S(1)}) custom-call(bf16[512,768]{1,0:T(8,128)(2,1)S(1)} %chunk12.2.refs_0_, bf16[512,768]{1,0:T(8,128)(2,1)S(1)} %collective-permute-done.6.refs_1_, bf16[768,768]{1,0:T(8,128)(2,1)S(1)} %get-tuple-element.38.refs_2_, ...), custom_call_target="tpu_custom_call" | custom-call | bytes 1024 | tf_op jit(solution)/shard_map/sum12/pallas_call | solution.py:47
  54.1 10.3 %collective-permute-done.10.refs_5_ = bf16[288,768]{1,0:T(8,128)(2,1)S(1)} collective-permute-done((bf16[288,768]{1,0:T(8,128)(2,1)S(1)}, bf16[288,768]{1,0:T(8,128)(2,1)S(1)}, u32[]{:S(2)}, u32[]{:S(2)}) %collective-permute-start.10) | collective-permute-done | bytes 442400 | tf_op jit(solution)/shard_map/chunk3/ppermute | solution.py:62
  65.7 15.9 %collective-permute-done.12.refs_1_ = bf16[320,384]{1,0:T(8,128)(2,1)S(1)} collective-permute-done((bf16[320,384]{1,0:T(8,128)(2,1)S(1)}, bf16[320,384]{1,0:T(8,128)(2,1)S(1)}, u32[]{:S(2)}, u32[]{:S(2)}) %collective-permute-start.12) | collective-permute-done | bytes 245792 | tf_op jit(solution)/shard_map/sum3/ppermute | solution.py:62
  81.9 2.9 %attention.2.refs_1_ = bf16[1024,128]{1,0:T(8,128)(2,1)S(1)} custom-call(s32[16]{0:T(128)S(1)} %weights.3.refs_7_.refs_0_, f32[1024,128]{1,0:T(8,128)S(1)} %get-tuple-element.52.refs_1_, f32[8,384]{1,0:T(8,128)S(1)} %get-tuple-element.53.refs_2_, f32[256,384]{1,0:T(8,128)S(1)} %get-tuple-element.54.refs_3_, f32[512,384]{1,0:T(8,128)S(1)} %get-tuple-element.55.refs_4_, ...), custom_call_target="tpu_custom_call" | custom-call | bytes 1024 | tf_op jit(solution)/shard_map/attention/pallas_call | solution.py:47
  86.2 3.9 %collective-permute-done.14.refs_2_ = bf16[1024,128]{1,0:T(8,128)(2,1)S(1)} collective-permute-done((bf16[1024,128]{1,0:T(8,128)(2,1)S(1)}, bf16[1024,128]{1,0:T(8,128)(2,1)S(1)}, u32[]{:S(2)}, u32[]{:S(2)}) %collective-permute-start.14) | collective-permute-done | bytes 262176 | tf_op jit(solution)/shard_map/attention/ppermute | solution.py:62
  92.4 1.6 %collective-permute-start.17 = (bf16[256,128]{1,0:T(8,128)(2,1)S(1)}, bf16[256,128]{1,0:T(8,128)(2,1)S(1)}, u32[]{:S(2)}, u32[]{:S(2)}) collective-permute-start(bf16[256,128]{1,0:T(8,128)(2,1)S(1)} %get-tuple-element.60), channel_id=1, source_target_pairs={{2,0},{3,1},{0,2},{1,3},{6,4},{7,5},{4,6},{5,7},{10,8},{11,9},{8,1... | collective-permute-start | bytes 196616 | tf_op jit(solution)/shard_map/attention/ppermute | solution.py:67
  94.2 1.9 %collective-permute-done.16.refs_2_ = bf16[256,128]{1,0:T(8,128)(2,1)S(1)} collective-permute-done((bf16[256,128]{1,0:T(8,128)(2,1)S(1)}, bf16[256,128]{1,0:T(8,128)(2,1)S(1)}, u32[]{:S(2)}, u32[]{:S(2)}) %collective-permute-start.16) | collective-permute-done | bytes 65568 | tf_op jit(solution)/shard_map/attention/ppermute | solution.py:67
  97.0 4.5 %collective-permute-start.20 = (bf16[256,512]{1,0:T(8,128)(2,1)S(1)}, bf16[256,512]{1,0:T(8,128)(2,1)S(1)}, u32[]{:S(2)}, u32[]{:S(2)}) collective-permute-start(bf16[256,512]{1,0:T(8,128)(2,1)S(1)} %out.3.refs_0_), channel_id=1, source_target_pairs={{0,24},{4,28},{8,16},{12,20},{16,8},{20,12},{24,0},{28,4},{1,25},{... | collective-permute-start | bytes 786440 | tf_op jit(solution)/shard_map/out/ppermute | solution.py:62
  102.9 2.3 %collective-permute-start.25 = (bf16[512,768]{1,0:T(8,128)(2,1)S(1)}, bf16[512,768]{1,0:T(8,128)(2,1)S(1)}, u32[]{:S(2)}, u32[]{:S(2)}) collective-permute-start(bf16[512,768]{1,0:T(8,128)(2,1)S(1)} %slice.8), channel_id=1, source_target_pairs={{1,0},{2,1},{3,2},{0,3},{5,4},{6,5},{7,6},{4,7},{9,8},{10,9},{11,1... | collective-permute-start | bytes 2359304 | tf_op jit(solution)/shard_map/out_weight/ppermute | solution.py:67
  105.5 16.3 %collective-permute-done.19.refs_2_ = bf16[256,512]{1,0:T(8,128)(2,1)S(1)} collective-permute-done((bf16[256,512]{1,0:T(8,128)(2,1)S(1)}, bf16[256,512]{1,0:T(8,128)(2,1)S(1)}, u32[]{:S(2)}, u32[]{:S(2)}) %collective-permute-start.19) | collective-permute-done | bytes 262176 | tf_op jit(solution)/shard_map/out/ppermute | solution.py:62
  122.1 2.3 %collective-permute-start.21 = (bf16[160,2048]{1,0:T(8,128)(2,1)S(1)}, bf16[160,2048]{1,0:T(8,128)(2,1)S(1)}, u32[]{:S(2)}, u32[]{:S(2)}) collective-permute-start(bf16[160,2048]{1,0:T(8,128)(2,1)S(1)} %get-tuple-element.61.refs_0_), channel_id=1, source_target_pairs={{0,4},{4,0},{8,12},{12,8},{16,20},{20,16},{24,28},{28,24},{1,5},{5... | collective-permute-start | bytes 1966088 | tf_op jit(solution)/shard_map/out/ppermute | solution.py:62
  124.5 2.2 %collective-permute-done.22.refs_3_ = bf16[96,2048]{1,0:T(8,128)(2,1)S(1)} collective-permute-done((bf16[96,2048]{1,0:T(8,128)(2,1)S(1)}, bf16[96,2048]{1,0:T(8,128)(2,1)S(1)}, u32[]{:S(2)}, u32[]{:S(2)}) %collective-permute-start.22) | collective-permute-done | bytes 393248 | tf_op jit(solution)/shard_map/out/ppermute | solution.py:62
  126.7 2.6 %out.5 = bf16[256,768]{1,0:T(8,128)(2,1)} custom-call(bf16[160,2048]{1,0:T(8,128)(2,1)S(1)} %get-tuple-element.61.refs_0_, bf16[96,2048]{1,0:T(8,128)(2,1)S(1)} %get-tuple-element.62.refs_1_, bf16[160,2048]{1,0:T(8,128)(2,1)S(1)} %collective-permute-done.21.refs_2_, bf16[96,2048]{1,0:T(8,128)(2,1)S(1)} %collective-permute-done.22.refs_3_, ...), custom_call_target="tpu_custom_call" | custom-call | bytes 1024 | tf_op jit(solution)/shard_map/out/pallas_call | solution.py:47
  (62 shorter events, 26.3 us)
Async XLA Ops:
  3.1 6.4 %collective-permute-start.1 = (bf16[768,768]{1,0:T(8,128)(2,1)S(1)}, bf16[768,768]{1,0:T(8,128)(2,1)S(1)}, u32[]{:S(2)}, u32[]{:S(2)}) collective-permute-start(bf16[768,768]{1,0:T(8,128)(2,1)S(1)} %get-tuple-element.35), channel_id=1, source_target_pairs={{0,4},{4,0},{8,12},{12,8},{16,20},{20,16},{24,28},{28,24},{1,5},{5... | collective-permute-start | bytes 3538952 | tf_op jit(solution)/shard_map/weights/ppermute | solution.py:62
  6.6 16.8 %collective-permute-start.7 = (bf16[768,768]{1,0:T(8,128)(2,1)S(1)}, bf16[768,768]{1,0:T(8,128)(2,1)S(1)}, u32[]{:S(2)}, u32[]{:S(2)}) collective-permute-start(bf16[768,768]{1,0:T(8,128)(2,1)S(1)} %get-tuple-element.39), channel_id=1, source_target_pairs={{0,4},{4,0},{8,12},{12,8},{16,20},{20,16},{24,28},{28,24},{1,5},{5... | collective-permute-start | bytes 3538952 | tf_op jit(solution)/shard_map/weights/ppermute | solution.py:62
  6.9 10.6 %collective-permute-start.3 = (bf16[256,768]{1,0:T(8,128)(2,1)S(1)}, bf16[256,768]{1,0:T(8,128)(2,1)S(1)}, u32[]{:S(2)}, u32[]{:S(2)}) collective-permute-start(bf16[256,768]{1,0:T(8,128)(2,1)S(1)} %copy-done.2), channel_id=1, source_target_pairs={{1,0},{2,1},{3,2},{0,3},{5,4},{6,5},{7,6},{4,7},{9,8},{10,9},{11,1... | collective-permute-start | bytes 1179656 | tf_op jit(solution)/shard_map/rows_near/ppermute | solution.py:67
  7.7 11.5 %collective-permute-start.4 = (bf16[256,768]{1,0:T(8,128)(2,1)S(1)}, bf16[256,768]{1,0:T(8,128)(2,1)S(1)}, u32[]{:S(2)}, u32[]{:S(2)}) collective-permute-start(bf16[256,768]{1,0:T(8,128)(2,1)S(1)} %copy-done.2), channel_id=1, source_target_pairs={{3,0},{0,1},{1,2},{2,3},{7,4},{4,5},{5,6},{6,7},{11,8},{8,9},{9,10... | collective-permute-start | bytes 1179656 | tf_op jit(solution)/shard_map/rows_near/ppermute | solution.py:67
  10.4 10.3 %collective-permute-start.5 = (bf16[256,768]{1,0:T(8,128)(2,1)S(1)}, bf16[256,768]{1,0:T(8,128)(2,1)S(1)}, u32[]{:S(2)}, u32[]{:S(2)}) collective-permute-start(bf16[256,768]{1,0:T(8,128)(2,1)S(1)} %get-tuple-element.37), channel_id=1, source_target_pairs={{0,8},{4,12},{8,0},{12,4},{16,24},{20,28},{24,16},{28,20},{1,9},{5... | collective-permute-start | bytes 1179656 | tf_op jit(solution)/shard_map/chunk0/ppermute | solution.py:62
  20.8 6.6 %collective-permute-start.6 = (bf16[512,768]{1,0:T(8,128)(2,1)S(1)}, bf16[512,768]{1,0:T(8,128)(2,1)S(1)}, u32[]{:S(2)}, u32[]{:S(2)}) collective-permute-start(bf16[512,768]{1,0:T(8,128)(2,1)S(1)} %chunk12.2.refs_0_), channel_id=1, source_target_pairs={{0,4},{4,0},{8,12},{12,8},{16,20},{20,16},{24,28},{28,24},{1,5},{5... | collective-permute-start | bytes 2359304 | tf_op jit(solution)/shard_map/chunk12/ppermute | solution.py:62
  22.2 12.2 %collective-permute-start.2 = (bf16[256,768]{1,0:T(8,128)(2,1)S(1)}, bf16[256,768]{1,0:T(8,128)(2,1)S(1)}, u32[]{:S(2)}, u32[]{:S(2)}) collective-permute-start(bf16[256,768]{1,0:T(8,128)(2,1)S(1)} %get-tuple-element.36), channel_id=1, source_target_pairs={{2,0},{3,1},{0,2},{1,3},{6,4},{7,5},{4,6},{5,7},{10,8},{11,9},{8,1... | collective-permute-start | bytes 1179656 | tf_op jit(solution)/shard_map/rows_far/ppermute | solution.py:67
  24.3 12.3 %collective-permute-start.8 = (bf16[256,384]{1,0:T(8,128)(2,1)S(1)}, bf16[256,384]{1,0:T(8,128)(2,1)S(1)}, u32[]{:S(2)}, u32[]{:S(2)}) collective-permute-start(bf16[256,384]{1,0:T(8,128)(2,1)S(1)} %get-tuple-element.41.refs_4_), channel_id=1, source_target_pairs={{0,16},{4,20},{8,24},{12,28},{16,0},{20,4},{24,8},{28,12},{1,17},{... | collective-permute-start | bytes 589832 | tf_op jit(solution)/shard_map/sum0/ppermute | solution.py:62
  30.1 21.5 %collective-permute-start.11 = (bf16[512,768]{1,0:T(8,128)(2,1)S(1)}, bf16[512,768]{1,0:T(8,128)(2,1)S(1)}, u32[]{:S(2)}, u32[]{:S(2)}) collective-permute-start(bf16[512,768]{1,0:T(8,128)(2,1)S(1)} %get-tuple-element.42.refs_1_.refs_6_), channel_id=1, source_target_pairs={{0,8},{4,12},{8,0},{12,4},{16,24},{20,28},{24,16},{28,20},{1,9},{5... | collective-permute-start | bytes 2359304 | tf_op jit(solution)/shard_map/chunk12/ppermute | solution.py:62
  37.5 64.5 %collective-permute-start.24 = (bf16[1024,768]{1,0:T(8,128)(2,1)S(1)}, bf16[1024,768]{1,0:T(8,128)(2,1)S(1)}, u32[]{:S(2)}, u32[]{:S(2)}) collective-permute-start(bf16[1024,768]{1,0:T(8,128)(2,1)S(1)} %out_weight.1.refs_4_), channel_id=1, source_target_pairs={{3,0},{0,1},{1,2},{2,3},{7,4},{4,5},{5,6},{6,7},{11,8},{8,9},{9,10... | collective-permute-start | bytes 4718600 | tf_op jit(solution)/shard_map/out_weight/ppermute | solution.py:67
  38.8 64.1 %collective-permute-start.23 = (bf16[1024,768]{1,0:T(8,128)(2,1)S(1)}, bf16[1024,768]{1,0:T(8,128)(2,1)S(1)}, u32[]{:S(2)}, u32[]{:S(2)}) collective-permute-start(bf16[1024,768]{1,0:T(8,128)(2,1)S(1)} %out_weight.1.refs_4_), channel_id=1, source_target_pairs={{1,0},{2,1},{3,2},{0,3},{5,4},{6,5},{7,6},{4,7},{9,8},{10,9},{11,1... | collective-permute-start | bytes 4718600 | tf_op jit(solution)/shard_map/out_weight/ppermute | solution.py:67
  44.8 19.7 %collective-permute-start.10 = (bf16[288,768]{1,0:T(8,128)(2,1)S(1)}, bf16[288,768]{1,0:T(8,128)(2,1)S(1)}, u32[]{:S(2)}, u32[]{:S(2)}) collective-permute-start(bf16[288,768]{1,0:T(8,128)(2,1)S(1)} %get-tuple-element.45.refs_8_), channel_id=1, source_target_pairs={{0,8},{4,12},{8,0},{12,4},{16,24},{20,28},{24,16},{28,20},{1,9},{5... | collective-permute-start | bytes 1327112 | tf_op jit(solution)/shard_map/chunk3/ppermute | solution.py:62
  53.4 28.5 %collective-permute-start.13 = (bf16[512,384]{1,0:T(8,128)(2,1)S(1)}, bf16[512,384]{1,0:T(8,128)(2,1)S(1)}, u32[]{:S(2)}, u32[]{:S(2)}) collective-permute-start(bf16[512,384]{1,0:T(8,128)(2,1)S(1)} %get-tuple-element.47.refs_6_), channel_id=1, source_target_pairs={{0,16},{4,20},{8,24},{12,28},{16,0},{20,4},{24,8},{28,12},{1,17},{... | collective-permute-start | bytes 1179656 | tf_op jit(solution)/shard_map/sum12/ppermute | solution.py:62
  65.5 16.1 %collective-permute-start.12 = (bf16[320,384]{1,0:T(8,128)(2,1)S(1)}, bf16[320,384]{1,0:T(8,128)(2,1)S(1)}, u32[]{:S(2)}, u32[]{:S(2)}) collective-permute-start(bf16[320,384]{1,0:T(8,128)(2,1)S(1)} %get-tuple-element.49), channel_id=1, source_target_pairs={{0,16},{4,20},{8,24},{12,28},{16,0},{20,4},{24,8},{28,12},{1,17},{... | collective-permute-start | bytes 737288 | tf_op jit(solution)/shard_map/sum3/ppermute | solution.py:62
  84.8 5.3 %collective-permute-start.14 = (bf16[1024,128]{1,0:T(8,128)(2,1)S(1)}, bf16[1024,128]{1,0:T(8,128)(2,1)S(1)}, u32[]{:S(2)}, u32[]{:S(2)}) collective-permute-start(bf16[1024,128]{1,0:T(8,128)(2,1)S(1)} %attention.2.refs_1_), channel_id=1, source_target_pairs={{0,32},{32,0},{64,96},{96,64},{128,160},{160,128},{192,224},{224,1... | collective-permute-start | bytes 786440 | tf_op jit(solution)/shard_map/attention/ppermute | solution.py:62
  90.8 3.4 %collective-permute-start.15 = (bf16[256,128]{1,0:T(8,128)(2,1)S(1)}, bf16[256,128]{1,0:T(8,128)(2,1)S(1)}, u32[]{:S(2)}, u32[]{:S(2)}) collective-permute-start(bf16[256,128]{1,0:T(8,128)(2,1)S(1)} %get-tuple-element.58), channel_id=1, source_target_pairs={{1,0},{2,1},{3,2},{0,3},{5,4},{6,5},{7,6},{4,7},{9,8},{10,9},{11,1... | collective-permute-start | bytes 196616 | tf_op jit(solution)/shard_map/attention/ppermute | solution.py:67
  91.7 4.3 %collective-permute-start.16 = (bf16[256,128]{1,0:T(8,128)(2,1)S(1)}, bf16[256,128]{1,0:T(8,128)(2,1)S(1)}, u32[]{:S(2)}, u32[]{:S(2)}) collective-permute-start(bf16[256,128]{1,0:T(8,128)(2,1)S(1)} %get-tuple-element.59), channel_id=1, source_target_pairs={{3,0},{0,1},{1,2},{2,3},{7,4},{4,5},{5,6},{6,7},{11,8},{8,9},{9,10... | collective-permute-start | bytes 196616 | tf_op jit(solution)/shard_map/attention/ppermute | solution.py:67
  92.4 4.6 %collective-permute-start.17 = (bf16[256,128]{1,0:T(8,128)(2,1)S(1)}, bf16[256,128]{1,0:T(8,128)(2,1)S(1)}, u32[]{:S(2)}, u32[]{:S(2)}) collective-permute-start(bf16[256,128]{1,0:T(8,128)(2,1)S(1)} %get-tuple-element.60), channel_id=1, source_target_pairs={{2,0},{3,1},{0,2},{1,3},{6,4},{7,5},{4,6},{5,7},{10,8},{11,9},{8,1... | collective-permute-start | bytes 196616 | tf_op jit(solution)/shard_map/attention/ppermute | solution.py:67
  97.0 8.5 %collective-permute-start.20 = (bf16[256,512]{1,0:T(8,128)(2,1)S(1)}, bf16[256,512]{1,0:T(8,128)(2,1)S(1)}, u32[]{:S(2)}, u32[]{:S(2)}) collective-permute-start(bf16[256,512]{1,0:T(8,128)(2,1)S(1)} %out.3.refs_0_), channel_id=1, source_target_pairs={{0,24},{4,28},{8,16},{12,20},{16,8},{20,12},{24,0},{28,4},{1,25},{... | collective-permute-start | bytes 786440 | tf_op jit(solution)/shard_map/out/ppermute | solution.py:62
  101.6 20.3 %collective-permute-start.19 = (bf16[256,512]{1,0:T(8,128)(2,1)S(1)}, bf16[256,512]{1,0:T(8,128)(2,1)S(1)}, u32[]{:S(2)}, u32[]{:S(2)}) collective-permute-start(bf16[256,512]{1,0:T(8,128)(2,1)S(1)} %out.3.refs_0_), channel_id=1, source_target_pairs={{0,16},{4,20},{8,24},{12,28},{16,0},{20,4},{24,8},{28,12},{1,17},{... | collective-permute-start | bytes 786440 | tf_op jit(solution)/shard_map/out/ppermute | solution.py:62
  101.6 20.3 %collective-permute-start.18 = (bf16[256,512]{1,0:T(8,128)(2,1)S(1)}, bf16[256,512]{1,0:T(8,128)(2,1)S(1)}, u32[]{:S(2)}, u32[]{:S(2)}) collective-permute-start(bf16[256,512]{1,0:T(8,128)(2,1)S(1)} %out.3.refs_0_), channel_id=1, source_target_pairs={{0,8},{4,12},{8,0},{12,4},{16,24},{20,28},{24,16},{28,20},{1,9},{5... | collective-permute-start | bytes 786440 | tf_op jit(solution)/shard_map/out/ppermute | solution.py:62
  102.0 24.7 %collective-permute-start.26 = (bf16[512,768]{1,0:T(8,128)(2,1)S(1)}, bf16[512,768]{1,0:T(8,128)(2,1)S(1)}, u32[]{:S(2)}, u32[]{:S(2)}) collective-permute-start(bf16[512,768]{1,0:T(8,128)(2,1)S(1)} %slice.9), channel_id=1, source_target_pairs={{3,0},{0,1},{1,2},{2,3},{7,4},{4,5},{5,6},{6,7},{11,8},{8,9},{9,10... | collective-permute-start | bytes 2359304 | tf_op jit(solution)/shard_map/out_weight/ppermute | solution.py:67
  102.9 23.8 %collective-permute-start.25 = (bf16[512,768]{1,0:T(8,128)(2,1)S(1)}, bf16[512,768]{1,0:T(8,128)(2,1)S(1)}, u32[]{:S(2)}, u32[]{:S(2)}) collective-permute-start(bf16[512,768]{1,0:T(8,128)(2,1)S(1)} %slice.8), channel_id=1, source_target_pairs={{1,0},{2,1},{3,2},{0,3},{5,4},{6,5},{7,6},{4,7},{9,8},{10,9},{11,1... | collective-permute-start | bytes 2359304 | tf_op jit(solution)/shard_map/out_weight/ppermute | solution.py:67
  122.1 4.6 %collective-permute-start.21 = (bf16[160,2048]{1,0:T(8,128)(2,1)S(1)}, bf16[160,2048]{1,0:T(8,128)(2,1)S(1)}, u32[]{:S(2)}, u32[]{:S(2)}) collective-permute-start(bf16[160,2048]{1,0:T(8,128)(2,1)S(1)} %get-tuple-element.61.refs_0_), channel_id=1, source_target_pairs={{0,4},{4,0},{8,12},{12,8},{16,20},{20,16},{24,28},{28,24},{1,5},{5... | collective-permute-start | bytes 1966088 | tf_op jit(solution)/shard_map/out/ppermute | solution.py:62
  (9 other events, 36.3 us)

commit v3 on v2

--- a/solution.py
+++ b/solution.py
@@ -93,21 +93,6 @@
     return call(kernel, [shape, shape], [HBM], [pltpu.SemaphoreType.DMA((12,))])(w3)
 
 
-def fetch(block, after):
-    rows = block.shape[0] // 4
-
-    def kernel(block_ref, out_ref, sems):
-        parts = [pl.ds(i * rows, rows) for i in range(4)]
-        copies = [pltpu.make_async_copy(block_ref.at[p, :], out_ref.at[p, :], sems.at[i]) for i, p in enumerate(parts)]
-        for copy in copies:
-            copy.start()
-        for copy in copies:
-            copy.wait()
-
-    (out,) = call(kernel, [(block.shape, BF16)], [HBM], [pltpu.SemaphoreType.DMA((4,))], after=after)(block)
-    return out
-
-
 def table(counts, owner, target):
     def kernel(counts_ref, owner_ref, target_ref, out_ref, source):
         group = lax.axis_index("img")
@@ -147,19 +132,25 @@
     return out
 
 
-def load_rows(rows, xo_ref, xs_ref):
-    count = xo_ref.shape[0]
-    rows[0:count, 0:DL] = xo_ref[...]
-    rows[0:count, DL:CHIP] = xs_ref[...]
-    rows[count : count + 16, :] = jnp.ones((16, CHIP), BF16)
-
-
-def row_stats(xo_ref, xs_ref):
-    fo, fs = xo_ref[...].astype(F32), xs_ref[...].astype(F32)
-    s1 = jnp.sum(fo, axis=1, keepdims=True) + jnp.sum(fs, axis=1, keepdims=True)
-    s2 = jnp.sum(fo * fo, axis=1, keepdims=True) + jnp.sum(fs * fs, axis=1, keepdims=True)
-    lane = lax.broadcasted_iota(jnp.int32, (xo_ref.shape[0], HD), 1)
-    return jnp.where(lane == 0, s1, jnp.where(lane == 1, s2, F32(0.0)))
+def load_rows(rows, xo_refs, xs_refs):
+    at = 0
+    for xo_ref, xs_ref in zip(xo_refs, xs_refs):
+        size = xo_ref.shape[0]
+        rows[at : at + size, 0:DL] = xo_ref[...]
+        rows[at : at + size, DL:CHIP] = xs_ref[...]
+        at += size
+    rows[at : at + 16, :] = jnp.ones((16, CHIP), BF16)
+
+
+def row_stats(xo_refs, xs_refs):
+    stats = []
+    for xo_ref, xs_ref in zip(xo_refs, xs_refs):
+        fo, fs = xo_ref[...].astype(F32), xs_ref[...].astype(F32)
+        s1 = jnp.sum(fo, axis=1, keepdims=True) + jnp.sum(fs, axis=1, keepdims=True)
+        s2 = jnp.sum(fo * fo, axis=1, keepdims=True) + jnp.sum(fs * fs, axis=1, keepdims=True)
+        lane = lax.broadcasted_iota(jnp.int32, (xo_ref.shape[0], HD), 1)
+        stats.append(jnp.where(lane == 0, s1, jnp.where(lane == 1, s2, F32(0.0))))
+    return stats[0] if len(stats) == 1 else jnp.concatenate(stats, axis=0)
 
 
 def partial_tile(rows, wo_ref, ws_ref, columns, center):
@@ -197,9 +188,9 @@
 
     def kernel(xo_ref, xs_ref, wo_ref, ws_ref, *refs):
         others, (out_ref, stat_ref, copy_ref, rows) = refs[: len(earlier)], refs[len(earlier) :]
-        load_rows(rows, xo_ref, xs_ref)
+        load_rows(rows, [xo_ref], [xs_ref])
         copy_ref[...] = xo_ref[...]
-        stat = row_stats(xo_ref, xs_ref)
+        stat = row_stats([xo_ref], [xs_ref])
         center = stat[:, 0:1] / CHIP
         column_sums = []
         for n in range(3):
@@ -222,42 +213,95 @@
     return call(kernel, outs, ins, [rows_scratch(count)], after=after)(xo, xs, wo, ws, *earlier)
 
 
-def keep_part(xo, xs, wo, ws, stat, got, more=None, last=False, after=()):
-    count = xo.shape[0]
+def own_product(blocks, weight, after):
+    size = blocks[0].shape[0]
+    count = len(blocks) * size
+
+    def kernel(*refs):
+        w_ref, out_ref, rows = refs[len(blocks) :]
+        for i in range(len(blocks)):
+            rows[i * size : (i + 1) * size, :] = refs[i][...]
+        rows[count : count + 16, :] = jnp.ones((16, DL), BF16)
+        for n in range(3):
+            columns = slice(n * 256, (n + 1) * 256)
+            out_ref[:, columns] = jnp.dot(rows[...], w_ref[:, columns], preferred_element_type=F32)
+
+    outs = [((count + 16, 2 * HEAD), F32)]
+    scratch = [pltpu.VMEM((count + 16, DL), BF16)]
+    (out,) = call(kernel, outs, [VMEM] * (1 + len(blocks)), scratch, after=after)(*blocks, weight)
+    return out
+
+
+def rest_part(xo, xs, weight, product, after):
+    size, blocks = xo[0].shape[0], len(xo)
+    count = blocks * size
+
+    def kernel(*refs):
+        xo_refs, xs_refs = refs[:blocks], refs[blocks : 2 * blocks]
+        w_ref, product_ref, out_ref, stat_ref, rows = refs[2 * blocks :]
+        for i, ref in enumerate(xs_refs):
+            rows[i * size : (i + 1) * size, :] = ref[...]
+        rows[count : count + 16, :] = jnp.ones((16, DL), BF16)
+        stat = row_stats(xo_refs, xs_refs)
+        stat_ref[...] = stat
+        center = stat[:, 0:1] / CHIP
+        for n in range(3):
+            columns = slice(n * 256, (n + 1) * 256)
+            acc = product_ref[:, columns] + jnp.dot(rows[...], w_ref[:, columns], preferred_element_type=F32)
+            out_ref[:, columns] = (acc[0:count, :] - center * acc[count : count + 1, :]).astype(BF16)
+
+    outs = [((count, 2 * HEAD), BF16), ((count, HD), F32)]
+    scratch = [pltpu.VMEM((count + 16, DL), BF16)]
+    return call(kernel, outs, [VMEM] * (2 * blocks + 2), scratch, after=after)(*xo, *xs, weight, product)
+
+
+def kept_part(xo, xs, wo, ws, stat, last=False, after=()):
+    blocks = len(xo)
+    count = sum(block.shape[0] for block in xo)
+
+    def kernel(*refs):
+        xo_refs, xs_refs = refs[:blocks], refs[blocks : 2 * blocks]
+        wo_ref, ws_ref, stat_ref, kept_ref = refs[2 * blocks : 2 * blocks + 4]
+        refs, rows = refs[2 * blocks + 4 : -1], refs[-1]
+        load_rows(rows, xo_refs, xs_refs)
+        stat = row_stats(xo_refs, xs_refs) if last else stat_ref[...]
+        center = stat[:, 0:1] / CHIP
+        column_sums = []
+        for n in range(3):
+            columns = slice(n * 256, (n + 1) * 256)
+            tile, sums = partial_tile(rows, wo_ref, ws_ref, columns, center)
+            kept_ref[:, columns] = tile
+            column_sums += [sums[0:1, 0:HD], sums[0:1, HD:256]]
+        if last:
+            refs[0][...] = head_note(stat_ref[...], column_sums[0:3])
+            refs[1][...] = note_terms(head_note(stat_ref[...], column_sums[3:6]))
+
+    outs = [((count, 2 * HEAD), F32)] + ([((8, HEAD), F32), ((EXTRA, HEAD), BF16)] if last else [])
+    return call(kernel, outs, [VMEM] * (2 * blocks + 3), [rows_scratch(count)], after=after)(*xo, *xs, wo, ws, stat)
+
+
+def add_part(kept, got, more=None, note=None, after=()):
+    count = kept.shape[0]
     extra = list(more or ())
-
-    def kernel(xo_ref, xs_ref, wo_ref, ws_ref, stat_ref, got_ref, *refs):
-        refs, rows = refs[:-1], refs[-1]
-        own_ref, send_ref = refs[len(extra)], refs[len(extra) + 1]
-        load_rows(rows, xo_ref, xs_ref)
-        stat = row_stats(xo_ref, xs_ref) if last else stat_ref[...]
-        center = stat[:, 0:1] / CHIP
-        column_sums = {}
-        for n in reversed(range(6)):
-            columns = slice(n * HD, (n + 1) * HD)
-            if n % 2 == 1:
-                pair, sums = partial_tile(rows, wo_ref, ws_ref, slice((n - 1) * HD, (n + 1) * HD), center)
-            half = slice((n % 2) * HD, (n % 2 + 1) * HD)
-            tile = pair[:, half] + got_ref[0:count, columns].astype(F32)
-            column_sums[n] = sums[0:1, half]
-            if n < 3:
-                own_ref[:, columns] = tile
-            else:
-                send_ref[0:count, (n - 3) * HD : (n - 2) * HD] = tile.astype(BF16)
+    last = note is not None
+    ins = [kept, got] + extra + ([note] if last else [])
+
+    def kernel(kept_ref, got_ref, *refs):
+        own_ref, send_ref = refs[len(ins) - 2], refs[len(ins) - 1]
+        own_ref[...] = kept_ref[:, 0:HEAD] + got_ref[0:count, 0:HEAD].astype(F32)
+        send_ref[0:count, :] = (kept_ref[:, HEAD:] + got_ref[0:count, HEAD:].astype(F32)).astype(BF16)
         if extra:
-            refs[-1][...] = refs[0][...] + refs[1][...].astype(F32)
+            refs[len(ins)][...] = refs[0][...] + refs[1][...].astype(F32)
         if last:
             under = slice(count, count + EXTRA)
-            send_ref[under, :] = note_terms(head_note(stat_ref[...], [column_sums[n] for n in (3, 4, 5)]))
-            send_ref[count + EXTRA : count + 2 * EXTRA, :] = got_ref[under, HEAD : 2 * HEAD]
-            refs[-2][...] = head_note(stat_ref[...], [column_sums[n] for n in (0, 1, 2)])
+            send_ref[under, :] = refs[len(ins) - 3][...]
+            send_ref[count + EXTRA : count + 2 * EXTRA, :] = got_ref[under, HEAD:]
             refs[-1][...] = read_note(got_ref[under, 0:HEAD])
 
     outs = [((count, HEAD), F32), ((count + 2 * EXTRA if last else count, HEAD), BF16)]
     outs += [((SH, HEAD), F32)] if extra else []
-    outs += [((8, HEAD), F32)] * 2 if last else []
-    ins = [VMEM] * (6 + len(extra))
-    return call(kernel, outs, ins, [rows_scratch(count)], after=after)(xo, xs, wo, ws, stat, got, *extra)
+    outs += [((8, HEAD), F32)] if last else []
+    return call(kernel, outs, [VMEM] * len(ins), after=after)(*ins)
 
 
 def last_sum(own, got, mine, near):
@@ -325,11 +369,11 @@
             value = jnp.where(rows < live, value, jnp.zeros_like(value))
             scores = lax.dot_general(q, key, (((1,), (1,)), ((), ())), preferred_element_type=F32)
             columns = lax.broadcasted_iota(jnp.int32, (IMG_ROWS, IMG_ROWS), 1)
-            scores = jnp.where(columns < live, scores * HD ** (-0.5), F32(-1e30))
+            scores = jnp.where(columns < live, scores, F32(-1e30))
             top = jnp.max(scores, axis=1, keepdims=True)
-            powers = jnp.exp(scores - top)
-            weights = (powers / jnp.sum(powers, axis=1, keepdims=True)).astype(BF16)
-            mixture = jnp.dot(weights, value, preferred_element_type=F32)
+            powers = jnp.exp((scores - top) * HD ** (-0.5))
+            mixture = jnp.dot(powers.astype(BF16), value, preferred_element_type=F32)
+            mixture = mixture / jnp.sum(powers, axis=1, keepdims=True)
             out_ref[image * IMG_ROWS : (image + 1) * IMG_ROWS, :] = mixture.astype(BF16)
 
     (out,) = call(
@@ -373,26 +417,47 @@
     return call(kernel, [((FIRST, 16 * HD), BF16), ((SH - FIRST, 16 * HD), BF16)], [VMEM] * 4)(*blocks)
 
 
-def project(lanes, sibs, weights):
-    def kernel(lane0_ref, lane1_ref, sib0_ref, sib1_ref, w0_ref, w1_ref, w2_ref, top_ref, bottom_ref, out_ref, low, high):
+def project_lane(lanes, weights):
+    def kernel(lane0_ref, lane1_ref, w0_ref, w1_ref, w2_ref, out_ref, rows):
         side = lax.axis_index("mx") & 1
-        for at, lane_ref, sib_ref in ((slice(0, FIRST), lane0_ref, sib0_ref), (slice(FIRST, SH), lane1_ref, sib1_ref)):
-            one, two = lane_ref[...], sib_ref[...]
-            low[at, :] = jnp.where(side == 0, one, two)
-            high[at, :] = jnp.where(side == 0, two, one)
+        rows[0:FIRST, :] = lane0_ref[:, 0 : 12 * HD]
+        rows[FIRST:SH, :] = lane1_ref[:, 0 : 12 * HD]
+        at = pl.ds(pl.multiple_of(side * 4 * HD, 4 * HD), 4 * HD)
         for n in range(3):
             columns = slice(n * 256, (n + 1) * 256)
             total = jnp.zeros((SH, 256), F32)
-            for d, ref in enumerate((w0_ref, w1_ref, w2_ref, None)):
+            for d, ref in enumerate((w0_ref, w1_ref, w2_ref)):
                 heads = slice(d * 4 * HD, (d + 1) * 4 * HD)
-                upper = top_ref[:, columns] if ref is None else ref[0 : 4 * HD, columns]
-                lower = bottom_ref[:, columns] if ref is None else ref[4 * HD : R, columns]
-                total = total + jnp.dot(low[:, heads], upper, preferred_element_type=F32)
-                total = total + jnp.dot(high[:, heads], lower, preferred_element_type=F32)
+                total = total + jnp.dot(rows[:, heads], ref[at, columns], preferred_element_type=F32)
+            out_ref[:, columns] = total
+
+    scratch = [pltpu.VMEM((SH, 12 * HD), BF16)]
+    (out,) = call(kernel, [((SH, DL), F32)], [VMEM] * 5, scratch, limit=24)(*lanes, *weights)
+    return out
+
+
+def project(so_far, lanes, sibs, weights):
+    def kernel(far_ref, lane0_ref, lane1_ref, sib0_ref, sib1_ref, w0_ref, w1_ref, w2_ref, top_ref, bottom_ref, out_ref, rows, low, high):
+        side = lax.axis_index("mx") & 1
+        last = slice(12 * HD, 16 * HD)
+        for at, lane_ref, sib_ref in ((slice(0, FIRST), lane0_ref, sib0_ref), (slice(FIRST, SH), lane1_ref, sib1_ref)):
+            rows[at, :] = sib_ref[:, 0 : 12 * HD]
+            one, two = lane_ref[:, last], sib_ref[:, last]
+            low[at, :] = jnp.where(side == 0, one, two)
+            high[at, :] = jnp.where(side == 0, two, one)
+        place = pl.ds(pl.multiple_of((1 - side) * 4 * HD, 4 * HD), 4 * HD)
+        for n in range(3):
+            columns = slice(n * 256, (n + 1) * 256)
+            total = far_ref[:, columns]
+            for d, ref in enumerate((w0_ref, w1_ref, w2_ref)):
+                heads = slice(d * 4 * HD, (d + 1) * 4 * HD)
+                total = total + jnp.dot(rows[:, heads], ref[place, columns], preferred_element_type=F32)
+            total = total + jnp.dot(low[...], top_ref[:, columns], preferred_element_type=F32)
+            total = total + jnp.dot(high[...], bottom_ref[:, columns], preferred_element_type=F32)
             out_ref[:, columns] = total.astype(BF16)
 
-    scratch = [pltpu.VMEM((SH, 16 * HD), BF16)] * 2
-    (out,) = call(kernel, [((SH, DL), BF16)], [VMEM] * 9, scratch, limit=24)(*lanes, *sibs, *weights)
+    scratch = [pltpu.VMEM((SH, 12 * HD), BF16)] + [pltpu.VMEM((SH, 4 * HD), BF16)] * 2
+    (out,) = call(kernel, [((SH, DL), BF16)], [VMEM] * 10, scratch, limit=24)(so_far, *lanes, *sibs, *weights)
     return out
 
 
@@ -415,14 +480,15 @@
         got0 = swap(part0, "mx", 2)
     with scope("rows_far"):
         x3 = shift(again, "my", 2)
+    with scope("sum0"):
+        (kept0,) = kept_part([patches], [s0], own_keep, sib_keep, stat0)
     with scope("chunk12"):
-        x12 = join([next_rows, last_rows], 0, (got0,))
-        s12 = swap(x12, "mx", 1)
-    with scope("sum0"):
-        own0, next0 = keep_part(patches, s0, own_keep, sib_keep, stat0, got0)
+        x12 = [next_rows, last_rows]
+        s12 = [swap(x, "mx", 1) for x in x12]
+        product = own_product(x12, own_send, (kept0,))
+        own0, next0 = add_part(kept0, got0, after=(product,))
         end0 = swap(next0, "mx", 4)
-    with scope("chunk12"):
-        part12, stat12, _ = send_part(x12, s12, own_send, sib_send, after=(next0,))
+        part12, stat12 = rest_part(x12, s12, sib_send, product, (next0,))
         got12 = swap(part12, "mx", 2)
     with scope("chunk3"):
         (x3,) = gate([x3], (part12, end0))
@@ -430,14 +496,15 @@
         part3, stat3, _ = send_part(x3, s3, own_send, sib_send, (stat0, stat12), (part12, places))
         got3 = swap(part3, "mx", 2)
     with scope("sum12"):
-        own12, next12, tot0 = keep_part(x12, s12, own_keep, sib_keep, stat12, got12, (own0, end0), after=(part3,))
+        (kept12,) = kept_part(x12, s12, own_keep, sib_keep, stat12, after=(part3,))
+        own12, next12, tot0 = add_part(kept12, got12, (own0, end0))
         end12 = swap(next12, "mx", 4)
     with scope("sum3"):
-        own3, next3, mine, near = keep_part(x3, s3, own_keep, sib_keep, stat3, got3, last=True, after=(next12,))
+        kept3, mine, note = kept_part([x3], [s3], own_keep, sib_keep, stat3, True, (part3,))
+        own3, next3, near = add_part(kept3, got3, note=note, after=(next12,))
         tot3, coef, cs = last_sum(own3, swap(next3, "mx", 4), mine, near)
     with scope("out_weight"):
-        held = fetch(out_weight, (x3,))
-        w_next, w_last = shift(held, "my", 1), shift(held, "my", -1)
+        w_next, w_last = shift(out_weight, "my", 1), shift(out_weight, "my", -1)
         w_far = [shift(w_next[: 4 * HD], "my", 1), shift(w_last[4 * HD :], "my", -1)]
 
     with scope("attention"):
@@ -449,7 +516,9 @@
     with scope("out"):
         block = join(near, 1)
         lanes = lane_rows([block] + [swap(block, "mx", 2 * j) for j in (1, 2, 3)])
-        return project(lanes, [swap(lane, "mx", 1) for lane in lanes], [held, w_next, w_last] + w_far)
+        sibs = [swap(lane, "mx", 1) for lane in lanes]
+        so_far = project_lane(lanes, [out_weight, w_next, w_last])
+        return project(so_far, lanes, sibs, [out_weight, w_next, w_last] + w_far)
 
 
 def solution(mesh):

time: 129 us -> 124 us (0.961)
  waiting for transfers between devices: 73.6 us -> 64.9 us
  starting transfers between devices: 33.7 us -> 37.9 us
  Pallas kernels: 19.4 us -> 17.9 us
    ppermute x17 -> x18, waiting for transfers between devices: 59.7 us -> 53.2 us  [swap(): return lax.ppermute(block, axis, [(i, i ^ bits) for i in range(count)])]
    ppermute x17 -> x18, starting transfers between devices: 22 us -> 27.6 us  [swap(): return lax.ppermute(block, axis, [(i, i ^ bits) for i in range(count)])]
    ppermute x10, waiting for transfers between devices: 13.9 us -> 11.7 us  [shift(): lax.ppermute(block, axis, [((i + step) % count, i) for i in range(count)])]
    pallas_call x18 -> x21, Pallas kernels: 19.4 us -> 17.9 us  [call(): return lambda *args: made(*args, *after)]
    ppermute x10, starting transfers between devices: 11.7 us -> 10.4 us  [shift(): lax.ppermute(block, axis, [((i + step) % count, i) for i in range(count)])]
  transfers between devices with their start and end apart: 27 -> 28, of which waited for: 17 -> 16; matrix products, arithmetic and copies ran while one was open for 0% -> 0% of each run, Pallas kernels for 12% -> 12%
where the time goes in v3:
time: 124 us; the launch traced here: 123 us
  waiting for transfers between devices  64.9 us (52%)
  starting transfers between devices  37.9 us (31%)
  Pallas kernels  17.9 us (14%)
  local copies, waits for them, and re-layouts  2.47 us (2%)
    ppermute x18, waiting for transfers between devices, swap(): return lax.ppermute(block, axis, [(i, i ^ bits) for i in range(count)])  53.2 us
    ppermute x18, starting transfers between devices, swap(): return lax.ppermute(block, axis, [(i, i ^ bits) for i in range(count)])  27.6 us
    pallas_call x21, Pallas kernels, call(): return lambda *args: made(*args, *after)  17.9 us
    ppermute x10, waiting for transfers between devices, shift(): lax.ppermute(block, axis, [((i + step) % count, i) for i in range(count)])  11.7 us
    ppermute x10, starting transfers between devices, shift(): lax.ppermute(block, axis, [((i + step) % count, i) for i in range(count)])  10.4 us
  transfers between devices with their start and end apart: 28, of which 16 were waited for; matrix products, arithmetic and copies ran while one was open for 0% of the time, Pallas kernels for 12%

profile of v3, /device:TPU:1, one launch (start us, length us, event | category | flops | bytes accessed | tf_op | source)
XLA Modules:
  0.0 123.5 jit_solution(4397020530318408459)
XLA Ops:
  0.0 2.3 %copy-done = bf16[768,3,1024]{2,0,1:T(8,128)(2,1)S(1)} copy-done((bf16[768,3,1024]{2,0,1:T(8,128)(2,1)S(1)}, bf16[768,3,1024]{2,0,1:T(8,128)(2,1)}, u32[]{:S(2)}) %copy-start) | copy-done | bytes 4718616
  3.1 3.3 %collective-permute-start.1 = (bf16[768,768]{1,0:T(8,128)(2,1)S(1)}, bf16[768,768]{1,0:T(8,128)(2,1)S(1)}, u32[]{:S(2)}, u32[]{:S(2)}) collective-permute-start(bf16[768,768]{1,0:T(8,128)(2,1)S(1)} %get-tuple-element.37), channel_id=1, source_target_pairs={{0,4},{4,0},{8,12},{12,8},{16,20},{20,16},{24,28},{28,24},{1,5},{5... | collective-permute-start | bytes 3538952 | tf_op jit(solution)/shard_map/weights/ppermute | solution.py:62
  9.2 2.0 %collective-permute-done.refs_1_ = bf16[256,768]{1,0:T(8,128)(2,1)S(1)} collective-permute-done((bf16[256,768]{1,0:T(8,128)(2,1)S(1)}, bf16[256,768]{1,0:T(8,128)(2,1)S(1)}, u32[]{:S(2)}, u32[]{:S(2)}) %collective-permute-start) | collective-permute-done | bytes 393248 | tf_op jit(solution)/shard_map/chunk0/ppermute | solution.py:62
  12.2 5.4 %collective-permute-done.3.refs_0_ = bf16[256,768]{1,0:T(8,128)(2,1)S(1)} collective-permute-done((bf16[256,768]{1,0:T(8,128)(2,1)S(1)}, bf16[256,768]{1,0:T(8,128)(2,1)S(1)}, u32[]{:S(2)}, u32[]{:S(2)}) %collective-permute-start.3) | collective-permute-done | bytes 393248 | tf_op jit(solution)/shard_map/rows_near/ppermute | solution.py:67
  22.6 2.7 %collective-permute-start.9 = (bf16[256,384]{1,0:T(8,128)(2,1)S(1)}, bf16[256,384]{1,0:T(8,128)(2,1)S(1)}, u32[]{:S(2)}, u32[]{:S(2)}) collective-permute-start(bf16[256,384]{1,0:T(8,128)(2,1)S(1)} %get-tuple-element.43.refs_6_), channel_id=1, source_target_pairs={{0,16},{4,20},{8,24},{12,28},{16,0},{20,4},{24,8},{28,12},{1,17},{... | collective-permute-start | bytes 589832 | tf_op jit(solution)/shard_map/chunk12/ppermute | solution.py:62
  26.6 1.7 %collective-permute-start.12 = (bf16[512,768]{1,0:T(8,128)(2,1)S(1)}, bf16[512,768]{1,0:T(8,128)(2,1)S(1)}, u32[]{:S(2)}, u32[]{:S(2)}) collective-permute-start(bf16[512,768]{1,0:T(8,128)(2,1)S(1)} %get-tuple-element.44.refs_1_.refs_6_), channel_id=1, source_target_pairs={{0,8},{4,12},{8,0},{12,4},{16,24},{20,28},{24,16},{28,20},{1,9},{5... | collective-permute-start | bytes 2359304 | tf_op jit(solution)/shard_map/chunk12/ppermute | solution.py:62
  29.8 2.9 %collective-permute-done.2.refs_0_ = bf16[256,768]{1,0:T(8,128)(2,1)S(1)} collective-permute-done((bf16[256,768]{1,0:T(8,128)(2,1)S(1)}, bf16[256,768]{1,0:T(8,128)(2,1)S(1)}, u32[]{:S(2)}, u32[]{:S(2)}) %collective-permute-start.2) | collective-permute-done | bytes 393248 | tf_op jit(solution)/shard_map/rows_far/ppermute | solution.py:67
  33.6 1.9 %collective-permute-start.10 = (bf16[256,768]{1,0:T(8,128)(2,1)S(1)}, bf16[256,768]{1,0:T(8,128)(2,1)S(1)}, u32[]{:S(2)}, u32[]{:S(2)}) collective-permute-start(bf16[256,768]{1,0:T(8,128)(2,1)S(1)} %chunk3.2.refs_0_), channel_id=1, source_target_pairs={{0,4},{4,0},{8,12},{12,8},{16,20},{20,16},{24,28},{28,24},{1,5},{5... | collective-permute-start | bytes 1179656 | tf_op jit(solution)/shard_map/chunk3/ppermute | solution.py:62
  36.8 1.7 %chunk3.3 = (bf16[288,768]{1,0:T(8,128)(2,1)S(1)}, f32[8,256]{1,0:T(8,128)S(1)}, bf16[256,768]{1,0:T(8,128)(2,1)}) custom-call(bf16[256,768]{1,0:T(8,128)(2,1)S(1)} %chunk3.2.refs_0_, bf16[256,768]{1,0:T(8,128)(2,1)S(1)} %collective-permute-done.10.refs_1_, bf16[768,768]{1,0:T(8,128)(2,1)S(1)} %get-tuple-element.36.refs_2_, ...), custom_call_target="tpu_custom_call" | custom-call | bytes 1024 | tf_op jit(solution)/shard_map/chunk3/pallas_call | solution.py:47
  39.0 1.6 %sum12.2.refs_0_ = f32[512,768]{1,0:T(8,128)S(1)} custom-call(bf16[256,768]{1,0:T(8,128)(2,1)S(1)} %collective-permute-done.3.refs_0_, bf16[256,768]{1,0:T(8,128)(2,1)S(1)} %collective-permute-done.4.refs_1_, bf16[256,768]{1,0:T(8,128)(2,1)S(1)} %collective-permute-done.5.refs_2_, bf16[256,768]{1,0:T(8,128)(2,1)S(1)} %collective-permute-done.6.refs_3_, ...), custom_call_target="tpu_custom_call" | custom-call | bytes 1024 | tf_op jit(solution)/shard_map/sum12/pallas_call | solution.py:47
  40.6 8.1 %collective-permute-done.12.refs_1_ = bf16[512,768]{1,0:T(8,128)(2,1)S(1)} collective-permute-done((bf16[512,768]{1,0:T(8,128)(2,1)S(1)}, bf16[512,768]{1,0:T(8,128)(2,1)S(1)}, u32[]{:S(2)}, u32[]{:S(2)}) %collective-permute-start.12) | collective-permute-done | bytes 786464 | tf_op jit(solution)/shard_map/chunk12/ppermute | solution.py:62
  50.8 13.4 %collective-permute-done.11.refs_1_ = bf16[288,768]{1,0:T(8,128)(2,1)S(1)} collective-permute-done((bf16[288,768]{1,0:T(8,128)(2,1)S(1)}, bf16[288,768]{1,0:T(8,128)(2,1)S(1)}, u32[]{:S(2)}, u32[]{:S(2)}) %collective-permute-start.11) | collective-permute-done | bytes 442400 | tf_op jit(solution)/shard_map/chunk3/ppermute | solution.py:62
  64.4 13.8 %collective-permute-done.13.refs_1_ = bf16[320,384]{1,0:T(8,128)(2,1)S(1)} collective-permute-done((bf16[320,384]{1,0:T(8,128)(2,1)S(1)}, bf16[320,384]{1,0:T(8,128)(2,1)S(1)}, u32[]{:S(2)}, u32[]{:S(2)}) %collective-permute-start.13) | collective-permute-done | bytes 245792 | tf_op jit(solution)/shard_map/sum3/ppermute | solution.py:62
  78.5 2.8 %attention.2.refs_1_ = bf16[1024,128]{1,0:T(8,128)(2,1)S(1)} custom-call(s32[16]{0:T(128)S(1)} %weights.3.refs_7_.refs_0_, f32[1024,128]{1,0:T(8,128)S(1)} %get-tuple-element.56.refs_1_, f32[8,384]{1,0:T(8,128)S(1)} %get-tuple-element.57.refs_2_, f32[256,384]{1,0:T(8,128)S(1)} %get-tuple-element.58.refs_3_, f32[512,384]{1,0:T(8,128)S(1)} %get-tuple-element.59.refs_4_, ...), custom_call_target="tpu_custom_call" | custom-call | bytes 1024 | tf_op jit(solution)/shard_map/attention/pallas_call | solution.py:47
  82.6 4.3 %collective-permute-done.15.refs_2_ = bf16[1024,128]{1,0:T(8,128)(2,1)S(1)} collective-permute-done((bf16[1024,128]{1,0:T(8,128)(2,1)S(1)}, bf16[1024,128]{1,0:T(8,128)(2,1)S(1)}, u32[]{:S(2)}, u32[]{:S(2)}) %collective-permute-start.15) | collective-permute-done | bytes 262176 | tf_op jit(solution)/shard_map/attention/ppermute | solution.py:62
  87.6 2.5 %collective-permute-start.16 = (bf16[256,128]{1,0:T(8,128)(2,1)S(1)}, bf16[256,128]{1,0:T(8,128)(2,1)S(1)}, u32[]{:S(2)}, u32[]{:S(2)}) collective-permute-start(bf16[256,128]{1,0:T(8,128)(2,1)S(1)} %get-tuple-element.62), channel_id=1, source_target_pairs={{1,0},{2,1},{3,2},{0,3},{5,4},{6,5},{7,6},{4,7},{9,8},{10,9},{11,1... | collective-permute-start | bytes 196616 | tf_op jit(solution)/shard_map/attention/ppermute | solution.py:67
  90.1 2.4 %collective-permute-start.18 = (bf16[256,128]{1,0:T(8,128)(2,1)S(1)}, bf16[256,128]{1,0:T(8,128)(2,1)S(1)}, u32[]{:S(2)}, u32[]{:S(2)}) collective-permute-start(bf16[256,128]{1,0:T(8,128)(2,1)S(1)} %get-tuple-element.64), channel_id=1, source_target_pairs={{2,0},{3,1},{0,2},{1,3},{6,4},{7,5},{4,6},{5,7},{10,8},{11,9},{8,1... | collective-permute-start | bytes 196616 | tf_op jit(solution)/shard_map/attention/ppermute | solution.py:67
  92.5 2.6 %collective-permute-done.17.refs_2_ = bf16[256,128]{1,0:T(8,128)(2,1)S(1)} collective-permute-done((bf16[256,128]{1,0:T(8,128)(2,1)S(1)}, bf16[256,128]{1,0:T(8,128)(2,1)S(1)}, u32[]{:S(2)}, u32[]{:S(2)}) %collective-permute-start.17) | collective-permute-done | bytes 65568 | tf_op jit(solution)/shard_map/attention/ppermute | solution.py:67
  95.3 2.2 %collective-permute-start.20 = (bf16[256,512]{1,0:T(8,128)(2,1)S(1)}, bf16[256,512]{1,0:T(8,128)(2,1)S(1)}, u32[]{:S(2)}, u32[]{:S(2)}) collective-permute-start(bf16[256,512]{1,0:T(8,128)(2,1)S(1)} %out.4.refs_0_), channel_id=1, source_target_pairs={{0,16},{4,20},{8,24},{12,28},{16,0},{20,4},{24,8},{28,12},{1,17},{... | collective-permute-start | bytes 786440 | tf_op jit(solution)/shard_map/out/ppermute | solution.py:62
  98.9 2.5 %collective-permute-start.26 = (bf16[512,768]{1,0:T(8,128)(2,1)S(1)}, bf16[512,768]{1,0:T(8,128)(2,1)S(1)}, u32[]{:S(2)}, u32[]{:S(2)}) collective-permute-start(bf16[512,768]{1,0:T(8,128)(2,1)S(1)} %slice.8), channel_id=1, source_target_pairs={{1,0},{2,1},{3,2},{0,3},{5,4},{6,5},{7,6},{4,7},{9,8},{10,9},{11,1... | collective-permute-start | bytes 2359304 | tf_op jit(solution)/shard_map/out_weight/ppermute | solution.py:67
  101.5 2.7 %collective-permute-done.19.refs_1_ = bf16[256,512]{1,0:T(8,128)(2,1)S(1)} collective-permute-done((bf16[256,512]{1,0:T(8,128)(2,1)S(1)}, bf16[256,512]{1,0:T(8,128)(2,1)S(1)}, u32[]{:S(2)}, u32[]{:S(2)}) %collective-permute-start.19) | collective-permute-done | bytes 262176 | tf_op jit(solution)/shard_map/out/ppermute | solution.py:62
  104.7 5.6 %collective-permute-done.21.refs_3_ = bf16[256,512]{1,0:T(8,128)(2,1)S(1)} collective-permute-done((bf16[256,512]{1,0:T(8,128)(2,1)S(1)}, bf16[256,512]{1,0:T(8,128)(2,1)S(1)}, u32[]{:S(2)}, u32[]{:S(2)}) %collective-permute-start.21) | collective-permute-done | bytes 262176 | tf_op jit(solution)/shard_map/out/ppermute | solution.py:62
  110.6 8.7 %collective-permute-start.24 = (bf16[160,2048]{1,0:T(8,128)(2,1)S(1)}, bf16[160,2048]{1,0:T(8,128)(2,1)S(1)}, u32[]{:S(2)}, u32[]{:S(2)}) collective-permute-start(bf16[160,2048]{1,0:T(8,128)(2,1)S(1)} %get-tuple-element.65.refs_0_.refs_1_), channel_id=1, source_target_pairs={{0,4},{4,0},{8,12},{12,8},{16,20},{20,16},{24,28},{28,24},{1,5},{5... | collective-permute-start | bytes 1966088 | tf_op jit(solution)/shard_map/out/ppermute | solution.py:62
  121.5 1.9 %out.7 = bf16[256,768]{1,0:T(8,128)(2,1)} custom-call(f32[256,768]{1,0:T(8,128)S(1)} %out.6.refs_0_, bf16[160,2048]{1,0:T(8,128)(2,1)S(1)} %get-tuple-element.65.refs_0_.refs_1_, bf16[96,2048]{1,0:T(8,128)(2,1)S(1)} %get-tuple-element.66.refs_1_.refs_2_, bf16[160,2048]{1,0:T(8,128)(2,1)S(1)} %collective-permute-done.24.refs_3_, ...), custom_call_target="tpu_custom_call" | custom-call | bytes 1024 | tf_op jit(solution)/shard_map/out/pallas_call | solution.py:47
  (67 shorter events, 24.1 us)
Async XLA Ops:
  3.1 8.1 %collective-permute-start.1 = (bf16[768,768]{1,0:T(8,128)(2,1)S(1)}, bf16[768,768]{1,0:T(8,128)(2,1)S(1)}, u32[]{:S(2)}, u32[]{:S(2)}) collective-permute-start(bf16[768,768]{1,0:T(8,128)(2,1)S(1)} %get-tuple-element.37), channel_id=1, source_target_pairs={{0,4},{4,0},{8,12},{12,8},{16,20},{20,16},{24,28},{28,24},{1,5},{5... | collective-permute-start | bytes 3538952 | tf_op jit(solution)/shard_map/weights/ppermute | solution.py:62
  6.4 14.0 %collective-permute-start.7 = (bf16[768,768]{1,0:T(8,128)(2,1)S(1)}, bf16[768,768]{1,0:T(8,128)(2,1)S(1)}, u32[]{:S(2)}, u32[]{:S(2)}) collective-permute-start(bf16[768,768]{1,0:T(8,128)(2,1)S(1)} %get-tuple-element.40), channel_id=1, source_target_pairs={{0,4},{4,0},{8,12},{12,8},{16,20},{20,16},{24,28},{28,24},{1,5},{5... | collective-permute-start | bytes 3538952 | tf_op jit(solution)/shard_map/weights/ppermute | solution.py:62
  6.9 10.7 %collective-permute-start.3 = (bf16[256,768]{1,0:T(8,128)(2,1)S(1)}, bf16[256,768]{1,0:T(8,128)(2,1)S(1)}, u32[]{:S(2)}, u32[]{:S(2)}) collective-permute-start(bf16[256,768]{1,0:T(8,128)(2,1)S(1)} %copy-done.2), channel_id=1, source_target_pairs={{1,0},{2,1},{3,2},{0,3},{5,4},{6,5},{7,6},{4,7},{9,8},{10,9},{11,1... | collective-permute-start | bytes 1179656 | tf_op jit(solution)/shard_map/rows_near/ppermute | solution.py:67
  7.7 11.6 %collective-permute-start.4 = (bf16[256,768]{1,0:T(8,128)(2,1)S(1)}, bf16[256,768]{1,0:T(8,128)(2,1)S(1)}, u32[]{:S(2)}, u32[]{:S(2)}) collective-permute-start(bf16[256,768]{1,0:T(8,128)(2,1)S(1)} %copy-done.2), channel_id=1, source_target_pairs={{3,0},{0,1},{1,2},{2,3},{7,4},{4,5},{5,6},{6,7},{11,8},{8,9},{9,10... | collective-permute-start | bytes 1179656 | tf_op jit(solution)/shard_map/rows_near/ppermute | solution.py:67
  12.1 10.4 %collective-permute-start.8 = (bf16[256,768]{1,0:T(8,128)(2,1)S(1)}, bf16[256,768]{1,0:T(8,128)(2,1)S(1)}, u32[]{:S(2)}, u32[]{:S(2)}) collective-permute-start(bf16[256,768]{1,0:T(8,128)(2,1)S(1)} %get-tuple-element.42), channel_id=1, source_target_pairs={{0,8},{4,12},{8,0},{12,4},{16,24},{20,28},{24,16},{28,20},{1,9},{5... | collective-permute-start | bytes 1179656 | tf_op jit(solution)/shard_map/chunk0/ppermute | solution.py:62
  17.6 7.7 %collective-permute-start.5 = (bf16[256,768]{1,0:T(8,128)(2,1)S(1)}, bf16[256,768]{1,0:T(8,128)(2,1)S(1)}, u32[]{:S(2)}, u32[]{:S(2)}) collective-permute-start(bf16[256,768]{1,0:T(8,128)(2,1)S(1)} %collective-permute-done.3.refs_0_), channel_id=1, source_target_pairs={{0,4},{4,0},{8,12},{12,8},{16,20},{20,16},{24,28},{28,24},{1,5},{5... | collective-permute-start | bytes 1179656 | tf_op jit(solution)/shard_map/chunk12/ppermute | solution.py:62
  19.2 6.1 %collective-permute-start.6 = (bf16[256,768]{1,0:T(8,128)(2,1)S(1)}, bf16[256,768]{1,0:T(8,128)(2,1)S(1)}, u32[]{:S(2)}, u32[]{:S(2)}) collective-permute-start(bf16[256,768]{1,0:T(8,128)(2,1)S(1)} %collective-permute-done.4.refs_1_), channel_id=1, source_target_pairs={{0,4},{4,0},{8,12},{12,8},{16,20},{20,16},{24,28},{28,24},{1,5},{5... | collective-permute-start | bytes 1179656 | tf_op jit(solution)/shard_map/chunk12/ppermute | solution.py:62
  20.4 12.2 %collective-permute-start.2 = (bf16[256,768]{1,0:T(8,128)(2,1)S(1)}, bf16[256,768]{1,0:T(8,128)(2,1)S(1)}, u32[]{:S(2)}, u32[]{:S(2)}) collective-permute-start(bf16[256,768]{1,0:T(8,128)(2,1)S(1)} %get-tuple-element.38), channel_id=1, source_target_pairs={{2,0},{3,1},{0,2},{1,3},{6,4},{7,5},{4,6},{5,7},{10,8},{11,9},{8,1... | collective-permute-start | bytes 1179656 | tf_op jit(solution)/shard_map/rows_far/ppermute | solution.py:67
  22.6 11.0 %collective-permute-start.9 = (bf16[256,384]{1,0:T(8,128)(2,1)S(1)}, bf16[256,384]{1,0:T(8,128)(2,1)S(1)}, u32[]{:S(2)}, u32[]{:S(2)}) collective-permute-start(bf16[256,384]{1,0:T(8,128)(2,1)S(1)} %get-tuple-element.43.refs_6_), channel_id=1, source_target_pairs={{0,16},{4,20},{8,24},{12,28},{16,0},{20,4},{24,8},{28,12},{1,17},{... | collective-permute-start | bytes 589832 | tf_op jit(solution)/shard_map/chunk12/ppermute | solution.py:62
  26.6 22.1 %collective-permute-start.12 = (bf16[512,768]{1,0:T(8,128)(2,1)S(1)}, bf16[512,768]{1,0:T(8,128)(2,1)S(1)}, u32[]{:S(2)}, u32[]{:S(2)}) collective-permute-start(bf16[512,768]{1,0:T(8,128)(2,1)S(1)} %get-tuple-element.44.refs_1_.refs_6_), channel_id=1, source_target_pairs={{0,8},{4,12},{8,0},{12,4},{16,24},{20,28},{24,16},{28,20},{1,9},{5... | collective-permute-start | bytes 2359304 | tf_op jit(solution)/shard_map/chunk12/ppermute | solution.py:62
  28.4 70.4 %collective-permute-start.22 = (bf16[1024,768]{1,0:T(8,128)(2,1)S(1)}, bf16[1024,768]{1,0:T(8,128)(2,1)S(1)}, u32[]{:S(2)}, u32[]{:S(2)}) collective-permute-start(bf16[1024,768]{1,0:T(8,128)(2,1)S(1)} %copy-done.1), channel_id=1, source_target_pairs={{1,0},{2,1},{3,2},{0,3},{5,4},{6,5},{7,6},{4,7},{9,8},{10,9},{11,1... | collective-permute-start | bytes 4718600 | tf_op jit(solution)/shard_map/out_weight/ppermute | solution.py:67
  29.5 71.8 %collective-permute-start.23 = (bf16[1024,768]{1,0:T(8,128)(2,1)S(1)}, bf16[1024,768]{1,0:T(8,128)(2,1)S(1)}, u32[]{:S(2)}, u32[]{:S(2)}) collective-permute-start(bf16[1024,768]{1,0:T(8,128)(2,1)S(1)} %copy-done.1), channel_id=1, source_target_pairs={{3,0},{0,1},{1,2},{2,3},{7,4},{4,5},{5,6},{6,7},{11,8},{8,9},{9,10... | collective-permute-start | bytes 4718600 | tf_op jit(solution)/shard_map/out_weight/ppermute | solution.py:67
  38.5 25.6 %collective-permute-start.11 = (bf16[288,768]{1,0:T(8,128)(2,1)S(1)}, bf16[288,768]{1,0:T(8,128)(2,1)S(1)}, u32[]{:S(2)}, u32[]{:S(2)}) collective-permute-start(bf16[288,768]{1,0:T(8,128)(2,1)S(1)} %get-tuple-element.47.refs_5_.refs_7_), channel_id=1, source_target_pairs={{0,8},{4,12},{8,0},{12,4},{16,24},{20,28},{24,16},{28,20},{1,9},{5... | collective-permute-start | bytes 1327112 | tf_op jit(solution)/shard_map/chunk3/ppermute | solution.py:62
  48.9 29.6 %collective-permute-start.14 = (bf16[512,384]{1,0:T(8,128)(2,1)S(1)}, bf16[512,384]{1,0:T(8,128)(2,1)S(1)}, u32[]{:S(2)}, u32[]{:S(2)}) collective-permute-start(bf16[512,384]{1,0:T(8,128)(2,1)S(1)} %get-tuple-element.51.refs_3_), channel_id=1, source_target_pairs={{0,16},{4,20},{8,24},{12,28},{16,0},{20,4},{24,8},{28,12},{1,17},{... | collective-permute-start | bytes 1179656 | tf_op jit(solution)/shard_map/sum12/ppermute | solution.py:62
  64.3 13.9 %collective-permute-start.13 = (bf16[320,384]{1,0:T(8,128)(2,1)S(1)}, bf16[320,384]{1,0:T(8,128)(2,1)S(1)}, u32[]{:S(2)}, u32[]{:S(2)}) collective-permute-start(bf16[320,384]{1,0:T(8,128)(2,1)S(1)} %get-tuple-element.53), channel_id=1, source_target_pairs={{0,16},{4,20},{8,24},{12,28},{16,0},{20,4},{24,8},{28,12},{1,17},{... | collective-permute-start | bytes 737288 | tf_op jit(solution)/shard_map/sum3/ppermute | solution.py:62
  81.2 5.7 %collective-permute-start.15 = (bf16[1024,128]{1,0:T(8,128)(2,1)S(1)}, bf16[1024,128]{1,0:T(8,128)(2,1)S(1)}, u32[]{:S(2)}, u32[]{:S(2)}) collective-permute-start(bf16[1024,128]{1,0:T(8,128)(2,1)S(1)} %attention.2.refs_1_), channel_id=1, source_target_pairs={{0,32},{32,0},{64,96},{96,64},{128,160},{160,128},{192,224},{224,1... | collective-permute-start | bytes 786440 | tf_op jit(solution)/shard_map/attention/ppermute | solution.py:62
  90.1 5.0 %collective-permute-start.17 = (bf16[256,128]{1,0:T(8,128)(2,1)S(1)}, bf16[256,128]{1,0:T(8,128)(2,1)S(1)}, u32[]{:S(2)}, u32[]{:S(2)}) collective-permute-start(bf16[256,128]{1,0:T(8,128)(2,1)S(1)} %get-tuple-element.63), channel_id=1, source_target_pairs={{3,0},{0,1},{1,2},{2,3},{7,4},{4,5},{5,6},{6,7},{11,8},{8,9},{9,10... | collective-permute-start | bytes 196616 | tf_op jit(solution)/shard_map/attention/ppermute | solution.py:67
  90.1 5.0 %collective-permute-start.18 = (bf16[256,128]{1,0:T(8,128)(2,1)S(1)}, bf16[256,128]{1,0:T(8,128)(2,1)S(1)}, u32[]{:S(2)}, u32[]{:S(2)}) collective-permute-start(bf16[256,128]{1,0:T(8,128)(2,1)S(1)} %get-tuple-element.64), channel_id=1, source_target_pairs={{2,0},{3,1},{0,2},{1,3},{6,4},{7,5},{4,6},{5,7},{10,8},{11,9},{8,1... | collective-permute-start | bytes 196616 | tf_op jit(solution)/shard_map/attention/ppermute | solution.py:67
  95.2 9.1 %collective-permute-start.19 = (bf16[256,512]{1,0:T(8,128)(2,1)S(1)}, bf16[256,512]{1,0:T(8,128)(2,1)S(1)}, u32[]{:S(2)}, u32[]{:S(2)}) collective-permute-start(bf16[256,512]{1,0:T(8,128)(2,1)S(1)} %out.4.refs_0_), channel_id=1, source_target_pairs={{0,8},{4,12},{8,0},{12,4},{16,24},{20,28},{24,16},{28,20},{1,9},{5... | collective-permute-start | bytes 786440 | tf_op jit(solution)/shard_map/out/ppermute | solution.py:62
  95.3 9.4 %collective-permute-start.20 = (bf16[256,512]{1,0:T(8,128)(2,1)S(1)}, bf16[256,512]{1,0:T(8,128)(2,1)S(1)}, u32[]{:S(2)}, u32[]{:S(2)}) collective-permute-start(bf16[256,512]{1,0:T(8,128)(2,1)S(1)} %out.4.refs_0_), channel_id=1, source_target_pairs={{0,16},{4,20},{8,24},{12,28},{16,0},{20,4},{24,8},{28,12},{1,17},{... | collective-permute-start | bytes 786440 | tf_op jit(solution)/shard_map/out/ppermute | solution.py:62
  97.5 12.8 %collective-permute-start.21 = (bf16[256,512]{1,0:T(8,128)(2,1)S(1)}, bf16[256,512]{1,0:T(8,128)(2,1)S(1)}, u32[]{:S(2)}, u32[]{:S(2)}) collective-permute-start(bf16[256,512]{1,0:T(8,128)(2,1)S(1)} %out.4.refs_0_), channel_id=1, source_target_pairs={{0,24},{4,28},{8,16},{12,20},{16,8},{20,12},{24,0},{28,4},{1,25},{... | collective-permute-start | bytes 786440 | tf_op jit(solution)/shard_map/out/ppermute | solution.py:62
  98.9 21.3 %collective-permute-start.26 = (bf16[512,768]{1,0:T(8,128)(2,1)S(1)}, bf16[512,768]{1,0:T(8,128)(2,1)S(1)}, u32[]{:S(2)}, u32[]{:S(2)}) collective-permute-start(bf16[512,768]{1,0:T(8,128)(2,1)S(1)} %slice.8), channel_id=1, source_target_pairs={{1,0},{2,1},{3,2},{0,3},{5,4},{6,5},{7,6},{4,7},{9,8},{10,9},{11,1... | collective-permute-start | bytes 2359304 | tf_op jit(solution)/shard_map/out_weight/ppermute | solution.py:67
  101.4 18.7 %collective-permute-start.27 = (bf16[512,768]{1,0:T(8,128)(2,1)S(1)}, bf16[512,768]{1,0:T(8,128)(2,1)S(1)}, u32[]{:S(2)}, u32[]{:S(2)}) collective-permute-start(bf16[512,768]{1,0:T(8,128)(2,1)S(1)} %slice.9), channel_id=1, source_target_pairs={{3,0},{0,1},{1,2},{2,3},{7,4},{4,5},{5,6},{6,7},{11,8},{8,9},{9,10... | collective-permute-start | bytes 2359304 | tf_op jit(solution)/shard_map/out_weight/ppermute | solution.py:67
  110.6 11.0 %collective-permute-start.24 = (bf16[160,2048]{1,0:T(8,128)(2,1)S(1)}, bf16[160,2048]{1,0:T(8,128)(2,1)S(1)}, u32[]{:S(2)}, u32[]{:S(2)}) collective-permute-start(bf16[160,2048]{1,0:T(8,128)(2,1)S(1)} %get-tuple-element.65.refs_0_.refs_1_), channel_id=1, source_target_pairs={{0,4},{4,0},{8,12},{12,8},{16,20},{20,16},{24,28},{28,24},{1,5},{5... | collective-permute-start | bytes 1966088 | tf_op jit(solution)/shard_map/out/ppermute | solution.py:62
  (10 other events, 53.9 us)

commit v4 on v3

--- a/solution.py
+++ b/solution.py
@@ -18,6 +18,8 @@
 ORDER = (0, 2, 1, 3)
 FIRST = 160
 EXTRA = 32
+TERMS = 24
+SENT = (2, 1, 3)
 F32 = jnp.float32
 BF16 = jnp.bfloat16
 
@@ -294,11 +296,12 @@
             refs[len(ins)][...] = refs[0][...] + refs[1][...].astype(F32)
         if last:
             under = slice(count, count + EXTRA)
-            send_ref[under, :] = refs[len(ins) - 3][...]
-            send_ref[count + EXTRA : count + 2 * EXTRA, :] = got_ref[under, HEAD:]
+            terms = [refs[len(ins) - 3][...], got_ref[under, HEAD:]]
+            terms = jnp.concatenate([rows.astype(F32)[0:TERMS, :] for rows in terms], axis=0)
+            send_ref[count : count + 2 * TERMS, :] = terms.astype(BF16)
             refs[-1][...] = read_note(got_ref[under, 0:HEAD])
 
-    outs = [((count, HEAD), F32), ((count + 2 * EXTRA if last else count, HEAD), BF16)]
+    outs = [((count, HEAD), F32), ((count + 2 * TERMS if last else count, HEAD), BF16)]
     outs += [((SH, HEAD), F32)] if extra else []
     outs += [((8, HEAD), F32)] if last else []
     return call(kernel, outs, [VMEM] * len(ins), after=after)(*ins)
@@ -308,8 +311,8 @@
     def kernel(own_ref, got_ref, mine_ref, near_ref, out_ref, coef_ref, cs_ref):
         out_ref[...] = own_ref[...] + got_ref[0:SH, :].astype(F32)
         notes = [mine_ref[...], near_ref[...]]
-        for at in (SH, SH + EXTRA):
-            notes.append(read_note(got_ref[at : at + EXTRA, :]))
+        terms = got_ref[SH : SH + 2 * TERMS, :].astype(F32)
+        notes += [read_note(terms[at : at + TERMS, :]) for at in (0, TERMS)]
         for k in range(4):
             sums = [n[k : k + 1, 0:SH] for n in notes]
             squares = [n[4 + k : 5 + k, 0:SH] for n in notes]
@@ -408,7 +411,7 @@
 def lane_rows(blocks):
     def kernel(*refs):
         z = lax.axis_index("mx") >> 1
-        for j, ref in enumerate(refs[:4]):
+        for j, ref in zip((0,) + SENT, refs[:4]):
             for d in range(4):
                 at = pl.multiple_of((d * 4 + (z ^ j)) * HD, HD)
                 refs[4][:, pl.ds(at, HD)] = ref[0:FIRST, d * HD : (d + 1) * HD]
@@ -493,14 +496,16 @@
     with scope("chunk3"):
         (x3,) = gate([x3], (part12, end0))
         s3 = swap(x3, "mx", 1)
-        part3, stat3, _ = send_part(x3, s3, own_send, sib_send, (stat0, stat12), (part12, places))
-        got3 = swap(part3, "mx", 2)
+        (kept12,) = kept_part(x12, s12, own_keep, sib_keep, stat12, after=(part12,))
+        part3, stat3, _ = send_part(x3, s3, own_send, sib_send, (stat0, stat12), (kept12, places))
+        kept3, mine, note = kept_part([x3], [s3], own_keep, sib_keep, stat3, True, (part3,))
+        (held3,) = gate([part3], (kept3, kept12))
+        got3 = swap(held3, "mx", 2)
     with scope("sum12"):
-        (kept12,) = kept_part(x12, s12, own_keep, sib_keep, stat12, after=(part3,))
+
         own12, next12, tot0 = add_part(kept12, got12, (own0, end0))
         end12 = swap(next12, "mx", 4)
     with scope("sum3"):
-        kept3, mine, note = kept_part([x3], [s3], own_keep, sib_keep, stat3, True, (part3,))
         own3, next3, near = add_part(kept3, got3, note=note, after=(next12,))
         tot3, coef, cs = last_sum(own3, swap(next3, "mx", 4), mine, near)
     with scope("out_weight"):
@@ -515,7 +520,7 @@
 
     with scope("out"):
         block = join(near, 1)
-        lanes = lane_rows([block] + [swap(block, "mx", 2 * j) for j in (1, 2, 3)])
+        lanes = lane_rows([block] + [swap(block, "mx", 2 * j) for j in SENT])
         sibs = [swap(lane, "mx", 1) for lane in lanes]
         so_far = project_lane(lanes, [out_weight, w_next, w_last])
         return project(so_far, lanes, sibs, [out_weight, w_next, w_last] + w_far)

time: 124 us -> 123 us (level)
    ppermute x18, starting transfers between devices: 27.6 us -> 26.3 us  [swap(): return lax.ppermute(block, axis, [(i, i ^ bits) for i in range(count)])]
    pallas_call x21 -> x22, Pallas kernels: 17.9 us -> 18.2 us  [call(): return lambda *args: made(*args, *after)]
  transfers between devices with their start and end apart: 28 -> 28, of which waited for: 16 -> 13; matrix products, arithmetic and copies ran while one was open for 0% -> 0% of each run, Pallas kernels for 12% -> 13%
where the time goes in v4:
time: 123 us; the launch traced here: 122 us
  waiting for transfers between devices  64.3 us (52%)
  starting transfers between devices  36.7 us (30%)
  Pallas kernels  18.2 us (15%)
  local copies, waits for them, and re-layouts  2.47 us (2%)
    ppermute x18, waiting for transfers between devices, swap(): return lax.ppermute(block, axis, [(i, i ^ bits) for i in range(count)])  52.7 us
    ppermute x18, starting transfers between devices, swap(): return lax.ppermute(block, axis, [(i, i ^ bits) for i in range(count)])  26.3 us
    pallas_call x22, Pallas kernels, call(): return lambda *args: made(*args, *after)  18.2 us
    ppermute x10, waiting for transfers between devices, shift(): lax.ppermute(block, axis, [((i + step) % count, i) for i in range(count)])  11.6 us
    ppermute x10, starting transfers between devices, shift(): lax.ppermute(block, axis, [((i + step) % count, i) for i in range(count)])  10.4 us
  transfers between devices with their start and end apart: 28, of which 13 were waited for; matrix products, arithmetic and copies ran while one was open for 0% of the time, Pallas kernels for 13%

profile of v4, /device:TPU:1, one launch (start us, length us, event | category | flops | bytes accessed | tf_op | source)
XLA Modules:
  0.0 121.9 jit_solution(12010771937415644011)
XLA Ops:
  0.0 2.3 %copy-done = bf16[768,3,1024]{2,0,1:T(8,128)(2,1)S(1)} copy-done((bf16[768,3,1024]{2,0,1:T(8,128)(2,1)S(1)}, bf16[768,3,1024]{2,0,1:T(8,128)(2,1)}, u32[]{:S(2)}) %copy-start) | copy-done | bytes 4718616
  3.1 3.3 %collective-permute-start.1 = (bf16[768,768]{1,0:T(8,128)(2,1)S(1)}, bf16[768,768]{1,0:T(8,128)(2,1)S(1)}, u32[]{:S(2)}, u32[]{:S(2)}) collective-permute-start(bf16[768,768]{1,0:T(8,128)(2,1)S(1)} %get-tuple-element.37), channel_id=1, source_target_pairs={{0,4},{4,0},{8,12},{12,8},{16,20},{20,16},{24,28},{28,24},{1,5},{5... | collective-permute-start | bytes 3538952 | tf_op jit(solution)/shard_map/weights/ppermute | solution.py:64
  9.2 2.0 %collective-permute-done.refs_1_ = bf16[256,768]{1,0:T(8,128)(2,1)S(1)} collective-permute-done((bf16[256,768]{1,0:T(8,128)(2,1)S(1)}, bf16[256,768]{1,0:T(8,128)(2,1)S(1)}, u32[]{:S(2)}, u32[]{:S(2)}) %collective-permute-start) | collective-permute-done | bytes 393248 | tf_op jit(solution)/shard_map/chunk0/ppermute | solution.py:64
  12.2 5.4 %collective-permute-done.3.refs_0_ = bf16[256,768]{1,0:T(8,128)(2,1)S(1)} collective-permute-done((bf16[256,768]{1,0:T(8,128)(2,1)S(1)}, bf16[256,768]{1,0:T(8,128)(2,1)S(1)}, u32[]{:S(2)}, u32[]{:S(2)}) %collective-permute-start.3) | collective-permute-done | bytes 393248 | tf_op jit(solution)/shard_map/rows_near/ppermute | solution.py:69
  22.7 2.7 %collective-permute-start.9 = (bf16[256,384]{1,0:T(8,128)(2,1)S(1)}, bf16[256,384]{1,0:T(8,128)(2,1)S(1)}, u32[]{:S(2)}, u32[]{:S(2)}) collective-permute-start(bf16[256,384]{1,0:T(8,128)(2,1)S(1)} %get-tuple-element.43.refs_6_), channel_id=1, source_target_pairs={{0,16},{4,20},{8,24},{12,28},{16,0},{20,4},{24,8},{28,12},{1,17},{... | collective-permute-start | bytes 589832 | tf_op jit(solution)/shard_map/chunk12/ppermute | solution.py:64
  26.7 1.7 %collective-permute-start.12 = (bf16[512,768]{1,0:T(8,128)(2,1)S(1)}, bf16[512,768]{1,0:T(8,128)(2,1)S(1)}, u32[]{:S(2)}, u32[]{:S(2)}) collective-permute-start(bf16[512,768]{1,0:T(8,128)(2,1)S(1)} %get-tuple-element.44.refs_1_.refs_7_), channel_id=1, source_target_pairs={{0,8},{4,12},{8,0},{12,4},{16,24},{20,28},{24,16},{28,20},{1,9},{5... | collective-permute-start | bytes 2359304 | tf_op jit(solution)/shard_map/chunk12/ppermute | solution.py:64
  29.9 2.8 %collective-permute-done.2.refs_0_ = bf16[256,768]{1,0:T(8,128)(2,1)S(1)} collective-permute-done((bf16[256,768]{1,0:T(8,128)(2,1)S(1)}, bf16[256,768]{1,0:T(8,128)(2,1)S(1)}, u32[]{:S(2)}, u32[]{:S(2)}) %collective-permute-start.2) | collective-permute-done | bytes 393248 | tf_op jit(solution)/shard_map/rows_far/ppermute | solution.py:69
  33.6 1.9 %collective-permute-start.10 = (bf16[256,768]{1,0:T(8,128)(2,1)S(1)}, bf16[256,768]{1,0:T(8,128)(2,1)S(1)}, u32[]{:S(2)}, u32[]{:S(2)}) collective-permute-start(bf16[256,768]{1,0:T(8,128)(2,1)S(1)} %chunk3.5.refs_0_), channel_id=1, source_target_pairs={{0,4},{4,0},{8,12},{12,8},{16,20},{20,16},{24,28},{28,24},{1,5},{5... | collective-permute-start | bytes 1179656 | tf_op jit(solution)/shard_map/chunk3/ppermute | solution.py:64
  36.7 1.6 %chunk3.6.refs_6_.refs_2_.refs_0_ = f32[512,768]{1,0:T(8,128)S(1)} custom-call(bf16[256,768]{1,0:T(8,128)(2,1)S(1)} %collective-permute-done.3.refs_0_, bf16[256,768]{1,0:T(8,128)(2,1)S(1)} %collective-permute-done.4.refs_1_, bf16[256,768]{1,0:T(8,128)(2,1)S(1)} %collective-permute-done.5.refs_2_, bf16[256,768]{1,0:T(8,128)(2,1)S(1)} %collective-permute-done.6.refs_3_, ...), custom_call_target="tpu_custom_call" | custom-call | bytes 1024 | tf_op jit(solution)/shard_map/chunk3/pallas_call | solution.py:49
  38.4 1.8 %chunk3.7 = (bf16[288,768]{1,0:T(8,128)(2,1)S(1)}, f32[8,256]{1,0:T(8,128)S(1)}, bf16[256,768]{1,0:T(8,128)(2,1)}) custom-call(bf16[256,768]{1,0:T(8,128)(2,1)S(1)} %chunk3.5.refs_0_, bf16[256,768]{1,0:T(8,128)(2,1)S(1)} %collective-permute-done.10.refs_1_, bf16[768,768]{1,0:T(8,128)(2,1)S(1)} %get-tuple-element.36.refs_2_, ...), custom_call_target="tpu_custom_call" | custom-call | bytes 1024 | tf_op jit(solution)/shard_map/chunk3/pallas_call | solution.py:49
  41.6 7.1 %collective-permute-done.12.refs_1_ = bf16[512,768]{1,0:T(8,128)(2,1)S(1)} collective-permute-done((bf16[512,768]{1,0:T(8,128)(2,1)S(1)}, bf16[512,768]{1,0:T(8,128)(2,1)S(1)}, u32[]{:S(2)}, u32[]{:S(2)}) %collective-permute-start.12) | collective-permute-done | bytes 786464 | tf_op jit(solution)/shard_map/chunk12/ppermute | solution.py:64
  49.9 14.3 %collective-permute-done.11.refs_1_ = bf16[288,768]{1,0:T(8,128)(2,1)S(1)} collective-permute-done((bf16[288,768]{1,0:T(8,128)(2,1)S(1)}, bf16[288,768]{1,0:T(8,128)(2,1)S(1)}, u32[]{:S(2)}, u32[]{:S(2)}) %collective-permute-start.11) | collective-permute-done | bytes 442400 | tf_op jit(solution)/shard_map/chunk3/ppermute | solution.py:64
  64.4 13.3 %collective-permute-done.13.refs_1_ = bf16[304,384]{1,0:T(8,128)(2,1)S(1)} collective-permute-done((bf16[304,384]{1,0:T(8,128)(2,1)S(1)}, bf16[304,384]{1,0:T(8,128)(2,1)S(1)}, u32[]{:S(2)}, u32[]{:S(2)}) %collective-permute-start.13) | collective-permute-done | bytes 233504 | tf_op jit(solution)/shard_map/sum3/ppermute | solution.py:64
  77.9 2.8 %attention.2.refs_1_ = bf16[1024,128]{1,0:T(8,128)(2,1)S(1)} custom-call(s32[16]{0:T(128)S(1)} %weights.3.refs_7_.refs_0_, f32[1024,128]{1,0:T(8,128)S(1)} %get-tuple-element.56.refs_1_, f32[8,384]{1,0:T(8,128)S(1)} %get-tuple-element.57.refs_2_, f32[256,384]{1,0:T(8,128)S(1)} %get-tuple-element.58.refs_3_, f32[512,384]{1,0:T(8,128)S(1)} %get-tuple-element.59.refs_4_, ...), custom_call_target="tpu_custom_call" | custom-call | bytes 1024 | tf_op jit(solution)/shard_map/attention/pallas_call | solution.py:49
  80.7 1.4 %collective-permute-start.15 = (bf16[1024,128]{1,0:T(8,128)(2,1)S(1)}, bf16[1024,128]{1,0:T(8,128)(2,1)S(1)}, u32[]{:S(2)}, u32[]{:S(2)}) collective-permute-start(bf16[1024,128]{1,0:T(8,128)(2,1)S(1)} %attention.2.refs_1_), channel_id=1, source_target_pairs={{0,32},{32,0},{64,96},{96,64},{128,160},{160,128},{192,224},{224,1... | collective-permute-start | bytes 786440 | tf_op jit(solution)/shard_map/attention/ppermute | solution.py:64
  82.1 4.3 %collective-permute-done.15.refs_2_ = bf16[1024,128]{1,0:T(8,128)(2,1)S(1)} collective-permute-done((bf16[1024,128]{1,0:T(8,128)(2,1)S(1)}, bf16[1024,128]{1,0:T(8,128)(2,1)S(1)}, u32[]{:S(2)}, u32[]{:S(2)}) %collective-permute-start.15) | collective-permute-done | bytes 262176 | tf_op jit(solution)/shard_map/attention/ppermute | solution.py:64
  87.1 2.4 %collective-permute-start.16 = (bf16[256,128]{1,0:T(8,128)(2,1)S(1)}, bf16[256,128]{1,0:T(8,128)(2,1)S(1)}, u32[]{:S(2)}, u32[]{:S(2)}) collective-permute-start(bf16[256,128]{1,0:T(8,128)(2,1)S(1)} %get-tuple-element.62), channel_id=1, source_target_pairs={{1,0},{2,1},{3,2},{0,3},{5,4},{6,5},{7,6},{4,7},{9,8},{10,9},{11,1... | collective-permute-start | bytes 196616 | tf_op jit(solution)/shard_map/attention/ppermute | solution.py:69
  89.5 2.4 %collective-permute-start.18 = (bf16[256,128]{1,0:T(8,128)(2,1)S(1)}, bf16[256,128]{1,0:T(8,128)(2,1)S(1)}, u32[]{:S(2)}, u32[]{:S(2)}) collective-permute-start(bf16[256,128]{1,0:T(8,128)(2,1)S(1)} %get-tuple-element.64), channel_id=1, source_target_pairs={{2,0},{3,1},{0,2},{1,3},{6,4},{7,5},{4,6},{5,7},{10,8},{11,9},{8,1... | collective-permute-start | bytes 196616 | tf_op jit(solution)/shard_map/attention/ppermute | solution.py:69
  91.9 2.6 %collective-permute-done.17.refs_2_ = bf16[256,128]{1,0:T(8,128)(2,1)S(1)} collective-permute-done((bf16[256,128]{1,0:T(8,128)(2,1)S(1)}, bf16[256,128]{1,0:T(8,128)(2,1)S(1)}, u32[]{:S(2)}, u32[]{:S(2)}) %collective-permute-start.17) | collective-permute-done | bytes 65568 | tf_op jit(solution)/shard_map/attention/ppermute | solution.py:69
  94.7 2.3 %collective-permute-start.20 = (bf16[256,512]{1,0:T(8,128)(2,1)S(1)}, bf16[256,512]{1,0:T(8,128)(2,1)S(1)}, u32[]{:S(2)}, u32[]{:S(2)}) collective-permute-start(bf16[256,512]{1,0:T(8,128)(2,1)S(1)} %out.4.refs_0_), channel_id=1, source_target_pairs={{0,8},{4,12},{8,0},{12,4},{16,24},{20,28},{24,16},{28,20},{1,9},{5... | collective-permute-start | bytes 786440 | tf_op jit(solution)/shard_map/out/ppermute | solution.py:64
  98.3 2.6 %collective-permute-start.26 = (bf16[512,768]{1,0:T(8,128)(2,1)S(1)}, bf16[512,768]{1,0:T(8,128)(2,1)S(1)}, u32[]{:S(2)}, u32[]{:S(2)}) collective-permute-start(bf16[512,768]{1,0:T(8,128)(2,1)S(1)} %slice.8), channel_id=1, source_target_pairs={{1,0},{2,1},{3,2},{0,3},{5,4},{6,5},{7,6},{4,7},{9,8},{10,9},{11,1... | collective-permute-start | bytes 2359304 | tf_op jit(solution)/shard_map/out_weight/ppermute | solution.py:69
  101.0 9.0 %collective-permute-done.19.refs_1_ = bf16[256,512]{1,0:T(8,128)(2,1)S(1)} collective-permute-done((bf16[256,512]{1,0:T(8,128)(2,1)S(1)}, bf16[256,512]{1,0:T(8,128)(2,1)S(1)}, u32[]{:S(2)}, u32[]{:S(2)}) %collective-permute-start.19) | collective-permute-done | bytes 262176 | tf_op jit(solution)/shard_map/out/ppermute | solution.py:64
  110.3 7.3 %collective-permute-start.24 = (bf16[160,2048]{1,0:T(8,128)(2,1)S(1)}, bf16[160,2048]{1,0:T(8,128)(2,1)S(1)}, u32[]{:S(2)}, u32[]{:S(2)}) collective-permute-start(bf16[160,2048]{1,0:T(8,128)(2,1)S(1)} %get-tuple-element.65.refs_0_.refs_1_), channel_id=1, source_target_pairs={{0,4},{4,0},{8,12},{12,8},{16,20},{20,16},{24,28},{28,24},{1,5},{5... | collective-permute-start | bytes 1966088 | tf_op jit(solution)/shard_map/out/ppermute | solution.py:64
  119.9 1.9 %out.7 = bf16[256,768]{1,0:T(8,128)(2,1)} custom-call(f32[256,768]{1,0:T(8,128)S(1)} %out.6.refs_0_, bf16[160,2048]{1,0:T(8,128)(2,1)S(1)} %get-tuple-element.65.refs_0_.refs_1_, bf16[96,2048]{1,0:T(8,128)(2,1)S(1)} %get-tuple-element.66.refs_1_.refs_2_, bf16[160,2048]{1,0:T(8,128)(2,1)S(1)} %collective-permute-done.24.refs_3_, ...), custom_call_target="tpu_custom_call" | custom-call | bytes 1024 | tf_op jit(solution)/shard_map/out/pallas_call | solution.py:49
  (68 shorter events, 22.3 us)
Async XLA Ops:
  3.1 8.1 %collective-permute-start.1 = (bf16[768,768]{1,0:T(8,128)(2,1)S(1)}, bf16[768,768]{1,0:T(8,128)(2,1)S(1)}, u32[]{:S(2)}, u32[]{:S(2)}) collective-permute-start(bf16[768,768]{1,0:T(8,128)(2,1)S(1)} %get-tuple-element.37), channel_id=1, source_target_pairs={{0,4},{4,0},{8,12},{12,8},{16,20},{20,16},{24,28},{28,24},{1,5},{5... | collective-permute-start | bytes 3538952 | tf_op jit(solution)/shard_map/weights/ppermute | solution.py:64
  6.4 14.0 %collective-permute-start.7 = (bf16[768,768]{1,0:T(8,128)(2,1)S(1)}, bf16[768,768]{1,0:T(8,128)(2,1)S(1)}, u32[]{:S(2)}, u32[]{:S(2)}) collective-permute-start(bf16[768,768]{1,0:T(8,128)(2,1)S(1)} %get-tuple-element.40), channel_id=1, source_target_pairs={{0,4},{4,0},{8,12},{12,8},{16,20},{20,16},{24,28},{28,24},{1,5},{5... | collective-permute-start | bytes 3538952 | tf_op jit(solution)/shard_map/weights/ppermute | solution.py:64
  6.9 10.7 %collective-permute-start.3 = (bf16[256,768]{1,0:T(8,128)(2,1)S(1)}, bf16[256,768]{1,0:T(8,128)(2,1)S(1)}, u32[]{:S(2)}, u32[]{:S(2)}) collective-permute-start(bf16[256,768]{1,0:T(8,128)(2,1)S(1)} %copy-done.2), channel_id=1, source_target_pairs={{1,0},{2,1},{3,2},{0,3},{5,4},{6,5},{7,6},{4,7},{9,8},{10,9},{11,1... | collective-permute-start | bytes 1179656 | tf_op jit(solution)/shard_map/rows_near/ppermute | solution.py:69
  7.7 11.6 %collective-permute-start.4 = (bf16[256,768]{1,0:T(8,128)(2,1)S(1)}, bf16[256,768]{1,0:T(8,128)(2,1)S(1)}, u32[]{:S(2)}, u32[]{:S(2)}) collective-permute-start(bf16[256,768]{1,0:T(8,128)(2,1)S(1)} %copy-done.2), channel_id=1, source_target_pairs={{3,0},{0,1},{1,2},{2,3},{7,4},{4,5},{5,6},{6,7},{11,8},{8,9},{9,10... | collective-permute-start | bytes 1179656 | tf_op jit(solution)/shard_map/rows_near/ppermute | solution.py:69
  12.1 10.4 %collective-permute-start.8 = (bf16[256,768]{1,0:T(8,128)(2,1)S(1)}, bf16[256,768]{1,0:T(8,128)(2,1)S(1)}, u32[]{:S(2)}, u32[]{:S(2)}) collective-permute-start(bf16[256,768]{1,0:T(8,128)(2,1)S(1)} %get-tuple-element.42), channel_id=1, source_target_pairs={{0,8},{4,12},{8,0},{12,4},{16,24},{20,28},{24,16},{28,20},{1,9},{5... | collective-permute-start | bytes 1179656 | tf_op jit(solution)/shard_map/chunk0/ppermute | solution.py:64
  17.6 7.7 %collective-permute-start.5 = (bf16[256,768]{1,0:T(8,128)(2,1)S(1)}, bf16[256,768]{1,0:T(8,128)(2,1)S(1)}, u32[]{:S(2)}, u32[]{:S(2)}) collective-permute-start(bf16[256,768]{1,0:T(8,128)(2,1)S(1)} %collective-permute-done.3.refs_0_), channel_id=1, source_target_pairs={{0,4},{4,0},{8,12},{12,8},{16,20},{20,16},{24,28},{28,24},{1,5},{5... | collective-permute-start | bytes 1179656 | tf_op jit(solution)/shard_map/chunk12/ppermute | solution.py:64
  19.2 6.1 %collective-permute-start.6 = (bf16[256,768]{1,0:T(8,128)(2,1)S(1)}, bf16[256,768]{1,0:T(8,128)(2,1)S(1)}, u32[]{:S(2)}, u32[]{:S(2)}) collective-permute-start(bf16[256,768]{1,0:T(8,128)(2,1)S(1)} %collective-permute-done.4.refs_1_), channel_id=1, source_target_pairs={{0,4},{4,0},{8,12},{12,8},{16,20},{20,16},{24,28},{28,24},{1,5},{5... | collective-permute-start | bytes 1179656 | tf_op jit(solution)/shard_map/chunk12/ppermute | solution.py:64
  20.4 12.2 %collective-permute-start.2 = (bf16[256,768]{1,0:T(8,128)(2,1)S(1)}, bf16[256,768]{1,0:T(8,128)(2,1)S(1)}, u32[]{:S(2)}, u32[]{:S(2)}) collective-permute-start(bf16[256,768]{1,0:T(8,128)(2,1)S(1)} %get-tuple-element.38), channel_id=1, source_target_pairs={{2,0},{3,1},{0,2},{1,3},{6,4},{7,5},{4,6},{5,7},{10,8},{11,9},{8,1... | collective-permute-start | bytes 1179656 | tf_op jit(solution)/shard_map/rows_far/ppermute | solution.py:69
  22.7 10.9 %collective-permute-start.9 = (bf16[256,384]{1,0:T(8,128)(2,1)S(1)}, bf16[256,384]{1,0:T(8,128)(2,1)S(1)}, u32[]{:S(2)}, u32[]{:S(2)}) collective-permute-start(bf16[256,384]{1,0:T(8,128)(2,1)S(1)} %get-tuple-element.43.refs_6_), channel_id=1, source_target_pairs={{0,16},{4,20},{8,24},{12,28},{16,0},{20,4},{24,8},{28,12},{1,17},{... | collective-permute-start | bytes 589832 | tf_op jit(solution)/shard_map/chunk12/ppermute | solution.py:64
  26.7 22.0 %collective-permute-start.12 = (bf16[512,768]{1,0:T(8,128)(2,1)S(1)}, bf16[512,768]{1,0:T(8,128)(2,1)S(1)}, u32[]{:S(2)}, u32[]{:S(2)}) collective-permute-start(bf16[512,768]{1,0:T(8,128)(2,1)S(1)} %get-tuple-element.44.refs_1_.refs_7_), channel_id=1, source_target_pairs={{0,8},{4,12},{8,0},{12,4},{16,24},{20,28},{24,16},{28,20},{1,9},{5... | collective-permute-start | bytes 2359304 | tf_op jit(solution)/shard_map/chunk12/ppermute | solution.py:64
  28.4 69.8 %collective-permute-start.22 = (bf16[1024,768]{1,0:T(8,128)(2,1)S(1)}, bf16[1024,768]{1,0:T(8,128)(2,1)S(1)}, u32[]{:S(2)}, u32[]{:S(2)}) collective-permute-start(bf16[1024,768]{1,0:T(8,128)(2,1)S(1)} %copy-done.1), channel_id=1, source_target_pairs={{1,0},{2,1},{3,2},{0,3},{5,4},{6,5},{7,6},{4,7},{9,8},{10,9},{11,1... | collective-permute-start | bytes 4718600 | tf_op jit(solution)/shard_map/out_weight/ppermute | solution.py:69
  29.6 71.3 %collective-permute-start.23 = (bf16[1024,768]{1,0:T(8,128)(2,1)S(1)}, bf16[1024,768]{1,0:T(8,128)(2,1)S(1)}, u32[]{:S(2)}, u32[]{:S(2)}) collective-permute-start(bf16[1024,768]{1,0:T(8,128)(2,1)S(1)} %copy-done.1), channel_id=1, source_target_pairs={{3,0},{0,1},{1,2},{2,3},{7,4},{4,5},{5,6},{6,7},{11,8},{8,9},{9,10... | collective-permute-start | bytes 4718600 | tf_op jit(solution)/shard_map/out_weight/ppermute | solution.py:69
  41.1 23.0 %collective-permute-start.11 = (bf16[288,768]{1,0:T(8,128)(2,1)S(1)}, bf16[288,768]{1,0:T(8,128)(2,1)S(1)}, u32[]{:S(2)}, u32[]{:S(2)}) collective-permute-start(bf16[288,768]{1,0:T(8,128)(2,1)S(1)} %chunk3.9), channel_id=1, source_target_pairs={{0,8},{4,12},{8,0},{12,4},{16,24},{20,28},{24,16},{28,20},{1,9},{5... | collective-permute-start | bytes 1327112 | tf_op jit(solution)/shard_map/chunk3/ppermute | solution.py:64
  48.9 29.1 %collective-permute-start.14 = (bf16[512,384]{1,0:T(8,128)(2,1)S(1)}, bf16[512,384]{1,0:T(8,128)(2,1)S(1)}, u32[]{:S(2)}, u32[]{:S(2)}) collective-permute-start(bf16[512,384]{1,0:T(8,128)(2,1)S(1)} %get-tuple-element.51.refs_3_), channel_id=1, source_target_pairs={{0,16},{4,20},{8,24},{12,28},{16,0},{20,4},{24,8},{28,12},{1,17},{... | collective-permute-start | bytes 1179656 | tf_op jit(solution)/shard_map/sum12/ppermute | solution.py:64
  64.3 13.4 %collective-permute-start.13 = (bf16[304,384]{1,0:T(8,128)(2,1)S(1)}, bf16[304,384]{1,0:T(8,128)(2,1)S(1)}, u32[]{:S(2)}, u32[]{:S(2)}) collective-permute-start(bf16[304,384]{1,0:T(8,128)(2,1)S(1)} %get-tuple-element.53), channel_id=1, source_target_pairs={{0,16},{4,20},{8,24},{12,28},{16,0},{20,4},{24,8},{28,12},{1,17},{... | collective-permute-start | bytes 700424 | tf_op jit(solution)/shard_map/sum3/ppermute | solution.py:64
  80.7 5.7 %collective-permute-start.15 = (bf16[1024,128]{1,0:T(8,128)(2,1)S(1)}, bf16[1024,128]{1,0:T(8,128)(2,1)S(1)}, u32[]{:S(2)}, u32[]{:S(2)}) collective-permute-start(bf16[1024,128]{1,0:T(8,128)(2,1)S(1)} %attention.2.refs_1_), channel_id=1, source_target_pairs={{0,32},{32,0},{64,96},{96,64},{128,160},{160,128},{192,224},{224,1... | collective-permute-start | bytes 786440 | tf_op jit(solution)/shard_map/attention/ppermute | solution.py:64
  89.5 5.0 %collective-permute-start.17 = (bf16[256,128]{1,0:T(8,128)(2,1)S(1)}, bf16[256,128]{1,0:T(8,128)(2,1)S(1)}, u32[]{:S(2)}, u32[]{:S(2)}) collective-permute-start(bf16[256,128]{1,0:T(8,128)(2,1)S(1)} %get-tuple-element.63), channel_id=1, source_target_pairs={{3,0},{0,1},{1,2},{2,3},{7,4},{4,5},{5,6},{6,7},{11,8},{8,9},{9,10... | collective-permute-start | bytes 196616 | tf_op jit(solution)/shard_map/attention/ppermute | solution.py:69
  89.5 5.0 %collective-permute-start.18 = (bf16[256,128]{1,0:T(8,128)(2,1)S(1)}, bf16[256,128]{1,0:T(8,128)(2,1)S(1)}, u32[]{:S(2)}, u32[]{:S(2)}) collective-permute-start(bf16[256,128]{1,0:T(8,128)(2,1)S(1)} %get-tuple-element.64), channel_id=1, source_target_pairs={{2,0},{3,1},{0,2},{1,3},{6,4},{7,5},{4,6},{5,7},{10,8},{11,9},{8,1... | collective-permute-start | bytes 196616 | tf_op jit(solution)/shard_map/attention/ppermute | solution.py:69
  94.6 15.5 %collective-permute-start.19 = (bf16[256,512]{1,0:T(8,128)(2,1)S(1)}, bf16[256,512]{1,0:T(8,128)(2,1)S(1)}, u32[]{:S(2)}, u32[]{:S(2)}) collective-permute-start(bf16[256,512]{1,0:T(8,128)(2,1)S(1)} %out.4.refs_0_), channel_id=1, source_target_pairs={{0,16},{4,20},{8,24},{12,28},{16,0},{20,4},{24,8},{28,12},{1,17},{... | collective-permute-start | bytes 786440 | tf_op jit(solution)/shard_map/out/ppermute | solution.py:64
  94.7 15.4 %collective-permute-start.20 = (bf16[256,512]{1,0:T(8,128)(2,1)S(1)}, bf16[256,512]{1,0:T(8,128)(2,1)S(1)}, u32[]{:S(2)}, u32[]{:S(2)}) collective-permute-start(bf16[256,512]{1,0:T(8,128)(2,1)S(1)} %out.4.refs_0_), channel_id=1, source_target_pairs={{0,8},{4,12},{8,0},{12,4},{16,24},{20,28},{24,16},{28,20},{1,9},{5... | collective-permute-start | bytes 786440 | tf_op jit(solution)/shard_map/out/ppermute | solution.py:64
  97.0 13.0 %collective-permute-start.21 = (bf16[256,512]{1,0:T(8,128)(2,1)S(1)}, bf16[256,512]{1,0:T(8,128)(2,1)S(1)}, u32[]{:S(2)}, u32[]{:S(2)}) collective-permute-start(bf16[256,512]{1,0:T(8,128)(2,1)S(1)} %out.4.refs_0_), channel_id=1, source_target_pairs={{0,24},{4,28},{8,16},{12,20},{16,8},{20,12},{24,0},{28,4},{1,25},{... | collective-permute-start | bytes 786440 | tf_op jit(solution)/shard_map/out/ppermute | solution.py:64
  98.3 20.2 %collective-permute-start.26 = (bf16[512,768]{1,0:T(8,128)(2,1)S(1)}, bf16[512,768]{1,0:T(8,128)(2,1)S(1)}, u32[]{:S(2)}, u32[]{:S(2)}) collective-permute-start(bf16[512,768]{1,0:T(8,128)(2,1)S(1)} %slice.8), channel_id=1, source_target_pairs={{1,0},{2,1},{3,2},{0,3},{5,4},{6,5},{7,6},{4,7},{9,8},{10,9},{11,1... | collective-permute-start | bytes 2359304 | tf_op jit(solution)/shard_map/out_weight/ppermute | solution.py:69
  100.9 17.6 %collective-permute-start.27 = (bf16[512,768]{1,0:T(8,128)(2,1)S(1)}, bf16[512,768]{1,0:T(8,128)(2,1)S(1)}, u32[]{:S(2)}, u32[]{:S(2)}) collective-permute-start(bf16[512,768]{1,0:T(8,128)(2,1)S(1)} %slice.9), channel_id=1, source_target_pairs={{3,0},{0,1},{1,2},{2,3},{7,4},{4,5},{5,6},{6,7},{11,8},{8,9},{9,10... | collective-permute-start | bytes 2359304 | tf_op jit(solution)/shard_map/out_weight/ppermute | solution.py:69
  110.3 9.6 %collective-permute-start.24 = (bf16[160,2048]{1,0:T(8,128)(2,1)S(1)}, bf16[160,2048]{1,0:T(8,128)(2,1)S(1)}, u32[]{:S(2)}, u32[]{:S(2)}) collective-permute-start(bf16[160,2048]{1,0:T(8,128)(2,1)S(1)} %get-tuple-element.65.refs_0_.refs_1_), channel_id=1, source_target_pairs={{0,4},{4,0},{8,12},{12,8},{16,20},{20,16},{24,28},{28,24},{1,5},{5... | collective-permute-start | bytes 1966088 | tf_op jit(solution)/shard_map/out/ppermute | solution.py:64
  (10 other events, 55.4 us)

commit v5 on v4

--- a/solution.py
+++ b/solution.py
@@ -329,11 +329,12 @@
     return call(kernel, outs, [VMEM] * 4)(own, got, mine, near)
 
 
-def join(blocks, axis, after=()):
+def join(blocks, axis, places=None, after=()):
     size = blocks[0].shape[axis]
+    places = places or range(len(blocks))
 
     def kernel(*refs):
-        for i, ref in enumerate(refs[:-1]):
+        for i, ref in zip(places, refs[:-1]):
             at = slice(i * size, (i + 1) * size)
             if axis == 0:
                 refs[-1][at, :] = ref[...]
@@ -516,10 +517,10 @@
         attended = attention(places, coef, cs, tot0, own12, end12, tot3)
         other = swap(attended, "img", 1)
         far, up, down, own = route(places, attended, other)
-        near = [own, shift(down, "my", 1), shift(up, "my", -1), shift(far, "my", 2)]
+        near = [own, shift(far, "my", 2), shift(down, "my", 1), shift(up, "my", -1)]
 
     with scope("out"):
-        block = join(near, 1)
+        block = join(near, 1, (0, 3, 1, 2))
         lanes = lane_rows([block] + [swap(block, "mx", 2 * j) for j in SENT])
         sibs = [swap(lane, "mx", 1) for lane in lanes]
         so_far = project_lane(lanes, [out_weight, w_next, w_last])

time: 123 us -> 123 us (level)
    ppermute x10, waiting for transfers between devices: 11.6 us -> 13.1 us  [shift(): lax.ppermute(block, axis, [((i + step) % count, i) for i in range(count)])]
  transfers between devices with their start and end apart: 28 -> 28, of which waited for: 13 -> 17; matrix products, arithmetic and copies ran while one was open for 0% -> 0% of each run, Pallas kernels for 13% -> 13%
where the time goes in v5:
time: 123 us; the launch traced here: 122 us
  waiting for transfers between devices  65.4 us (53%)
  starting transfers between devices  36.1 us (29%)
  Pallas kernels  18.2 us (15%)
  local copies, waits for them, and re-layouts  2.47 us (2%)
    ppermute x18, waiting for transfers between devices, swap(): return lax.ppermute(block, axis, [(i, i ^ bits) for i in range(count)])  52.3 us
    ppermute x18, starting transfers between devices, swap(): return lax.ppermute(block, axis, [(i, i ^ bits) for i in range(count)])  26.7 us
    pallas_call x22, Pallas kernels, call(): return lambda *args: made(*args, *after)  18.2 us
    ppermute x10, waiting for transfers between devices, shift(): lax.ppermute(block, axis, [((i + step) % count, i) for i in range(count)])  13.1 us
    ppermute x10, starting transfers between devices, shift(): lax.ppermute(block, axis, [((i + step) % count, i) for i in range(count)])  9.36 us
  transfers between devices with their start and end apart: 28, of which 17 were waited for; matrix products, arithmetic and copies ran while one was open for 0% of the time, Pallas kernels for 13%

profile of v5, /device:TPU:1, one launch (start us, length us, event | category | flops | bytes accessed | tf_op | source)
XLA Modules:
  0.0 122.4 jit_solution(10930677936692994368)
XLA Ops:
  0.0 2.3 %copy-done = bf16[768,3,1024]{2,0,1:T(8,128)(2,1)S(1)} copy-done((bf16[768,3,1024]{2,0,1:T(8,128)(2,1)S(1)}, bf16[768,3,1024]{2,0,1:T(8,128)(2,1)}, u32[]{:S(2)}) %copy-start) | copy-done | bytes 4718616
  3.1 3.3 %collective-permute-start.1 = (bf16[768,768]{1,0:T(8,128)(2,1)S(1)}, bf16[768,768]{1,0:T(8,128)(2,1)S(1)}, u32[]{:S(2)}, u32[]{:S(2)}) collective-permute-start(bf16[768,768]{1,0:T(8,128)(2,1)S(1)} %get-tuple-element.37), channel_id=1, source_target_pairs={{0,4},{4,0},{8,12},{12,8},{16,20},{20,16},{24,28},{28,24},{1,5},{5... | collective-permute-start | bytes 3538952 | tf_op jit(solution)/shard_map/weights/ppermute | solution.py:64
  9.2 2.0 %collective-permute-done.refs_1_ = bf16[256,768]{1,0:T(8,128)(2,1)S(1)} collective-permute-done((bf16[256,768]{1,0:T(8,128)(2,1)S(1)}, bf16[256,768]{1,0:T(8,128)(2,1)S(1)}, u32[]{:S(2)}, u32[]{:S(2)}) %collective-permute-start) | collective-permute-done | bytes 393248 | tf_op jit(solution)/shard_map/chunk0/ppermute | solution.py:64
  12.2 5.4 %collective-permute-done.3.refs_0_ = bf16[256,768]{1,0:T(8,128)(2,1)S(1)} collective-permute-done((bf16[256,768]{1,0:T(8,128)(2,1)S(1)}, bf16[256,768]{1,0:T(8,128)(2,1)S(1)}, u32[]{:S(2)}, u32[]{:S(2)}) %collective-permute-start.3) | collective-permute-done | bytes 393248 | tf_op jit(solution)/shard_map/rows_near/ppermute | solution.py:69
  22.7 2.7 %collective-permute-start.9 = (bf16[256,384]{1,0:T(8,128)(2,1)S(1)}, bf16[256,384]{1,0:T(8,128)(2,1)S(1)}, u32[]{:S(2)}, u32[]{:S(2)}) collective-permute-start(bf16[256,384]{1,0:T(8,128)(2,1)S(1)} %get-tuple-element.43.refs_6_), channel_id=1, source_target_pairs={{0,16},{4,20},{8,24},{12,28},{16,0},{20,4},{24,8},{28,12},{1,17},{... | collective-permute-start | bytes 589832 | tf_op jit(solution)/shard_map/chunk12/ppermute | solution.py:64
  26.7 1.7 %collective-permute-start.12 = (bf16[512,768]{1,0:T(8,128)(2,1)S(1)}, bf16[512,768]{1,0:T(8,128)(2,1)S(1)}, u32[]{:S(2)}, u32[]{:S(2)}) collective-permute-start(bf16[512,768]{1,0:T(8,128)(2,1)S(1)} %get-tuple-element.44.refs_1_.refs_7_), channel_id=1, source_target_pairs={{0,8},{4,12},{8,0},{12,4},{16,24},{20,28},{24,16},{28,20},{1,9},{5... | collective-permute-start | bytes 2359304 | tf_op jit(solution)/shard_map/chunk12/ppermute | solution.py:64
  29.9 2.8 %collective-permute-done.2.refs_0_ = bf16[256,768]{1,0:T(8,128)(2,1)S(1)} collective-permute-done((bf16[256,768]{1,0:T(8,128)(2,1)S(1)}, bf16[256,768]{1,0:T(8,128)(2,1)S(1)}, u32[]{:S(2)}, u32[]{:S(2)}) %collective-permute-start.2) | collective-permute-done | bytes 393248 | tf_op jit(solution)/shard_map/rows_far/ppermute | solution.py:69
  33.6 1.9 %collective-permute-start.10 = (bf16[256,768]{1,0:T(8,128)(2,1)S(1)}, bf16[256,768]{1,0:T(8,128)(2,1)S(1)}, u32[]{:S(2)}, u32[]{:S(2)}) collective-permute-start(bf16[256,768]{1,0:T(8,128)(2,1)S(1)} %chunk3.5.refs_0_), channel_id=1, source_target_pairs={{0,4},{4,0},{8,12},{12,8},{16,20},{20,16},{24,28},{28,24},{1,5},{5... | collective-permute-start | bytes 1179656 | tf_op jit(solution)/shard_map/chunk3/ppermute | solution.py:64
  36.7 1.6 %chunk3.6.refs_6_.refs_2_.refs_0_ = f32[512,768]{1,0:T(8,128)S(1)} custom-call(bf16[256,768]{1,0:T(8,128)(2,1)S(1)} %collective-permute-done.3.refs_0_, bf16[256,768]{1,0:T(8,128)(2,1)S(1)} %collective-permute-done.4.refs_1_, bf16[256,768]{1,0:T(8,128)(2,1)S(1)} %collective-permute-done.5.refs_2_, bf16[256,768]{1,0:T(8,128)(2,1)S(1)} %collective-permute-done.6.refs_3_, ...), custom_call_target="tpu_custom_call" | custom-call | bytes 1024 | tf_op jit(solution)/shard_map/chunk3/pallas_call | solution.py:49
  38.4 1.8 %chunk3.7 = (bf16[288,768]{1,0:T(8,128)(2,1)S(1)}, f32[8,256]{1,0:T(8,128)S(1)}, bf16[256,768]{1,0:T(8,128)(2,1)}) custom-call(bf16[256,768]{1,0:T(8,128)(2,1)S(1)} %chunk3.5.refs_0_, bf16[256,768]{1,0:T(8,128)(2,1)S(1)} %collective-permute-done.10.refs_1_, bf16[768,768]{1,0:T(8,128)(2,1)S(1)} %get-tuple-element.36.refs_2_, ...), custom_call_target="tpu_custom_call" | custom-call | bytes 1024 | tf_op jit(solution)/shard_map/chunk3/pallas_call | solution.py:49
  41.6 7.1 %collective-permute-done.12.refs_1_ = bf16[512,768]{1,0:T(8,128)(2,1)S(1)} collective-permute-done((bf16[512,768]{1,0:T(8,128)(2,1)S(1)}, bf16[512,768]{1,0:T(8,128)(2,1)S(1)}, u32[]{:S(2)}, u32[]{:S(2)}) %collective-permute-start.12) | collective-permute-done | bytes 786464 | tf_op jit(solution)/shard_map/chunk12/ppermute | solution.py:64
  49.9 14.3 %collective-permute-done.11.refs_1_ = bf16[288,768]{1,0:T(8,128)(2,1)S(1)} collective-permute-done((bf16[288,768]{1,0:T(8,128)(2,1)S(1)}, bf16[288,768]{1,0:T(8,128)(2,1)S(1)}, u32[]{:S(2)}, u32[]{:S(2)}) %collective-permute-start.11) | collective-permute-done | bytes 442400 | tf_op jit(solution)/shard_map/chunk3/ppermute | solution.py:64
  64.4 13.3 %collective-permute-done.13.refs_1_ = bf16[304,384]{1,0:T(8,128)(2,1)S(1)} collective-permute-done((bf16[304,384]{1,0:T(8,128)(2,1)S(1)}, bf16[304,384]{1,0:T(8,128)(2,1)S(1)}, u32[]{:S(2)}, u32[]{:S(2)}) %collective-permute-start.13) | collective-permute-done | bytes 233504 | tf_op jit(solution)/shard_map/sum3/ppermute | solution.py:64
  77.9 2.8 %attention.2.refs_1_ = bf16[1024,128]{1,0:T(8,128)(2,1)S(1)} custom-call(s32[16]{0:T(128)S(1)} %weights.3.refs_7_.refs_0_, f32[1024,128]{1,0:T(8,128)S(1)} %get-tuple-element.56.refs_1_, f32[8,384]{1,0:T(8,128)S(1)} %get-tuple-element.57.refs_2_, f32[256,384]{1,0:T(8,128)S(1)} %get-tuple-element.58.refs_3_, f32[512,384]{1,0:T(8,128)S(1)} %get-tuple-element.59.refs_4_, ...), custom_call_target="tpu_custom_call" | custom-call | bytes 1024 | tf_op jit(solution)/shard_map/attention/pallas_call | solution.py:49
  82.1 4.3 %collective-permute-done.15.refs_2_ = bf16[1024,128]{1,0:T(8,128)(2,1)S(1)} collective-permute-done((bf16[1024,128]{1,0:T(8,128)(2,1)S(1)}, bf16[1024,128]{1,0:T(8,128)(2,1)S(1)}, u32[]{:S(2)}, u32[]{:S(2)}) %collective-permute-start.15) | collective-permute-done | bytes 262176 | tf_op jit(solution)/shard_map/attention/ppermute | solution.py:64
  87.1 3.3 %collective-permute-start.16 = (bf16[256,128]{1,0:T(8,128)(2,1)S(1)}, bf16[256,128]{1,0:T(8,128)(2,1)S(1)}, u32[]{:S(2)}, u32[]{:S(2)}) collective-permute-start(bf16[256,128]{1,0:T(8,128)(2,1)S(1)} %get-tuple-element.62), channel_id=1, source_target_pairs={{2,0},{3,1},{0,2},{1,3},{6,4},{7,5},{4,6},{5,7},{10,8},{11,9},{8,1... | collective-permute-start | bytes 196616 | tf_op jit(solution)/shard_map/attention/ppermute | solution.py:69
  93.5 2.5 %collective-permute-done.18.refs_3_ = bf16[256,128]{1,0:T(8,128)(2,1)S(1)} collective-permute-done((bf16[256,128]{1,0:T(8,128)(2,1)S(1)}, bf16[256,128]{1,0:T(8,128)(2,1)S(1)}, u32[]{:S(2)}, u32[]{:S(2)}) %collective-permute-start.18) | collective-permute-done | bytes 65568 | tf_op jit(solution)/shard_map/attention/ppermute | solution.py:69
  96.7 3.0 %collective-permute-start.21 = (bf16[256,512]{1,0:T(8,128)(2,1)S(1)}, bf16[256,512]{1,0:T(8,128)(2,1)S(1)}, u32[]{:S(2)}, u32[]{:S(2)}) collective-permute-start(bf16[256,512]{1,0:T(8,128)(2,1)S(1)} %out.4.refs_0_), channel_id=1, source_target_pairs={{0,24},{4,28},{8,16},{12,20},{16,8},{20,12},{24,0},{28,4},{1,25},{... | collective-permute-start | bytes 786440 | tf_op jit(solution)/shard_map/out/ppermute | solution.py:64
  99.9 1.5 %collective-permute-start.27 = (bf16[512,768]{1,0:T(8,128)(2,1)S(1)}, bf16[512,768]{1,0:T(8,128)(2,1)S(1)}, u32[]{:S(2)}, u32[]{:S(2)}) collective-permute-start(bf16[512,768]{1,0:T(8,128)(2,1)S(1)} %slice.9), channel_id=1, source_target_pairs={{3,0},{0,1},{1,2},{2,3},{7,4},{4,5},{5,6},{6,7},{11,8},{8,9},{9,10... | collective-permute-start | bytes 2359304 | tf_op jit(solution)/shard_map/out_weight/ppermute | solution.py:69
  101.4 1.8 %collective-permute-done.19.refs_1_ = bf16[256,512]{1,0:T(8,128)(2,1)S(1)} collective-permute-done((bf16[256,512]{1,0:T(8,128)(2,1)S(1)}, bf16[256,512]{1,0:T(8,128)(2,1)S(1)}, u32[]{:S(2)}, u32[]{:S(2)}) %collective-permute-start.19) | collective-permute-done | bytes 262176 | tf_op jit(solution)/shard_map/out/ppermute | solution.py:64
  103.3 3.8 %collective-permute-done.20.refs_2_ = bf16[256,512]{1,0:T(8,128)(2,1)S(1)} collective-permute-done((bf16[256,512]{1,0:T(8,128)(2,1)S(1)}, bf16[256,512]{1,0:T(8,128)(2,1)S(1)}, u32[]{:S(2)}, u32[]{:S(2)}) %collective-permute-start.20) | collective-permute-done | bytes 262176 | tf_op jit(solution)/shard_map/out/ppermute | solution.py:64
  107.0 3.1 %collective-permute-done.21.refs_3_ = bf16[256,512]{1,0:T(8,128)(2,1)S(1)} collective-permute-done((bf16[256,512]{1,0:T(8,128)(2,1)S(1)}, bf16[256,512]{1,0:T(8,128)(2,1)S(1)}, u32[]{:S(2)}, u32[]{:S(2)}) %collective-permute-start.21) | collective-permute-done | bytes 262176 | tf_op jit(solution)/shard_map/out/ppermute | solution.py:64
  110.4 7.7 %collective-permute-start.24 = (bf16[160,2048]{1,0:T(8,128)(2,1)S(1)}, bf16[160,2048]{1,0:T(8,128)(2,1)S(1)}, u32[]{:S(2)}, u32[]{:S(2)}) collective-permute-start(bf16[160,2048]{1,0:T(8,128)(2,1)S(1)} %get-tuple-element.65.refs_0_.refs_1_), channel_id=1, source_target_pairs={{0,4},{4,0},{8,12},{12,8},{16,20},{20,16},{24,28},{28,24},{1,5},{5... | collective-permute-start | bytes 1966088 | tf_op jit(solution)/shard_map/out/ppermute | solution.py:64
  120.4 1.9 %out.7 = bf16[256,768]{1,0:T(8,128)(2,1)} custom-call(f32[256,768]{1,0:T(8,128)S(1)} %out.6.refs_0_, bf16[160,2048]{1,0:T(8,128)(2,1)S(1)} %get-tuple-element.65.refs_0_.refs_1_, bf16[96,2048]{1,0:T(8,128)(2,1)S(1)} %get-tuple-element.66.refs_1_.refs_2_, bf16[160,2048]{1,0:T(8,128)(2,1)S(1)} %collective-permute-done.24.refs_3_, ...), custom_call_target="tpu_custom_call" | custom-call | bytes 1024 | tf_op jit(solution)/shard_map/out/pallas_call | solution.py:49
  (68 shorter events, 26.1 us)
Async XLA Ops:
  3.1 8.1 %collective-permute-start.1 = (bf16[768,768]{1,0:T(8,128)(2,1)S(1)}, bf16[768,768]{1,0:T(8,128)(2,1)S(1)}, u32[]{:S(2)}, u32[]{:S(2)}) collective-permute-start(bf16[768,768]{1,0:T(8,128)(2,1)S(1)} %get-tuple-element.37), channel_id=1, source_target_pairs={{0,4},{4,0},{8,12},{12,8},{16,20},{20,16},{24,28},{28,24},{1,5},{5... | collective-permute-start | bytes 3538952 | tf_op jit(solution)/shard_map/weights/ppermute | solution.py:64
  6.4 14.0 %collective-permute-start.7 = (bf16[768,768]{1,0:T(8,128)(2,1)S(1)}, bf16[768,768]{1,0:T(8,128)(2,1)S(1)}, u32[]{:S(2)}, u32[]{:S(2)}) collective-permute-start(bf16[768,768]{1,0:T(8,128)(2,1)S(1)} %get-tuple-element.40), channel_id=1, source_target_pairs={{0,4},{4,0},{8,12},{12,8},{16,20},{20,16},{24,28},{28,24},{1,5},{5... | collective-permute-start | bytes 3538952 | tf_op jit(solution)/shard_map/weights/ppermute | solution.py:64
  6.9 10.7 %collective-permute-start.3 = (bf16[256,768]{1,0:T(8,128)(2,1)S(1)}, bf16[256,768]{1,0:T(8,128)(2,1)S(1)}, u32[]{:S(2)}, u32[]{:S(2)}) collective-permute-start(bf16[256,768]{1,0:T(8,128)(2,1)S(1)} %copy-done.2), channel_id=1, source_target_pairs={{1,0},{2,1},{3,2},{0,3},{5,4},{6,5},{7,6},{4,7},{9,8},{10,9},{11,1... | collective-permute-start | bytes 1179656 | tf_op jit(solution)/shard_map/rows_near/ppermute | solution.py:69
  7.7 11.6 %collective-permute-start.4 = (bf16[256,768]{1,0:T(8,128)(2,1)S(1)}, bf16[256,768]{1,0:T(8,128)(2,1)S(1)}, u32[]{:S(2)}, u32[]{:S(2)}) collective-permute-start(bf16[256,768]{1,0:T(8,128)(2,1)S(1)} %copy-done.2), channel_id=1, source_target_pairs={{3,0},{0,1},{1,2},{2,3},{7,4},{4,5},{5,6},{6,7},{11,8},{8,9},{9,10... | collective-permute-start | bytes 1179656 | tf_op jit(solution)/shard_map/rows_near/ppermute | solution.py:69
  12.1 10.4 %collective-permute-start.8 = (bf16[256,768]{1,0:T(8,128)(2,1)S(1)}, bf16[256,768]{1,0:T(8,128)(2,1)S(1)}, u32[]{:S(2)}, u32[]{:S(2)}) collective-permute-start(bf16[256,768]{1,0:T(8,128)(2,1)S(1)} %get-tuple-element.42), channel_id=1, source_target_pairs={{0,8},{4,12},{8,0},{12,4},{16,24},{20,28},{24,16},{28,20},{1,9},{5... | collective-permute-start | bytes 1179656 | tf_op jit(solution)/shard_map/chunk0/ppermute | solution.py:64
  17.6 7.7 %collective-permute-start.5 = (bf16[256,768]{1,0:T(8,128)(2,1)S(1)}, bf16[256,768]{1,0:T(8,128)(2,1)S(1)}, u32[]{:S(2)}, u32[]{:S(2)}) collective-permute-start(bf16[256,768]{1,0:T(8,128)(2,1)S(1)} %collective-permute-done.3.refs_0_), channel_id=1, source_target_pairs={{0,4},{4,0},{8,12},{12,8},{16,20},{20,16},{24,28},{28,24},{1,5},{5... | collective-permute-start | bytes 1179656 | tf_op jit(solution)/shard_map/chunk12/ppermute | solution.py:64
  19.2 6.1 %collective-permute-start.6 = (bf16[256,768]{1,0:T(8,128)(2,1)S(1)}, bf16[256,768]{1,0:T(8,128)(2,1)S(1)}, u32[]{:S(2)}, u32[]{:S(2)}) collective-permute-start(bf16[256,768]{1,0:T(8,128)(2,1)S(1)} %collective-permute-done.4.refs_1_), channel_id=1, source_target_pairs={{0,4},{4,0},{8,12},{12,8},{16,20},{20,16},{24,28},{28,24},{1,5},{5... | collective-permute-start | bytes 1179656 | tf_op jit(solution)/shard_map/chunk12/ppermute | solution.py:64
  20.4 12.2 %collective-permute-start.2 = (bf16[256,768]{1,0:T(8,128)(2,1)S(1)}, bf16[256,768]{1,0:T(8,128)(2,1)S(1)}, u32[]{:S(2)}, u32[]{:S(2)}) collective-permute-start(bf16[256,768]{1,0:T(8,128)(2,1)S(1)} %get-tuple-element.38), channel_id=1, source_target_pairs={{2,0},{3,1},{0,2},{1,3},{6,4},{7,5},{4,6},{5,7},{10,8},{11,9},{8,1... | collective-permute-start | bytes 1179656 | tf_op jit(solution)/shard_map/rows_far/ppermute | solution.py:69
  22.7 10.9 %collective-permute-start.9 = (bf16[256,384]{1,0:T(8,128)(2,1)S(1)}, bf16[256,384]{1,0:T(8,128)(2,1)S(1)}, u32[]{:S(2)}, u32[]{:S(2)}) collective-permute-start(bf16[256,384]{1,0:T(8,128)(2,1)S(1)} %get-tuple-element.43.refs_6_), channel_id=1, source_target_pairs={{0,16},{4,20},{8,24},{12,28},{16,0},{20,4},{24,8},{28,12},{1,17},{... | collective-permute-start | bytes 589832 | tf_op jit(solution)/shard_map/chunk12/ppermute | solution.py:64
  26.7 22.0 %collective-permute-start.12 = (bf16[512,768]{1,0:T(8,128)(2,1)S(1)}, bf16[512,768]{1,0:T(8,128)(2,1)S(1)}, u32[]{:S(2)}, u32[]{:S(2)}) collective-permute-start(bf16[512,768]{1,0:T(8,128)(2,1)S(1)} %get-tuple-element.44.refs_1_.refs_7_), channel_id=1, source_target_pairs={{0,8},{4,12},{8,0},{12,4},{16,24},{20,28},{24,16},{28,20},{1,9},{5... | collective-permute-start | bytes 2359304 | tf_op jit(solution)/shard_map/chunk12/ppermute | solution.py:64
  28.4 71.3 %collective-permute-start.22 = (bf16[1024,768]{1,0:T(8,128)(2,1)S(1)}, bf16[1024,768]{1,0:T(8,128)(2,1)S(1)}, u32[]{:S(2)}, u32[]{:S(2)}) collective-permute-start(bf16[1024,768]{1,0:T(8,128)(2,1)S(1)} %copy-done.1), channel_id=1, source_target_pairs={{1,0},{2,1},{3,2},{0,3},{5,4},{6,5},{7,6},{4,7},{9,8},{10,9},{11,1... | collective-permute-start | bytes 4718600 | tf_op jit(solution)/shard_map/out_weight/ppermute | solution.py:69
  29.6 70.3 %collective-permute-start.23 = (bf16[1024,768]{1,0:T(8,128)(2,1)S(1)}, bf16[1024,768]{1,0:T(8,128)(2,1)S(1)}, u32[]{:S(2)}, u32[]{:S(2)}) collective-permute-start(bf16[1024,768]{1,0:T(8,128)(2,1)S(1)} %copy-done.1), channel_id=1, source_target_pairs={{3,0},{0,1},{1,2},{2,3},{7,4},{4,5},{5,6},{6,7},{11,8},{8,9},{9,10... | collective-permute-start | bytes 4718600 | tf_op jit(solution)/shard_map/out_weight/ppermute | solution.py:69
  41.1 23.0 %collective-permute-start.11 = (bf16[288,768]{1,0:T(8,128)(2,1)S(1)}, bf16[288,768]{1,0:T(8,128)(2,1)S(1)}, u32[]{:S(2)}, u32[]{:S(2)}) collective-permute-start(bf16[288,768]{1,0:T(8,128)(2,1)S(1)} %chunk3.9), channel_id=1, source_target_pairs={{0,8},{4,12},{8,0},{12,4},{16,24},{20,28},{24,16},{28,20},{1,9},{5... | collective-permute-start | bytes 1327112 | tf_op jit(solution)/shard_map/chunk3/ppermute | solution.py:64
  48.9 29.1 %collective-permute-start.14 = (bf16[512,384]{1,0:T(8,128)(2,1)S(1)}, bf16[512,384]{1,0:T(8,128)(2,1)S(1)}, u32[]{:S(2)}, u32[]{:S(2)}) collective-permute-start(bf16[512,384]{1,0:T(8,128)(2,1)S(1)} %get-tuple-element.51.refs_3_), channel_id=1, source_target_pairs={{0,16},{4,20},{8,24},{12,28},{16,0},{20,4},{24,8},{28,12},{1,17},{... | collective-permute-start | bytes 1179656 | tf_op jit(solution)/shard_map/sum12/ppermute | solution.py:64
  64.3 13.4 %collective-permute-start.13 = (bf16[304,384]{1,0:T(8,128)(2,1)S(1)}, bf16[304,384]{1,0:T(8,128)(2,1)S(1)}, u32[]{:S(2)}, u32[]{:S(2)}) collective-permute-start(bf16[304,384]{1,0:T(8,128)(2,1)S(1)} %get-tuple-element.53), channel_id=1, source_target_pairs={{0,16},{4,20},{8,24},{12,28},{16,0},{20,4},{24,8},{28,12},{1,17},{... | collective-permute-start | bytes 700424 | tf_op jit(solution)/shard_map/sum3/ppermute | solution.py:64
  80.7 5.7 %collective-permute-start.15 = (bf16[1024,128]{1,0:T(8,128)(2,1)S(1)}, bf16[1024,128]{1,0:T(8,128)(2,1)S(1)}, u32[]{:S(2)}, u32[]{:S(2)}) collective-permute-start(bf16[1024,128]{1,0:T(8,128)(2,1)S(1)} %attention.2.refs_1_), channel_id=1, source_target_pairs={{0,32},{32,0},{64,96},{96,64},{128,160},{160,128},{192,224},{224,1... | collective-permute-start | bytes 786440 | tf_op jit(solution)/shard_map/attention/ppermute | solution.py:64
  87.1 5.0 %collective-permute-start.16 = (bf16[256,128]{1,0:T(8,128)(2,1)S(1)}, bf16[256,128]{1,0:T(8,128)(2,1)S(1)}, u32[]{:S(2)}, u32[]{:S(2)}) collective-permute-start(bf16[256,128]{1,0:T(8,128)(2,1)S(1)} %get-tuple-element.62), channel_id=1, source_target_pairs={{2,0},{3,1},{0,2},{1,3},{6,4},{7,5},{4,6},{5,7},{10,8},{11,9},{8,1... | collective-permute-start | bytes 196616 | tf_op jit(solution)/shard_map/attention/ppermute | solution.py:69
  91.0 5.0 %collective-permute-start.18 = (bf16[256,128]{1,0:T(8,128)(2,1)S(1)}, bf16[256,128]{1,0:T(8,128)(2,1)S(1)}, u32[]{:S(2)}, u32[]{:S(2)}) collective-permute-start(bf16[256,128]{1,0:T(8,128)(2,1)S(1)} %get-tuple-element.64), channel_id=1, source_target_pairs={{3,0},{0,1},{1,2},{2,3},{7,4},{4,5},{5,6},{6,7},{11,8},{8,9},{9,10... | collective-permute-start | bytes 196616 | tf_op jit(solution)/shard_map/attention/ppermute | solution.py:69
  96.1 7.2 %collective-permute-start.19 = (bf16[256,512]{1,0:T(8,128)(2,1)S(1)}, bf16[256,512]{1,0:T(8,128)(2,1)S(1)}, u32[]{:S(2)}, u32[]{:S(2)}) collective-permute-start(bf16[256,512]{1,0:T(8,128)(2,1)S(1)} %out.4.refs_0_), channel_id=1, source_target_pairs={{0,16},{4,20},{8,24},{12,28},{16,0},{20,4},{24,8},{28,12},{1,17},{... | collective-permute-start | bytes 786440 | tf_op jit(solution)/shard_map/out/ppermute | solution.py:64
  96.2 10.9 %collective-permute-start.20 = (bf16[256,512]{1,0:T(8,128)(2,1)S(1)}, bf16[256,512]{1,0:T(8,128)(2,1)S(1)}, u32[]{:S(2)}, u32[]{:S(2)}) collective-permute-start(bf16[256,512]{1,0:T(8,128)(2,1)S(1)} %out.4.refs_0_), channel_id=1, source_target_pairs={{0,8},{4,12},{8,0},{12,4},{16,24},{20,28},{24,16},{28,20},{1,9},{5... | collective-permute-start | bytes 786440 | tf_op jit(solution)/shard_map/out/ppermute | solution.py:64
  96.7 13.4 %collective-permute-start.21 = (bf16[256,512]{1,0:T(8,128)(2,1)S(1)}, bf16[256,512]{1,0:T(8,128)(2,1)S(1)}, u32[]{:S(2)}, u32[]{:S(2)}) collective-permute-start(bf16[256,512]{1,0:T(8,128)(2,1)S(1)} %out.4.refs_0_), channel_id=1, source_target_pairs={{0,24},{4,28},{8,16},{12,20},{16,8},{20,12},{24,0},{28,4},{1,25},{... | collective-permute-start | bytes 786440 | tf_op jit(solution)/shard_map/out/ppermute | solution.py:64
  99.8 19.3 %collective-permute-start.26 = (bf16[512,768]{1,0:T(8,128)(2,1)S(1)}, bf16[512,768]{1,0:T(8,128)(2,1)S(1)}, u32[]{:S(2)}, u32[]{:S(2)}) collective-permute-start(bf16[512,768]{1,0:T(8,128)(2,1)S(1)} %slice.8), channel_id=1, source_target_pairs={{1,0},{2,1},{3,2},{0,3},{5,4},{6,5},{7,6},{4,7},{9,8},{10,9},{11,1... | collective-permute-start | bytes 2359304 | tf_op jit(solution)/shard_map/out_weight/ppermute | solution.py:69
  99.9 19.1 %collective-permute-start.27 = (bf16[512,768]{1,0:T(8,128)(2,1)S(1)}, bf16[512,768]{1,0:T(8,128)(2,1)S(1)}, u32[]{:S(2)}, u32[]{:S(2)}) collective-permute-start(bf16[512,768]{1,0:T(8,128)(2,1)S(1)} %slice.9), channel_id=1, source_target_pairs={{3,0},{0,1},{1,2},{2,3},{7,4},{4,5},{5,6},{6,7},{11,8},{8,9},{9,10... | collective-permute-start | bytes 2359304 | tf_op jit(solution)/shard_map/out_weight/ppermute | solution.py:69
  110.4 10.0 %collective-permute-start.24 = (bf16[160,2048]{1,0:T(8,128)(2,1)S(1)}, bf16[160,2048]{1,0:T(8,128)(2,1)S(1)}, u32[]{:S(2)}, u32[]{:S(2)}) collective-permute-start(bf16[160,2048]{1,0:T(8,128)(2,1)S(1)} %get-tuple-element.65.refs_0_.refs_1_), channel_id=1, source_target_pairs={{0,4},{4,0},{8,12},{12,8},{16,20},{20,16},{24,28},{28,24},{1,5},{5... | collective-permute-start | bytes 1966088 | tf_op jit(solution)/shard_map/out/ppermute | solution.py:64
  (10 other events, 53.7 us)

commit v6 on v5

--- a/solution.py
+++ b/solution.py
@@ -19,7 +19,7 @@
 FIRST = 160
 EXTRA = 32
 TERMS = 24
-SENT = (2, 1, 3)
+SENT = (3, 1, 2)
 F32 = jnp.float32
 BF16 = jnp.bfloat16
 

time: 123 us -> 125 us (1.016)
  waiting for transfers between devices: 65.4 us -> 69.9 us
  starting transfers between devices: 36.1 us -> 34.6 us
    ppermute x18, waiting for transfers between devices: 52.3 us -> 56.9 us  [swap(): return lax.ppermute(block, axis, [(i, i ^ bits) for i in range(count)])]
    ppermute x18, starting transfers between devices: 26.7 us -> 25.2 us  [swap(): return lax.ppermute(block, axis, [(i, i ^ bits) for i in range(count)])]
  transfers between devices with their start and end apart: 28 -> 28, of which waited for: 17 -> 17; matrix products, arithmetic and copies ran while one was open for 0% -> 0% of each run, Pallas kernels for 13% -> 12%
where the time goes in v6:
time: 125 us
  waiting for transfers between devices  69.9 us (56%)
  starting transfers between devices  34.6 us (28%)
  Pallas kernels  18.2 us (15%)
  local copies, waits for them, and re-layouts  2.47 us (2%)
    ppermute x18, waiting for transfers between devices, swap(): return lax.ppermute(block, axis, [(i, i ^ bits) for i in range(count)])  56.9 us
    ppermute x18, starting transfers between devices, swap(): return lax.ppermute(block, axis, [(i, i ^ bits) for i in range(count)])  25.2 us
    pallas_call x22, Pallas kernels, call(): return lambda *args: made(*args, *after)  18.2 us
    ppermute x10, waiting for transfers between devices, shift(): lax.ppermute(block, axis, [((i + step) % count, i) for i in range(count)])  13.1 us
    ppermute x10, starting transfers between devices, shift(): lax.ppermute(block, axis, [((i + step) % count, i) for i in range(count)])  9.36 us
  transfers between devices with their start and end apart: 28, of which 17 were waited for; matrix products, arithmetic and copies ran while one was open for 0% of the time, Pallas kernels for 12%

profile of v6, /device:TPU:1, one launch (start us, length us, event | category | flops | bytes accessed | tf_op | source)
XLA Modules:
  0.0 125.4 jit_solution(9057019685290385439)
XLA Ops:
  0.0 2.3 %copy-done = bf16[768,3,1024]{2,0,1:T(8,128)(2,1)S(1)} copy-done((bf16[768,3,1024]{2,0,1:T(8,128)(2,1)S(1)}, bf16[768,3,1024]{2,0,1:T(8,128)(2,1)}, u32[]{:S(2)}) %copy-start) | copy-done | bytes 4718616
  3.1 3.3 %collective-permute-start.1 = (bf16[768,768]{1,0:T(8,128)(2,1)S(1)}, bf16[768,768]{1,0:T(8,128)(2,1)S(1)}, u32[]{:S(2)}, u32[]{:S(2)}) collective-permute-start(bf16[768,768]{1,0:T(8,128)(2,1)S(1)} %get-tuple-element.37), channel_id=1, source_target_pairs={{0,4},{4,0},{8,12},{12,8},{16,20},{20,16},{24,28},{28,24},{1,5},{5... | collective-permute-start | bytes 3538952 | tf_op jit(solution)/shard_map/weights/ppermute | solution.py:64
  9.2 2.0 %collective-permute-done.refs_1_ = bf16[256,768]{1,0:T(8,128)(2,1)S(1)} collective-permute-done((bf16[256,768]{1,0:T(8,128)(2,1)S(1)}, bf16[256,768]{1,0:T(8,128)(2,1)S(1)}, u32[]{:S(2)}, u32[]{:S(2)}) %collective-permute-start) | collective-permute-done | bytes 393248 | tf_op jit(solution)/shard_map/chunk0/ppermute | solution.py:64
  12.2 5.4 %collective-permute-done.3.refs_0_ = bf16[256,768]{1,0:T(8,128)(2,1)S(1)} collective-permute-done((bf16[256,768]{1,0:T(8,128)(2,1)S(1)}, bf16[256,768]{1,0:T(8,128)(2,1)S(1)}, u32[]{:S(2)}, u32[]{:S(2)}) %collective-permute-start.3) | collective-permute-done | bytes 393248 | tf_op jit(solution)/shard_map/rows_near/ppermute | solution.py:69
  22.7 2.7 %collective-permute-start.9 = (bf16[256,384]{1,0:T(8,128)(2,1)S(1)}, bf16[256,384]{1,0:T(8,128)(2,1)S(1)}, u32[]{:S(2)}, u32[]{:S(2)}) collective-permute-start(bf16[256,384]{1,0:T(8,128)(2,1)S(1)} %get-tuple-element.43.refs_6_), channel_id=1, source_target_pairs={{0,16},{4,20},{8,24},{12,28},{16,0},{20,4},{24,8},{28,12},{1,17},{... | collective-permute-start | bytes 589832 | tf_op jit(solution)/shard_map/chunk12/ppermute | solution.py:64
  26.7 1.7 %collective-permute-start.12 = (bf16[512,768]{1,0:T(8,128)(2,1)S(1)}, bf16[512,768]{1,0:T(8,128)(2,1)S(1)}, u32[]{:S(2)}, u32[]{:S(2)}) collective-permute-start(bf16[512,768]{1,0:T(8,128)(2,1)S(1)} %get-tuple-element.44.refs_1_.refs_7_), channel_id=1, source_target_pairs={{0,8},{4,12},{8,0},{12,4},{16,24},{20,28},{24,16},{28,20},{1,9},{5... | collective-permute-start | bytes 2359304 | tf_op jit(solution)/shard_map/chunk12/ppermute | solution.py:64
  29.9 2.8 %collective-permute-done.2.refs_0_ = bf16[256,768]{1,0:T(8,128)(2,1)S(1)} collective-permute-done((bf16[256,768]{1,0:T(8,128)(2,1)S(1)}, bf16[256,768]{1,0:T(8,128)(2,1)S(1)}, u32[]{:S(2)}, u32[]{:S(2)}) %collective-permute-start.2) | collective-permute-done | bytes 393248 | tf_op jit(solution)/shard_map/rows_far/ppermute | solution.py:69
  33.6 1.9 %collective-permute-start.10 = (bf16[256,768]{1,0:T(8,128)(2,1)S(1)}, bf16[256,768]{1,0:T(8,128)(2,1)S(1)}, u32[]{:S(2)}, u32[]{:S(2)}) collective-permute-start(bf16[256,768]{1,0:T(8,128)(2,1)S(1)} %chunk3.5.refs_0_), channel_id=1, source_target_pairs={{0,4},{4,0},{8,12},{12,8},{16,20},{20,16},{24,28},{28,24},{1,5},{5... | collective-permute-start | bytes 1179656 | tf_op jit(solution)/shard_map/chunk3/ppermute | solution.py:64
  36.7 1.6 %chunk3.6.refs_6_.refs_2_.refs_0_ = f32[512,768]{1,0:T(8,128)S(1)} custom-call(bf16[256,768]{1,0:T(8,128)(2,1)S(1)} %collective-permute-done.3.refs_0_, bf16[256,768]{1,0:T(8,128)(2,1)S(1)} %collective-permute-done.4.refs_1_, bf16[256,768]{1,0:T(8,128)(2,1)S(1)} %collective-permute-done.5.refs_2_, bf16[256,768]{1,0:T(8,128)(2,1)S(1)} %collective-permute-done.6.refs_3_, ...), custom_call_target="tpu_custom_call" | custom-call | bytes 1024 | tf_op jit(solution)/shard_map/chunk3/pallas_call | solution.py:49
  38.4 1.8 %chunk3.7 = (bf16[288,768]{1,0:T(8,128)(2,1)S(1)}, f32[8,256]{1,0:T(8,128)S(1)}, bf16[256,768]{1,0:T(8,128)(2,1)}) custom-call(bf16[256,768]{1,0:T(8,128)(2,1)S(1)} %chunk3.5.refs_0_, bf16[256,768]{1,0:T(8,128)(2,1)S(1)} %collective-permute-done.10.refs_1_, bf16[768,768]{1,0:T(8,128)(2,1)S(1)} %get-tuple-element.36.refs_2_, ...), custom_call_target="tpu_custom_call" | custom-call | bytes 1024 | tf_op jit(solution)/shard_map/chunk3/pallas_call | solution.py:49
  41.6 7.1 %collective-permute-done.12.refs_1_ = bf16[512,768]{1,0:T(8,128)(2,1)S(1)} collective-permute-done((bf16[512,768]{1,0:T(8,128)(2,1)S(1)}, bf16[512,768]{1,0:T(8,128)(2,1)S(1)}, u32[]{:S(2)}, u32[]{:S(2)}) %collective-permute-start.12) | collective-permute-done | bytes 786464 | tf_op jit(solution)/shard_map/chunk12/ppermute | solution.py:64
  49.9 14.3 %collective-permute-done.11.refs_1_ = bf16[288,768]{1,0:T(8,128)(2,1)S(1)} collective-permute-done((bf16[288,768]{1,0:T(8,128)(2,1)S(1)}, bf16[288,768]{1,0:T(8,128)(2,1)S(1)}, u32[]{:S(2)}, u32[]{:S(2)}) %collective-permute-start.11) | collective-permute-done | bytes 442400 | tf_op jit(solution)/shard_map/chunk3/ppermute | solution.py:64
  64.4 13.3 %collective-permute-done.13.refs_1_ = bf16[304,384]{1,0:T(8,128)(2,1)S(1)} collective-permute-done((bf16[304,384]{1,0:T(8,128)(2,1)S(1)}, bf16[304,384]{1,0:T(8,128)(2,1)S(1)}, u32[]{:S(2)}, u32[]{:S(2)}) %collective-permute-start.13) | collective-permute-done | bytes 233504 | tf_op jit(solution)/shard_map/sum3/ppermute | solution.py:64
  77.9 2.8 %attention.2.refs_1_ = bf16[1024,128]{1,0:T(8,128)(2,1)S(1)} custom-call(s32[16]{0:T(128)S(1)} %weights.3.refs_7_.refs_0_, f32[1024,128]{1,0:T(8,128)S(1)} %get-tuple-element.56.refs_1_, f32[8,384]{1,0:T(8,128)S(1)} %get-tuple-element.57.refs_2_, f32[256,384]{1,0:T(8,128)S(1)} %get-tuple-element.58.refs_3_, f32[512,384]{1,0:T(8,128)S(1)} %get-tuple-element.59.refs_4_, ...), custom_call_target="tpu_custom_call" | custom-call | bytes 1024 | tf_op jit(solution)/shard_map/attention/pallas_call | solution.py:49
  82.1 4.3 %collective-permute-done.15.refs_2_ = bf16[1024,128]{1,0:T(8,128)(2,1)S(1)} collective-permute-done((bf16[1024,128]{1,0:T(8,128)(2,1)S(1)}, bf16[1024,128]{1,0:T(8,128)(2,1)S(1)}, u32[]{:S(2)}, u32[]{:S(2)}) %collective-permute-start.15) | collective-permute-done | bytes 262176 | tf_op jit(solution)/shard_map/attention/ppermute | solution.py:64
  87.1 3.3 %collective-permute-start.16 = (bf16[256,128]{1,0:T(8,128)(2,1)S(1)}, bf16[256,128]{1,0:T(8,128)(2,1)S(1)}, u32[]{:S(2)}, u32[]{:S(2)}) collective-permute-start(bf16[256,128]{1,0:T(8,128)(2,1)S(1)} %get-tuple-element.62), channel_id=1, source_target_pairs={{2,0},{3,1},{0,2},{1,3},{6,4},{7,5},{4,6},{5,7},{10,8},{11,9},{8,1... | collective-permute-start | bytes 196616 | tf_op jit(solution)/shard_map/attention/ppermute | solution.py:69
  93.5 2.5 %collective-permute-done.18.refs_3_ = bf16[256,128]{1,0:T(8,128)(2,1)S(1)} collective-permute-done((bf16[256,128]{1,0:T(8,128)(2,1)S(1)}, bf16[256,128]{1,0:T(8,128)(2,1)S(1)}, u32[]{:S(2)}, u32[]{:S(2)}) %collective-permute-start.18) | collective-permute-done | bytes 65568 | tf_op jit(solution)/shard_map/attention/ppermute | solution.py:69
  96.4 3.3 %collective-permute-start.21 = (bf16[256,512]{1,0:T(8,128)(2,1)S(1)}, bf16[256,512]{1,0:T(8,128)(2,1)S(1)}, u32[]{:S(2)}, u32[]{:S(2)}) collective-permute-start(bf16[256,512]{1,0:T(8,128)(2,1)S(1)} %out.4.refs_0_), channel_id=1, source_target_pairs={{0,16},{4,20},{8,24},{12,28},{16,0},{20,4},{24,8},{28,12},{1,17},{... | collective-permute-start | bytes 786440 | tf_op jit(solution)/shard_map/out/ppermute | solution.py:64
  99.9 1.5 %collective-permute-start.27 = (bf16[512,768]{1,0:T(8,128)(2,1)S(1)}, bf16[512,768]{1,0:T(8,128)(2,1)S(1)}, u32[]{:S(2)}, u32[]{:S(2)}) collective-permute-start(bf16[512,768]{1,0:T(8,128)(2,1)S(1)} %slice.9), channel_id=1, source_target_pairs={{3,0},{0,1},{1,2},{2,3},{7,4},{4,5},{5,6},{6,7},{11,8},{8,9},{9,10... | collective-permute-start | bytes 2359304 | tf_op jit(solution)/shard_map/out_weight/ppermute | solution.py:69
  101.4 1.9 %collective-permute-done.19.refs_1_ = bf16[256,512]{1,0:T(8,128)(2,1)S(1)} collective-permute-done((bf16[256,512]{1,0:T(8,128)(2,1)S(1)}, bf16[256,512]{1,0:T(8,128)(2,1)S(1)}, u32[]{:S(2)}, u32[]{:S(2)}) %collective-permute-start.19) | collective-permute-done | bytes 262176 | tf_op jit(solution)/shard_map/out/ppermute | solution.py:64
  103.4 5.6 %collective-permute-done.20.refs_2_ = bf16[256,512]{1,0:T(8,128)(2,1)S(1)} collective-permute-done((bf16[256,512]{1,0:T(8,128)(2,1)S(1)}, bf16[256,512]{1,0:T(8,128)(2,1)S(1)}, u32[]{:S(2)}, u32[]{:S(2)}) %collective-permute-start.20) | collective-permute-done | bytes 262176 | tf_op jit(solution)/shard_map/out/ppermute | solution.py:64
  109.0 5.7 %collective-permute-done.21.refs_3_ = bf16[256,512]{1,0:T(8,128)(2,1)S(1)} collective-permute-done((bf16[256,512]{1,0:T(8,128)(2,1)S(1)}, bf16[256,512]{1,0:T(8,128)(2,1)S(1)}, u32[]{:S(2)}, u32[]{:S(2)}) %collective-permute-start.21) | collective-permute-done | bytes 262176 | tf_op jit(solution)/shard_map/out/ppermute | solution.py:64
  115.0 6.2 %collective-permute-start.24 = (bf16[160,2048]{1,0:T(8,128)(2,1)S(1)}, bf16[160,2048]{1,0:T(8,128)(2,1)S(1)}, u32[]{:S(2)}, u32[]{:S(2)}) collective-permute-start(bf16[160,2048]{1,0:T(8,128)(2,1)S(1)} %get-tuple-element.65.refs_0_.refs_1_), channel_id=1, source_target_pairs={{0,4},{4,0},{8,12},{12,8},{16,20},{20,16},{24,28},{28,24},{1,5},{5... | collective-permute-start | bytes 1966088 | tf_op jit(solution)/shard_map/out/ppermute | solution.py:64
  123.4 1.9 %out.7 = bf16[256,768]{1,0:T(8,128)(2,1)} custom-call(f32[256,768]{1,0:T(8,128)S(1)} %out.6.refs_0_, bf16[160,2048]{1,0:T(8,128)(2,1)S(1)} %get-tuple-element.65.refs_0_.refs_1_, bf16[96,2048]{1,0:T(8,128)(2,1)S(1)} %get-tuple-element.66.refs_1_.refs_2_, bf16[160,2048]{1,0:T(8,128)(2,1)S(1)} %collective-permute-done.24.refs_3_, ...), custom_call_target="tpu_custom_call" | custom-call | bytes 1024 | tf_op jit(solution)/shard_map/out/pallas_call | solution.py:49
  (68 shorter events, 25.8 us)
Async XLA Ops:
  3.1 8.1 %collective-permute-start.1 = (bf16[768,768]{1,0:T(8,128)(2,1)S(1)}, bf16[768,768]{1,0:T(8,128)(2,1)S(1)}, u32[]{:S(2)}, u32[]{:S(2)}) collective-permute-start(bf16[768,768]{1,0:T(8,128)(2,1)S(1)} %get-tuple-element.37), channel_id=1, source_target_pairs={{0,4},{4,0},{8,12},{12,8},{16,20},{20,16},{24,28},{28,24},{1,5},{5... | collective-permute-start | bytes 3538952 | tf_op jit(solution)/shard_map/weights/ppermute | solution.py:64
  6.4 14.0 %collective-permute-start.7 = (bf16[768,768]{1,0:T(8,128)(2,1)S(1)}, bf16[768,768]{1,0:T(8,128)(2,1)S(1)}, u32[]{:S(2)}, u32[]{:S(2)}) collective-permute-start(bf16[768,768]{1,0:T(8,128)(2,1)S(1)} %get-tuple-element.40), channel_id=1, source_target_pairs={{0,4},{4,0},{8,12},{12,8},{16,20},{20,16},{24,28},{28,24},{1,5},{5... | collective-permute-start | bytes 3538952 | tf_op jit(solution)/shard_map/weights/ppermute | solution.py:64
  6.9 10.7 %collective-permute-start.3 = (bf16[256,768]{1,0:T(8,128)(2,1)S(1)}, bf16[256,768]{1,0:T(8,128)(2,1)S(1)}, u32[]{:S(2)}, u32[]{:S(2)}) collective-permute-start(bf16[256,768]{1,0:T(8,128)(2,1)S(1)} %copy-done.2), channel_id=1, source_target_pairs={{1,0},{2,1},{3,2},{0,3},{5,4},{6,5},{7,6},{4,7},{9,8},{10,9},{11,1... | collective-permute-start | bytes 1179656 | tf_op jit(solution)/shard_map/rows_near/ppermute | solution.py:69
  7.7 11.6 %collective-permute-start.4 = (bf16[256,768]{1,0:T(8,128)(2,1)S(1)}, bf16[256,768]{1,0:T(8,128)(2,1)S(1)}, u32[]{:S(2)}, u32[]{:S(2)}) collective-permute-start(bf16[256,768]{1,0:T(8,128)(2,1)S(1)} %copy-done.2), channel_id=1, source_target_pairs={{3,0},{0,1},{1,2},{2,3},{7,4},{4,5},{5,6},{6,7},{11,8},{8,9},{9,10... | collective-permute-start | bytes 1179656 | tf_op jit(solution)/shard_map/rows_near/ppermute | solution.py:69
  12.1 10.4 %collective-permute-start.8 = (bf16[256,768]{1,0:T(8,128)(2,1)S(1)}, bf16[256,768]{1,0:T(8,128)(2,1)S(1)}, u32[]{:S(2)}, u32[]{:S(2)}) collective-permute-start(bf16[256,768]{1,0:T(8,128)(2,1)S(1)} %get-tuple-element.42), channel_id=1, source_target_pairs={{0,8},{4,12},{8,0},{12,4},{16,24},{20,28},{24,16},{28,20},{1,9},{5... | collective-permute-start | bytes 1179656 | tf_op jit(solution)/shard_map/chunk0/ppermute | solution.py:64
  17.6 7.7 %collective-permute-start.5 = (bf16[256,768]{1,0:T(8,128)(2,1)S(1)}, bf16[256,768]{1,0:T(8,128)(2,1)S(1)}, u32[]{:S(2)}, u32[]{:S(2)}) collective-permute-start(bf16[256,768]{1,0:T(8,128)(2,1)S(1)} %collective-permute-done.3.refs_0_), channel_id=1, source_target_pairs={{0,4},{4,0},{8,12},{12,8},{16,20},{20,16},{24,28},{28,24},{1,5},{5... | collective-permute-start | bytes 1179656 | tf_op jit(solution)/shard_map/chunk12/ppermute | solution.py:64
  19.2 6.1 %collective-permute-start.6 = (bf16[256,768]{1,0:T(8,128)(2,1)S(1)}, bf16[256,768]{1,0:T(8,128)(2,1)S(1)}, u32[]{:S(2)}, u32[]{:S(2)}) collective-permute-start(bf16[256,768]{1,0:T(8,128)(2,1)S(1)} %collective-permute-done.4.refs_1_), channel_id=1, source_target_pairs={{0,4},{4,0},{8,12},{12,8},{16,20},{20,16},{24,28},{28,24},{1,5},{5... | collective-permute-start | bytes 1179656 | tf_op jit(solution)/shard_map/chunk12/ppermute | solution.py:64
  20.4 12.2 %collective-permute-start.2 = (bf16[256,768]{1,0:T(8,128)(2,1)S(1)}, bf16[256,768]{1,0:T(8,128)(2,1)S(1)}, u32[]{:S(2)}, u32[]{:S(2)}) collective-permute-start(bf16[256,768]{1,0:T(8,128)(2,1)S(1)} %get-tuple-element.38), channel_id=1, source_target_pairs={{2,0},{3,1},{0,2},{1,3},{6,4},{7,5},{4,6},{5,7},{10,8},{11,9},{8,1... | collective-permute-start | bytes 1179656 | tf_op jit(solution)/shard_map/rows_far/ppermute | solution.py:69
  22.7 10.9 %collective-permute-start.9 = (bf16[256,384]{1,0:T(8,128)(2,1)S(1)}, bf16[256,384]{1,0:T(8,128)(2,1)S(1)}, u32[]{:S(2)}, u32[]{:S(2)}) collective-permute-start(bf16[256,384]{1,0:T(8,128)(2,1)S(1)} %get-tuple-element.43.refs_6_), channel_id=1, source_target_pairs={{0,16},{4,20},{8,24},{12,28},{16,0},{20,4},{24,8},{28,12},{1,17},{... | collective-permute-start | bytes 589832 | tf_op jit(solution)/shard_map/chunk12/ppermute | solution.py:64
  26.7 22.0 %collective-permute-start.12 = (bf16[512,768]{1,0:T(8,128)(2,1)S(1)}, bf16[512,768]{1,0:T(8,128)(2,1)S(1)}, u32[]{:S(2)}, u32[]{:S(2)}) collective-permute-start(bf16[512,768]{1,0:T(8,128)(2,1)S(1)} %get-tuple-element.44.refs_1_.refs_7_), channel_id=1, source_target_pairs={{0,8},{4,12},{8,0},{12,4},{16,24},{20,28},{24,16},{28,20},{1,9},{5... | collective-permute-start | bytes 2359304 | tf_op jit(solution)/shard_map/chunk12/ppermute | solution.py:64
  28.4 71.3 %collective-permute-start.22 = (bf16[1024,768]{1,0:T(8,128)(2,1)S(1)}, bf16[1024,768]{1,0:T(8,128)(2,1)S(1)}, u32[]{:S(2)}, u32[]{:S(2)}) collective-permute-start(bf16[1024,768]{1,0:T(8,128)(2,1)S(1)} %copy-done.1), channel_id=1, source_target_pairs={{1,0},{2,1},{3,2},{0,3},{5,4},{6,5},{7,6},{4,7},{9,8},{10,9},{11,1... | collective-permute-start | bytes 4718600 | tf_op jit(solution)/shard_map/out_weight/ppermute | solution.py:69
  29.6 70.3 %collective-permute-start.23 = (bf16[1024,768]{1,0:T(8,128)(2,1)S(1)}, bf16[1024,768]{1,0:T(8,128)(2,1)S(1)}, u32[]{:S(2)}, u32[]{:S(2)}) collective-permute-start(bf16[1024,768]{1,0:T(8,128)(2,1)S(1)} %copy-done.1), channel_id=1, source_target_pairs={{3,0},{0,1},{1,2},{2,3},{7,4},{4,5},{5,6},{6,7},{11,8},{8,9},{9,10... | collective-permute-start | bytes 4718600 | tf_op jit(solution)/shard_map/out_weight/ppermute | solution.py:69
  41.1 23.0 %collective-permute-start.11 = (bf16[288,768]{1,0:T(8,128)(2,1)S(1)}, bf16[288,768]{1,0:T(8,128)(2,1)S(1)}, u32[]{:S(2)}, u32[]{:S(2)}) collective-permute-start(bf16[288,768]{1,0:T(8,128)(2,1)S(1)} %chunk3.9), channel_id=1, source_target_pairs={{0,8},{4,12},{8,0},{12,4},{16,24},{20,28},{24,16},{28,20},{1,9},{5... | collective-permute-start | bytes 1327112 | tf_op jit(solution)/shard_map/chunk3/ppermute | solution.py:64
  48.9 29.1 %collective-permute-start.14 = (bf16[512,384]{1,0:T(8,128)(2,1)S(1)}, bf16[512,384]{1,0:T(8,128)(2,1)S(1)}, u32[]{:S(2)}, u32[]{:S(2)}) collective-permute-start(bf16[512,384]{1,0:T(8,128)(2,1)S(1)} %get-tuple-element.51.refs_3_), channel_id=1, source_target_pairs={{0,16},{4,20},{8,24},{12,28},{16,0},{20,4},{24,8},{28,12},{1,17},{... | collective-permute-start | bytes 1179656 | tf_op jit(solution)/shard_map/sum12/ppermute | solution.py:64
  64.3 13.4 %collective-permute-start.13 = (bf16[304,384]{1,0:T(8,128)(2,1)S(1)}, bf16[304,384]{1,0:T(8,128)(2,1)S(1)}, u32[]{:S(2)}, u32[]{:S(2)}) collective-permute-start(bf16[304,384]{1,0:T(8,128)(2,1)S(1)} %get-tuple-element.53), channel_id=1, source_target_pairs={{0,16},{4,20},{8,24},{12,28},{16,0},{20,4},{24,8},{28,12},{1,17},{... | collective-permute-start | bytes 700424 | tf_op jit(solution)/shard_map/sum3/ppermute | solution.py:64
  80.7 5.7 %collective-permute-start.15 = (bf16[1024,128]{1,0:T(8,128)(2,1)S(1)}, bf16[1024,128]{1,0:T(8,128)(2,1)S(1)}, u32[]{:S(2)}, u32[]{:S(2)}) collective-permute-start(bf16[1024,128]{1,0:T(8,128)(2,1)S(1)} %attention.2.refs_1_), channel_id=1, source_target_pairs={{0,32},{32,0},{64,96},{96,64},{128,160},{160,128},{192,224},{224,1... | collective-permute-start | bytes 786440 | tf_op jit(solution)/shard_map/attention/ppermute | solution.py:64
  87.1 5.0 %collective-permute-start.16 = (bf16[256,128]{1,0:T(8,128)(2,1)S(1)}, bf16[256,128]{1,0:T(8,128)(2,1)S(1)}, u32[]{:S(2)}, u32[]{:S(2)}) collective-permute-start(bf16[256,128]{1,0:T(8,128)(2,1)S(1)} %get-tuple-element.62), channel_id=1, source_target_pairs={{2,0},{3,1},{0,2},{1,3},{6,4},{7,5},{4,6},{5,7},{10,8},{11,9},{8,1... | collective-permute-start | bytes 196616 | tf_op jit(solution)/shard_map/attention/ppermute | solution.py:69
  91.0 5.0 %collective-permute-start.18 = (bf16[256,128]{1,0:T(8,128)(2,1)S(1)}, bf16[256,128]{1,0:T(8,128)(2,1)S(1)}, u32[]{:S(2)}, u32[]{:S(2)}) collective-permute-start(bf16[256,128]{1,0:T(8,128)(2,1)S(1)} %get-tuple-element.64), channel_id=1, source_target_pairs={{3,0},{0,1},{1,2},{2,3},{7,4},{4,5},{5,6},{6,7},{11,8},{8,9},{9,10... | collective-permute-start | bytes 196616 | tf_op jit(solution)/shard_map/attention/ppermute | solution.py:69
  96.1 7.3 %collective-permute-start.19 = (bf16[256,512]{1,0:T(8,128)(2,1)S(1)}, bf16[256,512]{1,0:T(8,128)(2,1)S(1)}, u32[]{:S(2)}, u32[]{:S(2)}) collective-permute-start(bf16[256,512]{1,0:T(8,128)(2,1)S(1)} %out.4.refs_0_), channel_id=1, source_target_pairs={{0,24},{4,28},{8,16},{12,20},{16,8},{20,12},{24,0},{28,4},{1,25},{... | collective-permute-start | bytes 786440 | tf_op jit(solution)/shard_map/out/ppermute | solution.py:64
  96.4 12.6 %collective-permute-start.20 = (bf16[256,512]{1,0:T(8,128)(2,1)S(1)}, bf16[256,512]{1,0:T(8,128)(2,1)S(1)}, u32[]{:S(2)}, u32[]{:S(2)}) collective-permute-start(bf16[256,512]{1,0:T(8,128)(2,1)S(1)} %out.4.refs_0_), channel_id=1, source_target_pairs={{0,8},{4,12},{8,0},{12,4},{16,24},{20,28},{24,16},{28,20},{1,9},{5... | collective-permute-start | bytes 786440 | tf_op jit(solution)/shard_map/out/ppermute | solution.py:64
  96.4 18.3 %collective-permute-start.21 = (bf16[256,512]{1,0:T(8,128)(2,1)S(1)}, bf16[256,512]{1,0:T(8,128)(2,1)S(1)}, u32[]{:S(2)}, u32[]{:S(2)}) collective-permute-start(bf16[256,512]{1,0:T(8,128)(2,1)S(1)} %out.4.refs_0_), channel_id=1, source_target_pairs={{0,16},{4,20},{8,24},{12,28},{16,0},{20,4},{24,8},{28,12},{1,17},{... | collective-permute-start | bytes 786440 | tf_op jit(solution)/shard_map/out/ppermute | solution.py:64
  99.8 22.3 %collective-permute-start.26 = (bf16[512,768]{1,0:T(8,128)(2,1)S(1)}, bf16[512,768]{1,0:T(8,128)(2,1)S(1)}, u32[]{:S(2)}, u32[]{:S(2)}) collective-permute-start(bf16[512,768]{1,0:T(8,128)(2,1)S(1)} %slice.8), channel_id=1, source_target_pairs={{1,0},{2,1},{3,2},{0,3},{5,4},{6,5},{7,6},{4,7},{9,8},{10,9},{11,1... | collective-permute-start | bytes 2359304 | tf_op jit(solution)/shard_map/out_weight/ppermute | solution.py:69
  99.9 22.1 %collective-permute-start.27 = (bf16[512,768]{1,0:T(8,128)(2,1)S(1)}, bf16[512,768]{1,0:T(8,128)(2,1)S(1)}, u32[]{:S(2)}, u32[]{:S(2)}) collective-permute-start(bf16[512,768]{1,0:T(8,128)(2,1)S(1)} %slice.9), channel_id=1, source_target_pairs={{3,0},{0,1},{1,2},{2,3},{7,4},{4,5},{5,6},{6,7},{11,8},{8,9},{9,10... | collective-permute-start | bytes 2359304 | tf_op jit(solution)/shard_map/out_weight/ppermute | solution.py:69
  115.0 8.5 %collective-permute-start.24 = (bf16[160,2048]{1,0:T(8,128)(2,1)S(1)}, bf16[160,2048]{1,0:T(8,128)(2,1)S(1)}, u32[]{:S(2)}, u32[]{:S(2)}) collective-permute-start(bf16[160,2048]{1,0:T(8,128)(2,1)S(1)} %get-tuple-element.65.refs_0_.refs_1_), channel_id=1, source_target_pairs={{0,4},{4,0},{8,12},{12,8},{16,20},{20,16},{24,28},{28,24},{1,5},{5... | collective-permute-start | bytes 1966088 | tf_op jit(solution)/shard_map/out/ppermute | solution.py:64
  (10 other events, 53.7 us)
